TPU v7x, 32 devices: a whole 2x2x4 slice. The times are simulated.
32 devices in a mesh: row: 4 (over z), col: 8 (over y, x, core).
Axes of the slice: x: 2, y: 2, z: 4, core: 2. Of those that a mesh axis runs over, the one named last changes fastest.
Arguments:
- activations: bfloat16 [96, 48, 3072], P('row', None, 'col'), may hold values from -30 to 30
- cotangent: bfloat16 [96, 48, 3072], P('row', None, 'col'), may hold values from -6 to 6
- kernel: float32 [7, 7, 3072], P(None, None, 'col'), may hold values from -0.875 to 0.875
- ln_gain: float32 [3072], replicated, may hold values from 0.25 to 1.75
- ln_bias: float32 [3072], replicated, may hold values from -3 to 3
- w_expand: bfloat16 [3072, 12288], P('row', 'col'), may hold values from -0.5 to 0.5
- b_expand: float32 [12288], P('col'), may hold values from -3 to 3
- w_reduce: bfloat16 [12288, 3072], P('col', 'row'), may hold values from -0.078125 to 0.078125
- b_reduce: float32 [3072], P('col'), may hold values from -3 to 3
- layer_scale: float32 [3072], P('col'), may hold values from 0.3 to 1.5
Outputs:
- block_out: bfloat16 [96, 48, 3072], P('row', None, 'col')
- grad_input: bfloat16 [96, 48, 3072], P('row', None, 'col')
All inputs are finite; a program needn't handle non-finite values.
Results may differ from a plain program's by a relative error of at most 0.015.
Values may be sent and summed in bfloat16 or wider, within the bound.
A program may use at most 128 MiB of HBM per device.

v0:
```python
import functools

import jax
import jax.numpy as jnp
from jax import lax
from jax.experimental import pallas as pl
from jax.experimental.pallas import tpu as pltpu
from jax.sharding import PartitionSpec as P

H = 48
LANES = 128

epsilon = 1e-06
root_half = 0.7071067811865476
density_scale = 0.3989422804014327


def conv_kernel(flip, add, x_ref, top_ref, bottom_ref, k_ref, *rest):
    if add:
        add_ref, o_ref, field = rest
    else:
        o_ref, field = rest
    rows, width, lanes = x_ref.shape
    field[...] = jnp.zeros_like(field)
    field[0:3, 8 : 8 + width, :] = top_ref[...].astype(jnp.float32)
    field[3 : 3 + rows, 8 : 8 + width, :] = x_ref[...].astype(jnp.float32)
    field[3 + rows : 6 + rows, 8 : 8 + width, :] = bottom_ref[...].astype(jnp.float32)

    @pl.loop(0, rows)
    def _(r):
        total = jnp.zeros((width, lanes), jnp.float32)
        for a in range(7):
            for b in range(7):
                weight = k_ref[6 - a, 6 - b] if flip else k_ref[a, b]
                total += weight[None, :] * field[r + a, 5 + b : 5 + b + width, :]
        mixed = total.astype(jnp.bfloat16)
        if add:
            mixed = (add_ref[r].astype(jnp.float32) + mixed.astype(jnp.float32)).astype(
                jnp.bfloat16
            )
        o_ref[r] = mixed


def depthwise(field, top, bottom, kernel, flip, add=None):
    rows, width, channels = field.shape
    lanes = LANES if channels % LANES == 0 else channels
    block = lambda n: pl.BlockSpec((n, width, lanes), lambda i: (0, 0, i))
    operands = [field, top, bottom, kernel]
    specs = [block(rows), block(3), block(3), pl.BlockSpec((7, 7, lanes), lambda i: (0, 0, i))]
    if add is not None:
        operands.append(add)
        specs.append(block(rows))
    return pl.pallas_call(
        functools.partial(conv_kernel, flip, add is not None),
        out_shape=jax.ShapeDtypeStruct(field.shape, jnp.bfloat16),
        grid=(channels // lanes,),
        in_specs=specs,
        out_specs=block(rows),
        scratch_shapes=[pltpu.VMEM((rows + 6, width + 16, lanes), jnp.float32)],
        compiler_params=pltpu.CompilerParams(vmem_limit_bytes=32 * 2**20),
        cost_estimate=pl.CostEstimate(
            flops=98 * rows * width * channels,
            bytes_accessed=6 * rows * width * channels,
            transcendentals=0,
        ),
        name="depthwise_flipped" if flip else "depthwise",
    )(*operands)


def halo(field):
    rows = field.shape[0]
    per_image = H // rows
    count = lax.axis_size("row")
    down = [(i, i + 1) for i in range(count - 1) if (i + 1) % per_image]
    up = [(j, i) for i, j in down]
    return lax.ppermute(field[-3:], "row", down), lax.ppermute(field[:3], "row", up)


def swap(value, distance):
    count = lax.axis_size("col")
    return lax.ppermute(value, "col", [(i, i ^ distance) for i in range(count)])


def gather_rows(piece):
    count = lax.axis_size("row")
    me = lax.axis_index("row")
    depth, wide = piece.shape
    out = jnp.zeros((depth, wide * count), piece.dtype)
    for distance in range(count - 1, -1, -1):
        pairs = [(i, i ^ distance) for i in range(count)]
        arrived = lax.ppermute(piece, "row", pairs) if distance else piece
        out = lax.dynamic_update_slice(out, arrived, (0, (me ^ distance) * wide))
    return out


def gather_columns(piece):
    count = lax.axis_size("col")
    me = lax.axis_index("col")
    tokens, narrow = piece.shape
    out = jnp.zeros((tokens, narrow * count), piece.dtype)
    for distance in range(0, count, 2):
        arrived = swap(piece, distance) if distance else piece
        other = swap(arrived, 1)
        out = lax.dynamic_update_slice(out, arrived, (0, (me ^ distance) * narrow))
        out = lax.dynamic_update_slice(out, other, (0, (me ^ distance ^ 1) * narrow))
    return out


def pair_sums(part):
    count = lax.axis_size("col")
    me = lax.axis_index("col")
    order = list(range(count - 2, -1, -2))
    arrived = {d: swap(part(me ^ d ^ 1).astype(jnp.bfloat16), 1) for d in order}
    pairs = []
    for d in order:
        pair = part(me ^ d) + arrived[d].astype(jnp.float32)
        pairs.append(pair.astype(jnp.bfloat16) if d else pair)
    return pairs


def sum_pairs(pairs):
    total = pairs[-1]
    for index, pair in enumerate(reversed(pairs[:-1])):
        total = total + swap(pair, 2 * index + 2).astype(jnp.float32)
    return total


def body(
    activations,
    cotangent,
    kernel,
    ln_gain,
    ln_bias,
    w_expand,
    b_expand,
    w_reduce,
    b_reduce,
    layer_scale,
):
    row_count, grid_width, narrow = activations.shape
    channels = narrow * lax.axis_size("col")
    col_start = lax.axis_index("col") * narrow
    tokens = row_count * grid_width
    units = w_expand.shape[1]
    cut = narrow // 3
    dot = functools.partial(jnp.dot, preferred_element_type=jnp.float32)

    def turned(left, right):
        return lax.dot_general(
            left, right, (((1,), (1,)), ((), ())), preferred_element_type=jnp.float32
        )

    owners = w_reduce.reshape(units, -1, narrow)
    expand_full = lax.all_gather(w_expand, "row", axis=0, tiled=True)
    reduce_first = gather_rows(owners[:, :, :cut].reshape(units, -1))
    reduce_last = lax.all_gather(
        owners[:, :, cut:].reshape(units, -1), "row", axis=1, tiled=True
    )

    top, bottom = halo(activations)
    mixed_bf = depthwise(activations, top, bottom, kernel, False)
    local_mixed = mixed_bf.reshape(tokens, narrow).astype(jnp.float32)
    row_sum, square_sum = lax.psum(
        (jnp.sum(local_mixed, 1), jnp.sum(local_mixed * local_mixed, 1)), "col"
    )
    row_mean = row_sum[:, None] / channels
    square = square_sum[:, None] / channels
    inv_std = lax.rsqrt(square - row_mean * row_mean + epsilon)
    normal_local = (local_mixed - row_mean) * inv_std
    local_gain = lax.dynamic_slice_in_dim(ln_gain, col_start, narrow)
    local_shift = lax.dynamic_slice_in_dim(ln_bias, col_start, narrow)
    normed = (normal_local * local_gain + local_shift).astype(jnp.bfloat16)
    normed_full = gather_columns(normed)

    cot_f = cotangent.astype(jnp.float32)
    grad_branch = (layer_scale * cot_f).reshape(tokens, narrow).astype(jnp.bfloat16)
    grad_first = gather_columns(grad_branch[:, :cut])
    grad_last = gather_columns(grad_branch[:, cut:])
    expand_full, reduce_first, grad_first, grad_last = lax.optimization_barrier(
        (expand_full, reduce_first, grad_first, grad_last)
    )

    preact = dot(normed_full, expand_full) + b_expand
    cumulative = 0.5 * (1.0 + lax.erf(preact * root_half))
    hidden = (preact * cumulative).astype(jnp.bfloat16)

    def branch_part(weights, activated):
        width = weights.shape[1] // lax.axis_size("col")
        return lambda owner: dot(
            activated, lax.dynamic_slice_in_dim(weights, owner * width, width, 1)
        )

    branch_first = sum_pairs(pair_sums(branch_part(reduce_first, hidden)))
    grad_hidden = turned(grad_first, reduce_first)
    slope = cumulative + preact * jnp.exp(-0.5 * preact * preact) * density_scale
    vectors = jnp.stack([ln_gain, ln_bias])
    gain_unit, bias_unit = jnp.dot(
        vectors, expand_full.astype(jnp.float32), precision=lax.Precision.HIGHEST
    )
    scaled = preact - (b_expand + bias_unit)
    reduce_last, branch_first, grad_hidden, slope, gain_unit, scaled = lax.optimization_barrier(
        (reduce_last, branch_first, grad_hidden, slope, gain_unit, scaled)
    )
    grad_hidden = grad_hidden + turned(grad_last, reduce_last)
    grad_preact = (grad_hidden * slope).astype(jnp.bfloat16)

    def grad_part(owner):
        return turned(
            grad_preact, lax.dynamic_slice_in_dim(expand_full, owner * narrow, narrow, 0)
        )

    grad_pairs = pair_sums(grad_part)
    grad_float = grad_preact.astype(jnp.float32)
    grad_sums = jnp.stack(
        [jnp.sum(grad_float * gain_unit, 1), jnp.sum(grad_float * scaled, 1)]
    )
    distance = 1
    while distance < lax.axis_size("col"):
        grad_sums = grad_sums + swap(grad_sums, distance)
        distance *= 2
    grad_total, grad_cross = grad_sums[0], grad_sums[1]
    hidden = lax.optimization_barrier((hidden, *grad_pairs))[0]
    grad_gain = sum_pairs(grad_pairs) * local_gain
    branch_last = sum_pairs(pair_sums(branch_part(reduce_last, hidden)))
    branch_out = jnp.concatenate([branch_first, branch_last], 1) + b_reduce

    grad_mixed = inv_std * (
        grad_gain - grad_total[:, None] / channels - normal_local * grad_cross[:, None] / channels
    )
    grad_mixed = grad_mixed.astype(jnp.bfloat16).reshape(row_count, grid_width, narrow)
    top, bottom = halo(grad_mixed)
    grad_input = depthwise(grad_mixed, top, bottom, kernel, True, cotangent)

    act_f = activations.astype(jnp.float32)
    block_out = (act_f + layer_scale * branch_out.reshape(row_count, grid_width, narrow)).astype(
        jnp.bfloat16
    )
    return (block_out, grad_input)


def solution(mesh):
    return jax.shard_map(
        body,
        mesh=mesh,
        in_specs=(
            P("row", None, "col"),
            P("row", None, "col"),
            P(None, None, "col"),
            P(),
            P(),
            P("row", "col"),
            P("col"),
            P("col", "row"),
            P("col"),
            P("col"),
        ),
        out_specs=(P("row", None, "col"), P("row", None, "col")),
        check_vma=False,
    )
```

profile of v0, /device:TPU:0, one launch (start us, length us, event | category | flops | bytes accessed | tf_op | source)
XLA Modules:
  0.0 479.6 jit_solution(9455971537768460767)
XLA Ops:
  8.0 5.9 %reshape.58 = bf16[1536,2,384]{2,1,0:T(2,128)(2,1)} reshape(bf16[1536,768]{1,0:T(8,128)(2,1)} %param.17) | data formatting | bytes 4718592 | tf_op jit(solution)/shard_map/reshape | solution.py:153
  13.8 1.6 slice.49
  17.3 5.0 %collective-permute-start.9 = (bf16[1536,256]{1,0:T(8,128)(2,1)}, bf16[1536,256]{1,0:T(8,128)(2,1)}, u32[]{:S(2)}, u32[]{:S(2)}) collective-permute-start(bf16[1536,256]{1,0:T(8,128)(2,1)} %bitcast.54), channel_id=1, source_target_pairs={{0,24},{8,16},{16,8},{24,0},{1,25},{9,17},{17,9},{25,1},{2,26},{10... | collective-permute-start | bytes 2359304 | tf_op jit(solution)/shard_map/ppermute | solution.py:91
  23.6 2.5 collective-permute-start
  26.1 1.3 collective-permute-start.1
  27.4 1.5 copy.12
  28.9 2.8 broadcast_in_dim.11
  31.7 1.2 fusion.102
  32.9 1.4 dynamic_slice.79
  35.0 60.0 %collective-permute-done.top_ref = bf16[3,48,384]{2,1,0:T(8,128)(2,1)S(1)} collective-permute-done((bf16[3,48,384]{2,1,0:T(8,128)(2,1)S(1)}, bf16[3,48,384]{2,1,0:T(8,128)(2,1)S(1)}, u32[]{:S(2)}, u32[]{:S(2)}) %collective-permute-start) | collective-permute-done | bytes 110624 | tf_op jit(solution)/shard_map/ppermute | solution.py:76
  95.1 1.2 collective-permute-start.13
  96.3 9.0 %depthwise.1 = bf16[24,48,384]{2,1,0:T(8,128)(2,1)S(1)} custom-call(bf16[24,48,384]{2,1,0:T(8,128)(2,1)S(1)} %copy-done, bf16[3,48,384]{2,1,0:T(8,128)(2,1)S(1)} %collective-permute-done.top_ref, bf16[3,48,384]{2,1,0:T(8,128)(2,1)S(1)} %collective-permute-done.1.bottom_ref, f32[7,7,384]{2,1,0:T(8,128)S(1)} %copy-done.2), custom_call_target="tpu_custom_call" | custom-call | flops 43352064 | bytes 2654208 | tf_op jit(solution)/shard_map/depthwise/pallas_call | solution.py:53
  105.9 25.9 %all-reduce = (f32[1152]{0:T(1024)S(1)}, f32[1152]{0:T(1024)S(1)}) all-reduce(f32[1152]{0:T(1024)S(1)} %reduce_sum.43, f32[1152]{0:T(1024)S(1)} %reduce_sum.41), channel_id=1, replica_groups=mesh['row'=4,'col'=8] {'col'}, use_global_device_ids=true, to_apply=%region_3.0 | all-reduce | flops 2304 | bytes 18432 | tf_op jit(solution)/shard_map/psum | solution.py:163
  131.9 3.8 broadcast_in_dim.8
  135.7 1.5 constant_dynamic-update-slice_fusion.27
  141.1 8.7 %collective-permute-done.20 = bf16[1152,256]{1,0:T(8,128)(2,1)S(1)} collective-permute-done((bf16[1152,256]{1,0:T(8,128)(2,1)S(1)}, bf16[1152,256]{1,0:T(8,128)(2,1)S(1)}, u32[]{:S(2)}, u32[]{:S(2)}) %collective-permute-start.20) | collective-permute-done | bytes 589856 | tf_op jit(solution)/shard_map/ppermute | solution.py:81
  149.9 1.7 collective-permute-start.11
  152.5 2.4 collective-permute-start.17
  155.0 5.8 %collective-permute-done.17 = bf16[1152,128]{1,0:T(8,128)(2,1)S(1)} collective-permute-done((bf16[1152,128]{1,0:T(8,128)(2,1)}, bf16[1152,128]{1,0:T(8,128)(2,1)S(1)}, u32[]{:S(2)}, u32[]{:S(2)}) %collective-permute-start.17) | collective-permute-done | bytes 294944 | tf_op jit(solution)/shard_map/ppermute | solution.py:81
  161.7 1.4 collective-permute-done.18
  163.4 2.3 collective-permute-start.24
  166.0 1.2 constant_dynamic-update-slice_fusion.19
  167.3 7.0 %collective-permute-done.10 = bf16[1536,256]{1,0:T(8,128)(2,1)} collective-permute-done((bf16[1536,256]{1,0:T(8,128)(2,1)}, bf16[1536,256]{1,0:T(8,128)(2,1)}, u32[]{:S(2)}, u32[]{:S(2)}) %collective-permute-start.10) | collective-permute-done | bytes 786464 | tf_op jit(solution)/shard_map/ppermute | solution.py:91
  174.2 1.5 collective-permute-start.3
  175.7 1.2 constant_dynamic-update-slice_fusion.18
  177.0 42.7 %collective-permute-done.11 = bf16[1536,256]{1,0:T(8,128)(2,1)S(1)} collective-permute-done((bf16[1536,256]{1,0:T(8,128)(2,1)}, bf16[1536,256]{1,0:T(8,128)(2,1)S(1)}, u32[]{:S(2)}, u32[]{:S(2)}) %collective-permute-start.11) | collective-permute-done | bytes 786464 | tf_op jit(solution)/shard_map/ppermute | solution.py:91
  219.7 1.5 collective-permute-start.5
  221.3 1.5 collective-permute-start.7
  223.0 1.1 constant_dynamic-update-slice_fusion.26
  225.9 33.9 %collective-permute-done.5 = bf16[1152,384]{1,0:T(8,128)(2,1)S(1)} collective-permute-done((bf16[1152,384]{1,0:T(8,128)(2,1)S(1)}, bf16[1152,384]{1,0:T(8,128)(2,1)S(1)}, u32[]{:S(2)}, u32[]{:S(2)}) %collective-permute-start.5) | collective-permute-done | bytes 884768 | tf_op jit(solution)/shard_map/ppermute | solution.py:81
  268.2 1.1 constant_dynamic-update-slice_fusion.21
  270.5 7.3 %fusion.70 = f32[2,1536]{1,0:T(2,128)S(1)} fusion(bf16[3072,1536]{1,0:T(8,128)(2,1)} %all-gather.5.cloned.1.call-done, f32[1,3072]{1,0:T(1,128)S(1)} %bitcast.68, f32[1,3072]{1,0:T(1,128)S(1)} %bitcast.69), kind=kOutput, calls=%fused_computation.88 | convolution fusion | flops 113252352 | bytes 9474048 | tf_op jit(solution)/shard_map/dot_general | solution.py:197
  277.9 17.7 %broadcast_subtract_fusion = (f32[1152,1536]{1,0:T(8,128)}, bf16[1152,1536]{1,0:T(8,128)(2,1)S(1)}, f32[1152,1536]{1,0:T(8,128)}) fusion(f32[1536]{0:T(1024)S(1)} %add.280, f32[1536]{0:T(1024)S(1)} %copy-done.21, bf16[1152,3072]{1,0:T(8,128)(2,1)} %constant_dynamic-update-slice_fusion.20, bf16[3072,1536]{1,0:T(8,128)(2,1)S(1)} %copy-done.3), kind=kOutput, calls=%fused_computation.15 | convolution fusion | flops 10892869632 | bytes 34222080 | tf_op jit(solution)/shard_map/dot_general | solution.py:183
  295.6 2.6 convolution_convert_fusion.8
  304.4 2.7 collective-permute-start.32
  310.3 5.9 %fusion.105 = f32[1152,1536]{1,0:T(8,128)} fusion(bf16[1152,1024]{1,0:T(8,128)(2,1)S(1)} %copy-done.13, bf16[1536,1024]{1,0:T(8,128)(2,1)S(1)} %copy-done.9), kind=kOutput, calls=%fused_computation.158 | convolution fusion | flops 3623878656 | bytes 12582912 | tf_op jit(solution)/shard_map/dot_general | solution.py:149
  316.3 4.5 collective-permute-done.30
  322.0 37.1 %all-gather.3.cloned.1.call-done = bf16[1536,2048]{1,0:T(8,128)(2,1)} async-done(((bf16[1536,512]{1,0:T(8,128)(2,1)}), bf16[1536,2048]{1,0:T(8,128)(2,1)}) %all-gather.3.cloned.1.call-update) | async-done | bytes 6291472 | tf_op jit(solution)/shard_map/all_gather | solution.py:156
  359.0 14.6 %fusion.1 = bf16[1152,1536]{1,0:T(8,128)(2,1)S(1)} fusion(f32[1152,1536]{1,0:T(8,128)} %get-tuple-element.20, f32[1152,1536]{1,0:T(8,128)} %fusion.105, bf16[1152,2048]{1,0:T(8,128)(2,1)} %constant_dynamic-update-slice_fusion, bf16[1536,2048]{1,0:T(8,128)(2,1)} %all-gather.3.cloned.1.call-done), kind=kOutput, calls=%fused_computation.6 | convolution fusion | flops 7253065728 | bytes 28704768 | tf_op jit(solution)/shard_map/dot_general | solution.py:149
  373.7 3.4 convolution_convert_fusion.3
  377.1 4.7 fusion.2
  382.0 2.0 convolution_convert_fusion.2
  384.0 1.5 collective-permute-start.48
  385.6 2.0 convolution_convert_fusion.1
  388.2 1.6 collective-permute-start.49
  389.7 2.0 convolution_convert_fusion
  392.4 2.0 add_convert_fusion.2
  394.5 2.1 add_convert_fusion.1
  396.6 2.2 add_convert_fusion
  398.8 2.0 convert_add_fusion
  400.9 1.2 slice-done.5
  403.2 1.1 convolution_convert_fusion.5
  404.3 1.6 collective-permute-start.46
  413.5 1.6 collective-permute-start.43
  416.2 11.6 %collective-permute-done.46 = bf16[1152,384]{1,0:T(8,128)(2,1)S(1)} collective-permute-done((bf16[1152,384]{1,0:T(8,128)(2,1)S(1)}, bf16[1152,384]{1,0:T(8,128)(2,1)S(1)}, u32[]{:S(2)}, u32[]{:S(2)}) %collective-permute-start.46) | collective-permute-done | bytes 884768 | tf_op jit(solution)/shard_map/ppermute | solution.py:81
  428.9 17.9 %collective-permute-done.45 = bf16[1152,384]{1,0:T(8,128)(2,1)S(1)} collective-permute-done((bf16[1152,384]{1,0:T(8,128)(2,1)S(1)}, bf16[1152,384]{1,0:T(8,128)(2,1)S(1)}, u32[]{:S(2)}, u32[]{:S(2)}) %collective-permute-start.45) | collective-permute-done | bytes 884768 | tf_op jit(solution)/shard_map/ppermute | solution.py:81
  447.9 1.2 multiply_convert_fusion.1
  449.1 1.3 collective-permute-start.50
  450.4 2.3 collective-permute-done.50.top_ref
  452.8 1.3 collective-permute-start.51
  455.1 4.2 collective-permute-done.51.bottom_ref
  459.4 10.1 %depthwise_flipped.1 = bf16[24,48,384]{2,1,0:T(8,128)(2,1)} custom-call(bf16[24,48,384]{2,1,0:T(8,128)(2,1)S(1)} %bitcast.55, bf16[3,48,384]{2,1,0:T(8,128)(2,1)S(1)} %collective-permute-done.50.top_ref, bf16[3,48,384]{2,1,0:T(8,128)(2,1)S(1)} %collective-permute-done.51.bottom_ref, f32[7,7,384]{2,1,0:T(8,128)S(1)} %copy-done.2, ...), custom_call_target="tpu_custom_call" | custom-call | flops 43352064 | bytes 2654208 | tf_op jit(solution)/shard_map/depthwise_flipped/pallas_call | solution.py:53
  469.5 1.5 collective-permute-done.41
  471.3 1.2 fusion.10
  (201 shorter events, 48.8 us)
Async XLA Ops:
  7.2 263.3 %all-gather.5.cloned.1.call-start = ((), (), s32[]{:S(2)}) async-start(), calls=%async_computation.1 | async-start | bytes 11796480 | tf_op jit(solution)/shard_map/all_gather | solution.py:154
  7.9 14.4 %copy-start.1 = (bf16[24,48,384]{2,1,0:T(8,128)(2,1)S(1)}, bf16[24,48,384]{2,1,0:T(8,128)(2,1)}, u32[]{:S(2)}) copy-start(bf16[24,48,384]{2,1,0:T(8,128)(2,1)} %rest_0_.1) | copy-start | bytes 2654212
  7.9 14.4 %copy-start.22 = (f32[384]{0:T(512)S(1)}, f32[384]{0:T(512)}, u32[]{:S(2)}) copy-start(f32[384]{0:T(512)} %param.19) | copy-start | bytes 4612
  7.9 351.1 %all-gather.3.cloned.1.call-start = ((), (), s32[]{:S(2)}) async-start(), calls=%async_computation | async-start | bytes 7864320 | tf_op jit(solution)/shard_map/all_gather | solution.py:156
  17.3 146.1 %collective-permute-start.9 = (bf16[1536,256]{1,0:T(8,128)(2,1)}, bf16[1536,256]{1,0:T(8,128)(2,1)}, u32[]{:S(2)}, u32[]{:S(2)}) collective-permute-start(bf16[1536,256]{1,0:T(8,128)(2,1)} %bitcast.54), channel_id=1, source_target_pairs={{0,24},{8,16},{16,8},{24,0},{1,25},{9,17},{17,9},{25,1},{2,26},{10... | collective-permute-start | bytes 2359304 | tf_op jit(solution)/shard_map/ppermute | solution.py:91
  22.3 151.9 %collective-permute-start.10 = (bf16[1536,256]{1,0:T(8,128)(2,1)}, bf16[1536,256]{1,0:T(8,128)(2,1)}, u32[]{:S(2)}, u32[]{:S(2)}) collective-permute-start(bf16[1536,256]{1,0:T(8,128)(2,1)} %bitcast.54), channel_id=1, source_target_pairs={{0,16},{8,24},{16,0},{24,8},{1,17},{9,25},{17,1},{25,9},{2,18},{10... | collective-permute-start | bytes 2359304 | tf_op jit(solution)/shard_map/ppermute | solution.py:91
  23.6 113.7 %collective-permute-start.12 = (bf16[1152,128]{1,0:T(8,128)(2,1)}, bf16[1152,128]{1,0:T(8,128)(2,1)}, u32[]{:S(2)}, u32[]{:S(2)}) collective-permute-start(bf16[1152,128]{1,0:T(8,128)(2,1)} %get-tuple-element.41), channel_id=1, source_target_pairs={{0,1},{1,0},{2,3},{3,2},{4,5},{5,4},{6,7},{7,6},{8,9},{9,8},{10,11... | collective-permute-start | bytes 884744 | tf_op jit(solution)/shard_map/ppermute | solution.py:81
  23.6 71.5 %collective-permute-start = (bf16[3,48,384]{2,1,0:T(8,128)(2,1)S(1)}, bf16[3,48,384]{2,1,0:T(8,128)(2,1)S(1)}, u32[]{:S(2)}, u32[]{:S(2)}) collective-permute-start(bf16[3,48,384]{2,1,0:T(8,128)(2,1)S(1)} %get-tuple-element.44), channel_id=1, source_target_pairs={{0,8},{16,24},{1,9},{17,25},{2,10},{18,26},{3,11},{19,27},{4,12},{... | collective-permute-start | bytes 331784 | tf_op jit(solution)/shard_map/ppermute | solution.py:76
  26.1 70.2 %collective-permute-start.1 = (bf16[3,48,384]{2,1,0:T(8,128)(2,1)S(1)}, bf16[3,48,384]{2,1,0:T(8,128)(2,1)S(1)}, u32[]{:S(2)}, u32[]{:S(2)}) collective-permute-start(bf16[3,48,384]{2,1,0:T(8,128)(2,1)S(1)} %get-tuple-element.43), channel_id=1, source_target_pairs={{8,0},{24,16},{9,1},{25,17},{10,2},{26,18},{11,3},{27,19},{12,4},{... | collective-permute-start | bytes 331784 | tf_op jit(solution)/shard_map/ppermute | solution.py:76
  28.9 67.4 %copy-start.2 = (f32[7,7,384]{2,1,0:T(8,128)S(1)}, f32[7,7,384]{2,1,0:T(8,128)}, u32[]{:S(2)}) copy-start(f32[7,7,384]{2,1,0:T(8,128)} %k_ref.3) | copy-start | bytes 225796
  95.1 43.2 %collective-permute-start.13 = (bf16[1152,128]{1,0:T(8,128)(2,1)}, bf16[1152,128]{1,0:T(8,128)(2,1)}, u32[]{:S(2)}, u32[]{:S(2)}) collective-permute-start(bf16[1152,128]{1,0:T(8,128)(2,1)} %get-tuple-element.41), channel_id=1, source_target_pairs={{0,2},{1,3},{2,0},{3,1},{4,6},{5,7},{6,4},{7,5},{8,10},{9,11},{10,... | collective-permute-start | bytes 884744 | tf_op jit(solution)/shard_map/ppermute | solution.py:81
  96.3 43.8 %collective-permute-start.19 = (bf16[1152,256]{1,0:T(8,128)(2,1)}, bf16[1152,256]{1,0:T(8,128)(2,1)S(1)}, u32[]{:S(2)}, u32[]{:S(2)}) collective-permute-start(bf16[1152,256]{1,0:T(8,128)(2,1)} %get-tuple-element.39), channel_id=1, source_target_pairs={{0,1},{1,0},{2,3},{3,2},{4,5},{5,4},{6,7},{7,6},{8,9},{9,8},{10,11... | collective-permute-start | bytes 1769480 | tf_op jit(solution)/shard_map/ppermute | solution.py:81
  137.2 12.6 %collective-permute-start.20 = (bf16[1152,256]{1,0:T(8,128)(2,1)S(1)}, bf16[1152,256]{1,0:T(8,128)(2,1)S(1)}, u32[]{:S(2)}, u32[]{:S(2)}) collective-permute-start(bf16[1152,256]{1,0:T(8,128)(2,1)S(1)} %copy-done.14), channel_id=1, source_target_pairs={{0,2},{1,3},{2,0},{3,1},{4,6},{5,7},{6,4},{7,5},{8,10},{9,11},{10,... | collective-permute-start | bytes 1769480 | tf_op jit(solution)/shard_map/ppermute | solution.py:81
  138.3 14.1 %collective-permute-start.15 = (bf16[1152,128]{1,0:T(8,128)(2,1)}, bf16[1152,128]{1,0:T(8,128)(2,1)S(1)}, u32[]{:S(2)}, u32[]{:S(2)}) collective-permute-start(bf16[1152,128]{1,0:T(8,128)(2,1)} %get-tuple-element.41), channel_id=1, source_target_pairs={{0,4},{1,5},{2,6},{3,7},{4,0},{5,1},{6,2},{7,3},{8,12},{9,13},{10,... | collective-permute-start | bytes 884744 | tf_op jit(solution)/shard_map/ppermute | solution.py:81
  140.2 14.7 %collective-permute-start.14 = (bf16[1152,128]{1,0:T(8,128)(2,1)}, bf16[1152,128]{1,0:T(8,128)(2,1)S(1)}, u32[]{:S(2)}, u32[]{:S(2)}) collective-permute-start(bf16[1152,128]{1,0:T(8,128)(2,1)} %collective-permute-done.13), channel_id=1, source_target_pairs={{0,1},{1,0},{2,3},{3,2},{4,5},{5,4},{6,7},{7,6},{8,9},{9,8},{10,11... | collective-permute-start | bytes 884744 | tf_op jit(solution)/shard_map/ppermute | solution.py:81
  149.9 69.8 %collective-permute-start.11 = (bf16[1536,256]{1,0:T(8,128)(2,1)}, bf16[1536,256]{1,0:T(8,128)(2,1)S(1)}, u32[]{:S(2)}, u32[]{:S(2)}) collective-permute-start(bf16[1536,256]{1,0:T(8,128)(2,1)} %bitcast.54), channel_id=1, source_target_pairs={{0,8},{8,0},{16,24},{24,16},{1,9},{9,1},{17,25},{25,17},{2,10},{10... | collective-permute-start | bytes 2359304 | tf_op jit(solution)/shard_map/ppermute | solution.py:91
  152.5 8.4 %collective-permute-start.17 = (bf16[1152,128]{1,0:T(8,128)(2,1)}, bf16[1152,128]{1,0:T(8,128)(2,1)S(1)}, u32[]{:S(2)}, u32[]{:S(2)}) collective-permute-start(bf16[1152,128]{1,0:T(8,128)(2,1)} %get-tuple-element.41), channel_id=1, source_target_pairs={{0,6},{1,7},{2,4},{3,5},{4,2},{5,3},{6,0},{7,1},{8,14},{9,15},{10,... | collective-permute-start | bytes 884744 | tf_op jit(solution)/shard_map/ppermute | solution.py:81
  154.8 6.7 %collective-permute-start.16 = (bf16[1152,128]{1,0:T(8,128)(2,1)S(1)}, bf16[1152,128]{1,0:T(8,128)(2,1)S(1)}, u32[]{:S(2)}, u32[]{:S(2)}) collective-permute-start(bf16[1152,128]{1,0:T(8,128)(2,1)S(1)} %collective-permute-done.15), channel_id=1, source_target_pairs={{0,1},{1,0},{2,3},{3,2},{4,5},{5,4},{6,7},{7,6},{8,9},{9,8},{10,11... | collective-permute-start | bytes 884744 | tf_op jit(solution)/shard_map/ppermute | solution.py:81
  160.8 60.5 %collective-permute-start.22 = (bf16[1152,256]{1,0:T(8,128)(2,1)S(1)}, bf16[1152,256]{1,0:T(8,128)(2,1)S(1)}, u32[]{:S(2)}, u32[]{:S(2)}) collective-permute-start(bf16[1152,256]{1,0:T(8,128)(2,1)S(1)} %copy-done.14), channel_id=1, source_target_pairs={{0,4},{1,5},{2,6},{3,7},{4,0},{5,1},{6,2},{7,3},{8,12},{9,13},{10,... | collective-permute-start | bytes 1769480 | tf_op jit(solution)/shard_map/ppermute | solution.py:81
  161.5 1.6 collective-permute-start.18
  163.1 59.7 %collective-permute-start.2 = (bf16[1152,384]{1,0:T(8,128)(2,1)S(1)}, bf16[1152,384]{1,0:T(8,128)(2,1)S(1)}, u32[]{:S(2)}, u32[]{:S(2)}) collective-permute-start(bf16[1152,384]{1,0:T(8,128)(2,1)S(1)} %get-tuple-element.48), channel_id=1, source_target_pairs={{0,1},{1,0},{2,3},{3,2},{4,5},{5,4},{6,7},{7,6},{8,9},{9,8},{10,11... | collective-permute-start | bytes 2654216 | tf_op jit(solution)/shard_map/ppermute | solution.py:81
  163.3 58.0 %copy-start.12 = (bf16[1152,1024]{1,0:T(8,128)(2,1)}, bf16[1152,1024]{1,0:T(8,128)(2,1)S(1)}, u32[]{:S(2)}) copy-start(bf16[1152,1024]{1,0:T(8,128)(2,1)S(1)} %constant_dynamic-update-slice_fusion.8) | copy-start | bytes 7077892
  163.3 59.5 %copy-start.5 = (bf16[1536,2,128]{2,1,0:T(2,128)(2,1)S(1)}, bf16[1536,2,128]{2,1,0:T(2,128)(2,1)}, u32[]{:S(2)}) copy-start(bf16[1536,2,128]{2,1,0:T(2,128)(2,1)} %copy-done.4) | copy-start | bytes 2359300
  163.4 60.8 %collective-permute-start.24 = (bf16[1152,256]{1,0:T(8,128)(2,1)S(1)}, bf16[1152,256]{1,0:T(8,128)(2,1)S(1)}, u32[]{:S(2)}, u32[]{:S(2)}) collective-permute-start(bf16[1152,256]{1,0:T(8,128)(2,1)S(1)} %copy-done.14), channel_id=1, source_target_pairs={{0,6},{1,7},{2,4},{3,5},{4,2},{5,3},{6,0},{7,1},{8,14},{9,15},{10,... | collective-permute-start | bytes 1769480 | tf_op jit(solution)/shard_map/ppermute | solution.py:81
  174.2 50.5 %collective-permute-start.3 = (bf16[1152,384]{1,0:T(8,128)(2,1)S(1)}, bf16[1152,384]{1,0:T(8,128)(2,1)S(1)}, u32[]{:S(2)}, u32[]{:S(2)}) collective-permute-start(bf16[1152,384]{1,0:T(8,128)(2,1)S(1)} %get-tuple-element.48), channel_id=1, source_target_pairs={{0,2},{1,3},{2,0},{3,1},{4,6},{5,7},{6,4},{7,5},{8,10},{9,11},{10,... | collective-permute-start | bytes 2654216 | tf_op jit(solution)/shard_map/ppermute | solution.py:81
  219.7 40.1 %collective-permute-start.5 = (bf16[1152,384]{1,0:T(8,128)(2,1)S(1)}, bf16[1152,384]{1,0:T(8,128)(2,1)S(1)}, u32[]{:S(2)}, u32[]{:S(2)}) collective-permute-start(bf16[1152,384]{1,0:T(8,128)(2,1)S(1)} %get-tuple-element.48), channel_id=1, source_target_pairs={{0,4},{1,5},{2,6},{3,7},{4,0},{5,1},{6,2},{7,3},{8,12},{9,13},{10,... | collective-permute-start | bytes 2654216 | tf_op jit(solution)/shard_map/ppermute | solution.py:81
  221.3 38.5 %collective-permute-start.7 = (bf16[1152,384]{1,0:T(8,128)(2,1)S(1)}, bf16[1152,384]{1,0:T(8,128)(2,1)S(1)}, u32[]{:S(2)}, u32[]{:S(2)}) collective-permute-start(bf16[1152,384]{1,0:T(8,128)(2,1)S(1)} %get-tuple-element.48), channel_id=1, source_target_pairs={{0,6},{1,7},{2,4},{3,5},{4,2},{5,3},{6,0},{7,1},{8,14},{9,15},{10,... | collective-permute-start | bytes 2654216 | tf_op jit(solution)/shard_map/ppermute | solution.py:81
  222.8 37.5 %collective-permute-start.21 = (bf16[1152,256]{1,0:T(8,128)(2,1)S(1)}, bf16[1152,256]{1,0:T(8,128)(2,1)S(1)}, u32[]{:S(2)}, u32[]{:S(2)}) collective-permute-start(bf16[1152,256]{1,0:T(8,128)(2,1)S(1)} %collective-permute-done.20), channel_id=1, source_target_pairs={{0,1},{1,0},{2,3},{3,2},{4,5},{5,4},{6,7},{7,6},{8,9},{9,8},{10,11... | collective-permute-start | bytes 1769480 | tf_op jit(solution)/shard_map/ppermute | solution.py:81
  223.0 40.2 %copy-start.8 = (bf16[1536,1024]{1,0:T(8,128)(2,1)}, bf16[1536,1024]{1,0:T(8,128)(2,1)S(1)}, u32[]{:S(2)}) copy-start(bf16[1536,1024]{1,0:T(8,128)(2,1)S(1)} %constant_dynamic-update-slice_fusion.16) | copy-start | bytes 9437188
  224.1 38.1 %collective-permute-start.23 = (bf16[1152,256]{1,0:T(8,128)(2,1)S(1)}, bf16[1152,256]{1,0:T(8,128)(2,1)S(1)}, u32[]{:S(2)}, u32[]{:S(2)}) collective-permute-start(bf16[1152,256]{1,0:T(8,128)(2,1)S(1)} %collective-permute-done.22), channel_id=1, source_target_pairs={{0,1},{1,0},{2,3},{3,2},{4,5},{5,4},{6,7},{7,6},{8,9},{9,8},{10,11... | collective-permute-start | bytes 1769480 | tf_op jit(solution)/shard_map/ppermute | solution.py:81
  224.7 39.3 %collective-permute-start.25 = (bf16[1152,256]{1,0:T(8,128)(2,1)S(1)}, bf16[1152,256]{1,0:T(8,128)(2,1)S(1)}, u32[]{:S(2)}, u32[]{:S(2)}) collective-permute-start(bf16[1152,256]{1,0:T(8,128)(2,1)S(1)} %collective-permute-done.24), channel_id=1, source_target_pairs={{0,1},{1,0},{2,3},{3,2},{4,5},{5,4},{6,7},{7,6},{8,9},{9,8},{10,11... | collective-permute-start | bytes 1769480 | tf_op jit(solution)/shard_map/ppermute | solution.py:81
  259.8 5.2 %collective-permute-start.4 = (bf16[1152,384]{1,0:T(8,128)(2,1)S(1)}, bf16[1152,384]{1,0:T(8,128)(2,1)S(1)}, u32[]{:S(2)}, u32[]{:S(2)}) collective-permute-start(bf16[1152,384]{1,0:T(8,128)(2,1)S(1)} %collective-permute-done.3), channel_id=1, source_target_pairs={{0,1},{1,0},{2,3},{3,2},{4,5},{5,4},{6,7},{7,6},{8,9},{9,8},{10,11... | collective-permute-start | bytes 2654216 | tf_op jit(solution)/shard_map/ppermute | solution.py:81
  259.8 7.3 %collective-permute-start.6 = (bf16[1152,384]{1,0:T(8,128)(2,1)S(1)}, bf16[1152,384]{1,0:T(8,128)(2,1)S(1)}, u32[]{:S(2)}, u32[]{:S(2)}) collective-permute-start(bf16[1152,384]{1,0:T(8,128)(2,1)S(1)} %collective-permute-done.5), channel_id=1, source_target_pairs={{0,1},{1,0},{2,3},{3,2},{4,5},{5,4},{6,7},{7,6},{8,9},{9,8},{10,11... | collective-permute-start | bytes 2654216 | tf_op jit(solution)/shard_map/ppermute | solution.py:81
  260.3 9.1 %collective-permute-start.8 = (bf16[1152,384]{1,0:T(8,128)(2,1)S(1)}, bf16[1152,384]{1,0:T(8,128)(2,1)S(1)}, u32[]{:S(2)}, u32[]{:S(2)}) collective-permute-start(bf16[1152,384]{1,0:T(8,128)(2,1)S(1)} %collective-permute-done.7), channel_id=1, source_target_pairs={{0,1},{1,0},{2,3},{3,2},{4,5},{5,4},{6,7},{7,6},{8,9},{9,8},{10,11... | collective-permute-start | bytes 2654216 | tf_op jit(solution)/shard_map/ppermute | solution.py:81
  295.5 25.3 %copy-start.6 = (bf16[1152,1536]{1,0:T(8,128)(2,1)}, bf16[1152,1536]{1,0:T(8,128)(2,1)S(1)}, u32[]{:S(2)}) copy-start(bf16[1152,1536]{1,0:T(8,128)(2,1)S(1)} %get-tuple-element.21) | copy-start | bytes 10616836
  298.1 5.2 %collective-permute-start.31 = (bf16[1152,128]{1,0:T(8,128)(2,1)S(1)}, bf16[1152,128]{1,0:T(8,128)(2,1)S(1)}, u32[]{:S(2)}, u32[]{:S(2)}) collective-permute-start(bf16[1152,128]{1,0:T(8,128)(2,1)S(1)} %convolution_convert_fusion.8), channel_id=1, source_target_pairs={{0,1},{1,0},{2,3},{3,2},{4,5},{5,4},{6,7},{7,6},{8,9},{9,8},{10,11... | collective-permute-start | bytes 884744 | tf_op jit(solution)/shard_map/ppermute | solution.py:81
  300.0 7.1 %collective-permute-start.29 = (bf16[1152,128]{1,0:T(8,128)(2,1)S(1)}, bf16[1152,128]{1,0:T(8,128)(2,1)S(1)}, u32[]{:S(2)}, u32[]{:S(2)}) collective-permute-start(bf16[1152,128]{1,0:T(8,128)(2,1)S(1)} %convolution_convert_fusion.9), channel_id=1, source_target_pairs={{0,1},{1,0},{2,3},{3,2},{4,5},{5,4},{6,7},{7,6},{8,9},{9,8},{10,11... | collective-permute-start | bytes 884744 | tf_op jit(solution)/shard_map/ppermute | solution.py:81
  301.5 7.3 %collective-permute-start.27 = (bf16[1152,128]{1,0:T(8,128)(2,1)S(1)}, bf16[1152,128]{1,0:T(8,128)(2,1)S(1)}, u32[]{:S(2)}, u32[]{:S(2)}) collective-permute-start(bf16[1152,128]{1,0:T(8,128)(2,1)S(1)} %convolution_convert_fusion.10), channel_id=1, source_target_pairs={{0,1},{1,0},{2,3},{3,2},{4,5},{5,4},{6,7},{7,6},{8,9},{9,8},{10,11... | collective-permute-start | bytes 884744 | tf_op jit(solution)/shard_map/ppermute | solution.py:81
  302.8 13.5 %collective-permute-start.26 = (bf16[1152,128]{1,0:T(8,128)(2,1)S(1)}, bf16[1152,128]{1,0:T(8,128)(2,1)S(1)}, u32[]{:S(2)}, u32[]{:S(2)}) collective-permute-start(bf16[1152,128]{1,0:T(8,128)(2,1)S(1)} %convolution_convert_fusion.11), channel_id=1, source_target_pairs={{0,1},{1,0},{2,3},{3,2},{4,5},{5,4},{6,7},{7,6},{8,9},{9,8},{10,11... | collective-permute-start | bytes 884744 | tf_op jit(solution)/shard_map/ppermute | solution.py:81
  304.4 11.9 %collective-permute-start.32 = (bf16[1152,128]{1,0:T(8,128)(2,1)S(1)}, bf16[1152,128]{1,0:T(8,128)(2,1)S(1)}, u32[]{:S(2)}, u32[]{:S(2)}) collective-permute-start(bf16[1152,128]{1,0:T(8,128)(2,1)S(1)} %add_convert_fusion.7), channel_id=1, source_target_pairs={{0,6},{1,7},{2,4},{3,5},{4,2},{5,3},{6,0},{7,1},{8,14},{9,15},{10,... | collective-permute-start | bytes 884744 | tf_op jit(solution)/shard_map/ppermute | solution.py:81
  308.2 12.5 %collective-permute-start.30 = (bf16[1152,128]{1,0:T(8,128)(2,1)S(1)}, bf16[1152,128]{1,0:T(8,128)(2,1)S(1)}, u32[]{:S(2)}, u32[]{:S(2)}) collective-permute-start(bf16[1152,128]{1,0:T(8,128)(2,1)S(1)} %add_convert_fusion.8), channel_id=1, source_target_pairs={{0,4},{1,5},{2,6},{3,7},{4,0},{5,1},{6,2},{7,3},{8,12},{9,13},{10,... | collective-permute-start | bytes 884744 | tf_op jit(solution)/shard_map/ppermute | solution.py:81
  309.9 11.0 %collective-permute-start.28 = (bf16[1152,128]{1,0:T(8,128)(2,1)S(1)}, bf16[1152,128]{1,0:T(8,128)(2,1)S(1)}, u32[]{:S(2)}, u32[]{:S(2)}) collective-permute-start(bf16[1152,128]{1,0:T(8,128)(2,1)S(1)} %add_convert_fusion.9), channel_id=1, source_target_pairs={{0,2},{1,3},{2,0},{3,1},{4,6},{5,7},{6,4},{7,5},{8,10},{9,11},{10,... | collective-permute-start | bytes 884744 | tf_op jit(solution)/shard_map/ppermute | solution.py:81
  381.8 2.2 collective-permute-start.47
  384.0 4.1 collective-permute-start.48
  387.6 4.8 %collective-permute-start.33 = (bf16[1152,384]{1,0:T(8,128)(2,1)S(1)}, bf16[1152,384]{1,0:T(8,128)(2,1)S(1)}, u32[]{:S(2)}, u32[]{:S(2)}) collective-permute-start(bf16[1152,384]{1,0:T(8,128)(2,1)S(1)} %convolution_convert_fusion.3), channel_id=1, source_target_pairs={{0,1},{1,0},{2,3},{3,2},{4,5},{5,4},{6,7},{7,6},{8,9},{9,8},{10,11... | collective-permute-start | bytes 2654216 | tf_op jit(solution)/shard_map/ppermute | solution.py:81
  387.8 6.6 %collective-permute-start.34 = (bf16[1152,384]{1,0:T(8,128)(2,1)S(1)}, bf16[1152,384]{1,0:T(8,128)(2,1)S(1)}, u32[]{:S(2)}, u32[]{:S(2)}) collective-permute-start(bf16[1152,384]{1,0:T(8,128)(2,1)S(1)} %convolution_convert_fusion.2), channel_id=1, source_target_pairs={{0,1},{1,0},{2,3},{3,2},{4,5},{5,4},{6,7},{7,6},{8,9},{9,8},{10,11... | collective-permute-start | bytes 2654216 | tf_op jit(solution)/shard_map/ppermute | solution.py:81
  388.2 4.2 collective-permute-start.49
  391.8 4.8 collective-permute-start.35
  391.8 7.0 %collective-permute-start.36 = (bf16[1152,384]{1,0:T(8,128)(2,1)S(1)}, bf16[1152,384]{1,0:T(8,128)(2,1)S(1)}, u32[]{:S(2)}, u32[]{:S(2)}) collective-permute-start(bf16[1152,384]{1,0:T(8,128)(2,1)S(1)} %convolution_convert_fusion), channel_id=1, source_target_pairs={{0,1},{1,0},{2,3},{3,2},{4,5},{5,4},{6,7},{7,6},{8,9},{9,8},{10,11... | collective-permute-start | bytes 2654216 | tf_op jit(solution)/shard_map/ppermute | solution.py:81
  404.3 23.5 %collective-permute-start.46 = (bf16[1152,384]{1,0:T(8,128)(2,1)S(1)}, bf16[1152,384]{1,0:T(8,128)(2,1)S(1)}, u32[]{:S(2)}, u32[]{:S(2)}) collective-permute-start(bf16[1152,384]{1,0:T(8,128)(2,1)S(1)} %add_convert_fusion.2), channel_id=1, source_target_pairs={{0,6},{1,7},{2,4},{3,5},{4,2},{5,3},{6,0},{7,1},{8,14},{9,15},{10,... | collective-permute-start | bytes 2654216 | tf_op jit(solution)/shard_map/ppermute | solution.py:81
  405.9 40.9 %collective-permute-start.45 = (bf16[1152,384]{1,0:T(8,128)(2,1)S(1)}, bf16[1152,384]{1,0:T(8,128)(2,1)S(1)}, u32[]{:S(2)}, u32[]{:S(2)}) collective-permute-start(bf16[1152,384]{1,0:T(8,128)(2,1)S(1)} %add_convert_fusion.1), channel_id=1, source_target_pairs={{0,4},{1,5},{2,6},{3,7},{4,0},{5,1},{6,2},{7,3},{8,12},{9,13},{10,... | collective-permute-start | bytes 2654216 | tf_op jit(solution)/shard_map/ppermute | solution.py:81
  406.9 41.0 %collective-permute-start.44 = (bf16[1152,384]{1,0:T(8,128)(2,1)S(1)}, bf16[1152,384]{1,0:T(8,128)(2,1)S(1)}, u32[]{:S(2)}, u32[]{:S(2)}) collective-permute-start(bf16[1152,384]{1,0:T(8,128)(2,1)S(1)} %add_convert_fusion), channel_id=1, source_target_pairs={{0,2},{1,3},{2,0},{3,1},{4,6},{5,7},{6,4},{7,5},{8,10},{9,11},{10,... | collective-permute-start | bytes 2654216 | tf_op jit(solution)/shard_map/ppermute | solution.py:81
  407.9 2.7 collective-permute-start.42
  407.9 4.0 collective-permute-start.40
  410.6 2.9 collective-permute-start.38
  411.8 57.6 %collective-permute-start.37 = (bf16[1152,256]{1,0:T(8,128)(2,1)S(1)}, bf16[1152,256]{1,0:T(8,128)(2,1)S(1)}, u32[]{:S(2)}, u32[]{:S(2)}) collective-permute-start(bf16[1152,256]{1,0:T(8,128)(2,1)S(1)} %convolution_convert_fusion.7), channel_id=1, source_target_pairs={{0,1},{1,0},{2,3},{3,2},{4,5},{5,4},{6,7},{7,6},{8,9},{9,8},{10,11... | collective-permute-start | bytes 1769480 | tf_op jit(solution)/shard_map/ppermute | solution.py:81
  413.5 34.4 %copy-start.16 = (f32[1152]{0:T(1024)S(1)}, f32[1152]{0:T(1024)}, u32[]{:S(2)}) copy-start(f32[1152]{0:T(1024)} %copy-done.15) | copy-start | bytes 13828
  413.5 34.4 %copy-start.18 = (f32[1152]{0:T(1024)S(1)}, f32[1152]{0:T(1024)}, u32[]{:S(2)}) copy-start(f32[1152]{0:T(1024)} %copy-done.17) | copy-start | bytes 13828
  413.5 55.9 %collective-permute-start.43 = (bf16[1152,256]{1,0:T(8,128)(2,1)S(1)}, bf16[1152,256]{1,0:T(8,128)(2,1)S(1)}, u32[]{:S(2)}, u32[]{:S(2)}) collective-permute-start(bf16[1152,256]{1,0:T(8,128)(2,1)S(1)} %add_convert_fusion.4), channel_id=1, source_target_pairs={{0,6},{1,7},{2,4},{3,5},{4,2},{5,3},{6,0},{7,1},{8,14},{9,15},{10,... | collective-permute-start | bytes 1769480 | tf_op jit(solution)/shard_map/ppermute | solution.py:81
  427.8 43.1 %collective-permute-start.41 = (bf16[1152,256]{1,0:T(8,128)(2,1)S(1)}, bf16[1152,256]{1,0:T(8,128)(2,1)S(1)}, u32[]{:S(2)}, u32[]{:S(2)}) collective-permute-start(bf16[1152,256]{1,0:T(8,128)(2,1)S(1)} %add_convert_fusion.5), channel_id=1, source_target_pairs={{0,4},{1,5},{2,6},{3,7},{4,0},{5,1},{6,2},{7,3},{8,12},{9,13},{10,... | collective-permute-start | bytes 1769480 | tf_op jit(solution)/shard_map/ppermute | solution.py:81
  446.8 24.1 %collective-permute-start.39 = (bf16[1152,256]{1,0:T(8,128)(2,1)S(1)}, bf16[1152,256]{1,0:T(8,128)(2,1)S(1)}, u32[]{:S(2)}, u32[]{:S(2)}) collective-permute-start(bf16[1152,256]{1,0:T(8,128)(2,1)S(1)} %add_convert_fusion.6), channel_id=1, source_target_pairs={{0,2},{1,3},{2,0},{3,1},{4,6},{5,7},{6,4},{7,5},{8,10},{9,11},{10,... | collective-permute-start | bytes 1769480 | tf_op jit(solution)/shard_map/ppermute | solution.py:81
  449.1 3.6 collective-permute-start.50
  452.8 6.6 %collective-permute-start.51 = (bf16[3,48,384]{2,1,0:T(8,128)(2,1)S(1)}, bf16[3,48,384]{2,1,0:T(8,128)(2,1)S(1)}, u32[]{:S(2)}, u32[]{:S(2)}) collective-permute-start(bf16[3,48,384]{2,1,0:T(8,128)(2,1)S(1)} %bitcast.66), channel_id=1, source_target_pairs={{8,0},{24,16},{9,1},{25,17},{10,2},{26,18},{11,3},{27,19},{12,4},{... | collective-permute-start | bytes 331784 | tf_op jit(solution)/shard_map/ppermute | solution.py:76
  459.4 12.0 %copy-start.25 = (f32[384]{0:T(512)S(1)}, f32[384]{0:T(512)}, u32[]{:S(2)}) copy-start(f32[384]{0:T(512)} %param.18) | copy-start | bytes 4612
  (22 other events, 113.6 us)
Sparse Core Ops, SparseCore 0:
  9.6 232.3 all-gather.4
  243.6 115.4 all-gather.2
where the time goes:
time: 484 us; the launch traced here: 480 us
  waiting for transfers between devices  240 us (50%)
  matrix products  82.5 us (17%)
  starting transfers between devices  44.6 us (9%)
  local copies, waits for them, and re-layouts  43.3 us (9%)
  blocking collectives  25.9 us (5%)
  Pallas kernels  19 us (4%)
  between operations  15.1 us (3%)
  other arithmetic  9.65 us (2%)
    ppermute x45, waiting for transfers between devices, swap(): return lax.ppermute(value, 'col', [(i, i ^ distance) for i in range(count)])  85.5 us
    ppermute x2, waiting for transfers between devices, halo(): lax.ppermute(field[-3:], 'row', down)  62.4 us
    ppermute x3, waiting for transfers between devices, gather_rows(): arrived = lax.ppermute(piece, 'row', pairs) if distance else piece  49.6 us
    dot_general x10, matrix products, turned(): lax.dot_general(left, right, (((1,), (1,)), ((), ())), preferred_element_...  38.4 us
    all_gather x1, waiting for transfers between devices, body(): lax.all_gather(owners[:, :, cut:].reshape(units, -1), 'row', axis=1, tile...  37.1 us
    ppermute x45, starting transfers between devices, swap(): return lax.ppermute(value, 'col', [(i, i ^ distance) for i in range(count)])  31.4 us
    psum x1, blocking collectives, body(): lax.psum((jnp.sum(local_mixed, 1), jnp.sum(local_mixed * local_mixed, 1))...  25.9 us
    dot_general x16, matrix products, branch_part(): dot(activated, lax.dynamic_slice_in_dim(weights, owner * width, width, 1))  19.1 us
  transfers between devices with their start and end apart: 54, of which 15 were waited for; matrix products, arithmetic and copies ran while one was open for 22% of the time, Pallas kernels for 4%

commit v1 on v0

v1 whole, which is shorter than its diff:
```python
import functools

import jax
import jax.numpy as jnp
from jax import lax
from jax.experimental import pallas as pl
from jax.experimental.pallas import tpu as pltpu
from jax.sharding import PartitionSpec as P

H = 48
LANES = 128

epsilon = 1e-06
root_half = 0.7071067811865476
density_scale = 0.3989422804014327


def conv_kernel(flip, add, x_ref, top_ref, bottom_ref, k_ref, *rest):
    if add:
        add_ref, o_ref, field = rest
    else:
        o_ref, field = rest
    rows, width, lanes = x_ref.shape
    field[...] = jnp.zeros_like(field)
    field[0:3, 8 : 8 + width, :] = top_ref[...].astype(jnp.float32)
    field[3 : 3 + rows, 8 : 8 + width, :] = x_ref[...].astype(jnp.float32)
    field[3 + rows : 6 + rows, 8 : 8 + width, :] = bottom_ref[...].astype(jnp.float32)

    @pl.loop(0, rows)
    def _(r):
        total = jnp.zeros((width, lanes), jnp.float32)
        for a in range(7):
            for b in range(7):
                weight = k_ref[6 - a, 6 - b] if flip else k_ref[a, b]
                total += weight[None, :] * field[r + a, 5 + b : 5 + b + width, :]
        mixed = total.astype(jnp.bfloat16)
        if add:
            mixed = (add_ref[r].astype(jnp.float32) + mixed.astype(jnp.float32)).astype(
                jnp.bfloat16
            )
        o_ref[r] = mixed


def depthwise(field, top, bottom, kernel, flip, add=None):
    rows, width, channels = field.shape
    lanes = LANES if channels % LANES == 0 else channels
    block = lambda n: pl.BlockSpec((n, width, lanes), lambda i: (0, 0, i))
    operands = [field, top, bottom, kernel]
    specs = [block(rows), block(3), block(3), pl.BlockSpec((7, 7, lanes), lambda i: (0, 0, i))]
    if add is not None:
        operands.append(add)
        specs.append(block(rows))
    return pl.pallas_call(
        functools.partial(conv_kernel, flip, add is not None),
        out_shape=jax.ShapeDtypeStruct(field.shape, jnp.bfloat16),
        grid=(channels // lanes,),
        in_specs=specs,
        out_specs=block(rows),
        scratch_shapes=[pltpu.VMEM((rows + 6, width + 16, lanes), jnp.float32)],
        compiler_params=pltpu.CompilerParams(vmem_limit_bytes=32 * 2**20),
        cost_estimate=pl.CostEstimate(
            flops=98 * rows * width * channels,
            bytes_accessed=6 * rows * width * channels,
            transcendentals=0,
        ),
        name="depthwise_flipped" if flip else "depthwise",
    )(*operands)


def halo(field):
    rows = field.shape[0]
    per_image = H // rows
    count = lax.axis_size("row")
    down = [(i, i + 1) for i in range(count - 1) if (i + 1) % per_image]
    up = [(j, i) for i, j in down]
    return lax.ppermute(field[-3:], "row", down), lax.ppermute(field[:3], "row", up)


MATMUL_VMEM = 56 * 2**20


def exchange(value, row_distance=0, masks=(0, 0), parity=0):
    rows, cols = lax.axis_size("row"), lax.axis_size("col")
    pairs = []
    for r in range(rows):
        mask = masks[0] if r % 2 == parity else masks[1]
        for c in range(cols):
            pairs.append((r * cols + c, (r ^ row_distance) * cols + (c ^ mask)))
    return lax.ppermute(value, ("row", "col"), pairs)


def orders():
    count = lax.axis_size("col")
    bits = [1 << b for b in range(1, count.bit_length() - 1)]
    half = len(bits) // 2
    return bits, bits[half:] + bits[:half]


def gather_pieces(piece, parity):
    first, second = orders()
    held = [(piece, 0, 0)]
    for one, two in zip(first, second):
        held += [
            (exchange(value, 0, (one, two), parity), a ^ one, b ^ two) for value, a, b in held
        ]
    held += [(exchange(value, 0, (1, 1)), a ^ 1, b ^ 1) for value, a, b in held]
    mine = lax.axis_index("row") % 2 == parity
    me = lax.axis_index("col")
    owners = [me ^ jnp.where(mine, a, b) for _, a, b in held]
    return [value for value, _, _ in held], jnp.stack(owners).astype(jnp.int32)


def reduce_pieces(part, parity):
    first, second = orders()
    mine = lax.axis_index("row") % 2 == parity
    me = lax.axis_index("col")
    offsets = [(0, 0)]
    for one, two in zip(first, second):
        offsets += [(a ^ one, b ^ two) for a, b in offsets]
    order = list(reversed(offsets))
    owner = lambda pair: me ^ jnp.where(mine, pair[0], pair[1])
    arrived = [
        exchange(part(owner(pair) ^ 1).astype(jnp.bfloat16), 0, (1, 1)) for pair in order
    ]
    sums = [part(owner(pair)) + got.astype(jnp.float32) for pair, got in zip(order, arrived)]
    sums.reverse()
    for one, two in reversed(list(zip(first, second))):
        half = len(sums) // 2
        moved = [
            exchange(value.astype(jnp.bfloat16), 0, (one, two), parity) for value in sums[half:]
        ]
        sums = [keep + got.astype(jnp.float32) for keep, got in zip(sums[:half], moved)]
    return sums[0]


def expand_kernel(count, channels, owners, *refs):
    pieces = refs[:count]
    weights, bias, gain, shift, hidden, slope, preact_out, mean_out, inv_out = refs[count:]
    total = square = 0.0
    for ref in pieces:
        value = ref[...].astype(jnp.float32)
        total += jnp.sum(value, 1, keepdims=True)
        square += jnp.sum(value * value, 1, keepdims=True)
    mean = total / channels
    inv = lax.rsqrt(square / channels - mean * mean + epsilon)
    preact = bias[...]
    for index, ref in enumerate(pieces):
        owner = owners[index]
        normal = (ref[...].astype(jnp.float32) - mean) * inv
        normed = (normal * gain[owner] + shift[owner]).astype(jnp.bfloat16)
        preact = preact + jnp.dot(normed, weights[owner], preferred_element_type=jnp.float32)
    cumulative = 0.5 * (1.0 + lax.erf(preact * root_half))
    hidden[...] = (preact * cumulative).astype(jnp.bfloat16)
    slope[...] = cumulative + preact * jnp.exp(-0.5 * preact * preact) * density_scale
    preact_out[...] = preact
    mean_out[...] = mean
    inv_out[...] = inv


def token_tile(tokens):
    for tile in (384, 288, 192, 96, 64, 48, 32, 16):
        if tokens % tile == 0:
            return tile
    return tokens


def expand(pieces, owners, weights, bias, gain, shift, channels):
    tokens, narrow = pieces[0].shape
    count, _, units = weights.shape
    tile = token_tile(tokens)
    row = lambda width: pl.BlockSpec((tile, width), lambda i, *_: (i, 0))
    whole = lambda array: pl.BlockSpec(array.shape, lambda i, *_: (0,) * array.ndim)
    operands = [weights, bias[None, :], gain.reshape(count, 1, narrow), shift.reshape(count, 1, narrow)]
    wide = jax.ShapeDtypeStruct((tokens, units), jnp.float32)
    thin = jax.ShapeDtypeStruct((tokens, 1), jnp.float32)
    return pl.pallas_call(
        functools.partial(expand_kernel, count, channels),
        grid_spec=pltpu.PrefetchScalarGridSpec(
            num_scalar_prefetch=1,
            grid=(tokens // tile,),
            in_specs=[row(narrow)] * count + [whole(array) for array in operands],
            out_specs=[row(units), row(units), row(units), row(1), row(1)],
        ),
        out_shape=[jax.ShapeDtypeStruct((tokens, units), jnp.bfloat16), wide, wide, thin, thin],
        compiler_params=pltpu.CompilerParams(vmem_limit_bytes=MATMUL_VMEM),
        cost_estimate=pl.CostEstimate(
            flops=2 * tokens * channels * units,
            bytes_accessed=2 * tokens * channels + 2 * channels * units + 10 * tokens * units,
            transcendentals=2 * tokens * units,
        ),
        name="expand",
    )(owners, *pieces, *operands)


def slope_kernel(count, owners, *refs):
    pieces = refs[:count]
    weights, slope, preact, known, vector, out, sums = refs[count:]
    grad_hidden = 0.0
    for index, ref in enumerate(pieces):
        grad_hidden += lax.dot_general(
            ref[...],
            weights[owners[index]],
            (((1,), (1,)), ((), ())),
            preferred_element_type=jnp.float32,
        )
    grad = (grad_hidden * slope[...]).astype(jnp.bfloat16)
    out[...] = grad
    grad = grad.astype(jnp.float32)
    total = jnp.sum(grad * vector[...], 1, keepdims=True)
    cross = jnp.sum(grad * (preact[...] - known[...]), 1, keepdims=True)
    sums[...] = jnp.concatenate([total, cross], 1)


def grad_units(pieces, owners, weights, slope, preact, known, vector):
    tokens, narrow = pieces[0].shape
    count, units, _ = weights.shape
    tile = token_tile(tokens)
    row = lambda width: pl.BlockSpec((tile, width), lambda i, *_: (i, 0))
    whole = lambda array: pl.BlockSpec(array.shape, lambda i, *_: (0,) * array.ndim)
    return pl.pallas_call(
        functools.partial(slope_kernel, count),
        grid_spec=pltpu.PrefetchScalarGridSpec(
            num_scalar_prefetch=1,
            grid=(tokens // tile,),
            in_specs=[row(narrow)] * count
            + [whole(weights), row(units), row(units)]
            + [pl.BlockSpec((1, units), lambda i, *_: (0, 0))] * 2,
            out_specs=[row(units), row(2)],
        ),
        out_shape=[
            jax.ShapeDtypeStruct((tokens, units), jnp.bfloat16),
            jax.ShapeDtypeStruct((tokens, 2), jnp.float32),
        ],
        compiler_params=pltpu.CompilerParams(vmem_limit_bytes=MATMUL_VMEM),
        cost_estimate=pl.CostEstimate(
            flops=2 * tokens * count * narrow * units,
            bytes_accessed=2 * (tokens + units) * count * narrow + 10 * tokens * units,
            transcendentals=0,
        ),
        name="grad_units",
    )(owners, *pieces, weights, slope, preact, known[None, :], vector[None, :])


def body(
    activations,
    cotangent,
    kernel,
    ln_gain,
    ln_bias,
    w_expand,
    b_expand,
    w_reduce,
    b_reduce,
    layer_scale,
):
    row_count, grid_width, narrow = activations.shape
    rows, cols = lax.axis_size("row"), lax.axis_size("col")
    me_row, me_col = lax.axis_index("row"), lax.axis_index("col")
    channels = narrow * cols
    depth = channels // rows
    tokens = row_count * grid_width
    units = w_expand.shape[1] // 2
    parity = me_row % 2

    top, bottom = halo(activations)
    cot_f = cotangent.astype(jnp.float32)
    grad_branch = (layer_scale * cot_f).reshape(tokens, narrow).astype(jnp.bfloat16)

    expand_halves = [
        lax.dynamic_slice_in_dim(w_expand, (parity ^ flip) * units, units, 1) for flip in (0, 1)
    ]
    slabs = w_reduce.reshape(2, units, depth // narrow, narrow).transpose(0, 2, 1, 3)
    reduce_halves = [
        lax.dynamic_index_in_dim(slabs, parity ^ flip, 0, keepdims=False) for flip in (0, 1)
    ]

    def assemble(halves, sent):
        own = halves[0]
        out = jnp.zeros((rows,) + own.shape, own.dtype)
        for distance in range(rows):
            block = sent[distance] if distance else own
            out = lax.dynamic_update_index_in_dim(out, block, me_row ^ distance, 0)
        return out

    expand_sent = [None] + [exchange(expand_halves[d % 2], d) for d in range(1, rows)]
    grad_partner = exchange(grad_branch, 1)
    grad_own_pieces, own_owners = gather_pieces(grad_branch, 0)
    grad_partner_pieces, partner_owners = gather_pieces(grad_partner, 1)

    mixed = depthwise(activations, top, bottom, kernel, False).reshape(tokens, narrow)
    mixed_partner = exchange(mixed, 1)
    mixed_own_pieces, _ = gather_pieces(mixed, 0)
    mixed_partner_pieces, _ = gather_pieces(mixed_partner, 1)

    held = lax.optimization_barrier((*reduce_halves, *expand_sent[1:]))
    reduce_halves, expand_sent = held[:2], (None,) + tuple(held[2:])
    reduce_sent = [None] + [exchange(reduce_halves[d % 2], d) for d in range(1, rows)]

    expand_full = assemble(expand_halves, expand_sent).reshape(cols, narrow, units)
    bias = lax.dynamic_slice_in_dim(b_expand, parity * units, units)
    own = expand(mixed_own_pieces, own_owners, expand_full, bias, ln_gain, ln_bias, channels)
    other = expand(
        mixed_partner_pieces, partner_owners, expand_full, bias, ln_gain, ln_bias, channels
    )
    mean, inv_std = own[3], own[4]
    vectors = jnp.stack([ln_gain, ln_bias])
    gain_unit, bias_unit = jnp.dot(
        vectors,
        expand_full.reshape(channels, units).astype(jnp.float32),
        precision=lax.Precision.HIGHEST,
    )

    reduce_full = assemble(reduce_halves, reduce_sent).reshape(cols, units, narrow)
    known = bias + bias_unit
    grad_own, sums_own = grad_units(
        grad_own_pieces, own_owners, reduce_full, own[1], own[2], known, gain_unit
    )
    grad_other, sums_other = grad_units(
        grad_partner_pieces, partner_owners, reduce_full, other[1], other[2], known, gain_unit
    )

    def branch_part(hidden):
        return lambda owner: jnp.dot(
            hidden,
            lax.dynamic_index_in_dim(reduce_full, owner, 0, keepdims=False),
            preferred_element_type=jnp.float32,
        )

    def grad_part(grad):
        return lambda owner: lax.dot_general(
            grad,
            lax.dynamic_index_in_dim(expand_full, owner, 0, keepdims=False),
            (((1,), (1,)), ((), ())),
            preferred_element_type=jnp.float32,
        )

    def pair_sum(part, own_value, other_value):
        away = reduce_pieces(part(other_value), 1).astype(jnp.bfloat16)
        return reduce_pieces(part(own_value), 0) + exchange(away, 1).astype(jnp.float32)

    branch = pair_sum(branch_part, own[0], other[0]) + b_reduce
    local_gain = lax.dynamic_slice_in_dim(ln_gain, me_col * narrow, narrow)
    grad_gain = pair_sum(grad_part, grad_own, grad_other) * local_gain

    sums = sums_own.T + exchange(sums_other.T, 1)
    distance = 1
    while distance < cols:
        sums = sums + exchange(sums, 0, (distance, distance))
        distance *= 2
    normal = (mixed.astype(jnp.float32) - mean) * inv_std
    grad_mixed = inv_std * (
        grad_gain - sums[0][:, None] / channels - normal * sums[1][:, None] / channels
    )
    grad_mixed = grad_mixed.astype(jnp.bfloat16).reshape(row_count, grid_width, narrow)
    top, bottom = halo(grad_mixed)
    grad_input = depthwise(grad_mixed, top, bottom, kernel, True, cotangent)

    act_f = activations.astype(jnp.float32)
    block_out = (act_f + layer_scale * branch.reshape(row_count, grid_width, narrow)).astype(
        jnp.bfloat16
    )
    return (block_out, grad_input)


def solution(mesh):
    return jax.shard_map(
        body,
        mesh=mesh,
        in_specs=(
            P("row", None, "col"),
            P("row", None, "col"),
            P(None, None, "col"),
            P(),
            P(),
            P("row", "col"),
            P("col"),
            P("col", "row"),
            P("col"),
            P("col"),
        ),
        out_specs=(P("row", None, "col"), P("row", None, "col")),
        check_vma=False,
    )
```

time: 484 us -> 549 us (1.13)
  Pallas kernels: 19 us -> 83 us
  waiting for transfers between devices: 240 us -> 286 us
  starting transfers between devices: 44.6 us -> 85.6 us
  matrix products: 82.5 us -> 50.8 us
  blocking collectives: 25.9 us -> 0 us
  local copies, waits for them, and re-layouts: 43.3 us -> 28.8 us
  between operations: 15.1 us -> 2.15 us
    ppermute x48 -> x70, waiting for transfers between devices: 135 us -> 258 us  [exchange(): return lax.ppermute(value, ('row', 'col'), pairs)]
    pallas_call x0 -> x4, Pallas kernels: none -> 64 us  [the longest x2 35 us: expand(): pl.pallas_call(functools.partial(expand_kernel, count, channels), grid_sp...]
    ppermute x2, waiting for transfers between devices: 62.4 us -> 1.26 us  [halo(): lax.ppermute(field[-3:], 'row', down)]
    ppermute x48 -> x70, starting transfers between devices: 38.2 us -> 76.1 us  [exchange(): return lax.ppermute(value, ('row', 'col'), pairs)]
    all_gather x2 -> x0, waiting for transfers between devices: 37.1 us -> none  [the longest x1 37.1 us: body(): lax.all_gather(owners[:, :, cut:].reshape(units, -1), 'row', axis=1, tile...]
    dot_general x28 -> x33, matrix products: 82.5 us -> 50.8 us  [the longest x16 27.8 us: grad_part(): lax.dot_general(grad, lax.dynamic_index_in_dim(expand_full, owner, 0, kee...]
    psum x1 -> x0, blocking collectives: 25.9 us -> none  [body(): lax.psum((jnp.sum(local_mixed, 1), jnp.sum(local_mixed * local_mixed, 1))...]
    ppermute x2, waiting for transfers between devices: 4.24 us -> 27.1 us  [halo(): lax.ppermute(field[:3], 'row', up)]
  transfers between devices with their start and end apart: 54 -> 74, of which waited for: 15 -> 27; matrix products, arithmetic and copies ran while one was open for 22% -> 12% of each run, Pallas kernels for 4% -> 8%
where the time goes in v1:
time: 549 us; the launch traced here: 542 us
  waiting for transfers between devices  286 us (52%)
  starting transfers between devices  85.6 us (16%)
  Pallas kernels  83 us (15%)
  matrix products  50.8 us (9%)
  local copies, waits for them, and re-layouts  28.8 us (5%)
    ppermute x70, waiting for transfers between devices, exchange(): return lax.ppermute(value, ('row', 'col'), pairs)  258 us
    ppermute x70, starting transfers between devices, exchange(): return lax.ppermute(value, ('row', 'col'), pairs)  76.1 us
    pallas_call x2, Pallas kernels, expand(): pl.pallas_call(functools.partial(expand_kernel, count, channels), grid_sp...  35 us
    pallas_call x2, Pallas kernels, grad_units(): pl.pallas_call(functools.partial(slope_kernel, count), grid_spec=pltpu.Pr...  29 us
    dot_general x16, matrix products, grad_part(): lax.dot_general(grad, lax.dynamic_index_in_dim(expand_full, owner, 0, kee...  27.8 us
    ppermute x2, waiting for transfers between devices, halo(): lax.ppermute(field[:3], 'row', up)  27.1 us
    dot_general x16, matrix products, branch_part(): jnp.dot(hidden, lax.dynamic_index_in_dim(reduce_full, owner, 0, keepdims=...  21 us
    pallas_call x2, Pallas kernels, depthwise(): pl.pallas_call(functools.partial(conv_kernel, flip, add is not None), out...  19 us
  transfers between devices with their start and end apart: 74, of which 27 were waited for; matrix products, arithmetic and copies ran while one was open for 12% of the time, Pallas kernels for 8%

profile of v1, /device:TPU:0, one launch (start us, length us, event | category | flops | bytes accessed | tf_op | source)
XLA Modules:
  0.0 541.7 jit_solution(3344165250315609958)
XLA Ops:
  0.7 2.4 constant_dynamic-slice_fusion
  3.1 5.0 collective-permute-start.11
  9.5 4.6 collective-permute-start
  14.1 22.8 %collective-permute-done.1.bottom_ref = bf16[3,48,384]{2,1,0:T(8,128)(2,1)S(1)} collective-permute-done((bf16[3,48,384]{2,1,0:T(8,128)(2,1)S(1)}, bf16[3,48,384]{2,1,0:T(8,128)(2,1)S(1)}, u32[]{:S(2)}, u32[]{:S(2)}) %collective-permute-start.1) | collective-permute-done | bytes 110624 | tf_op jit(solution)/shard_map/ppermute | solution.py:76
  37.2 9.0 %depthwise.1 = bf16[24,48,384]{2,1,0:T(8,128)(2,1)S(1)} custom-call(bf16[24,48,384]{2,1,0:T(8,128)(2,1)S(1)} %copy-done, bf16[3,48,384]{2,1,0:T(8,128)(2,1)S(1)} %collective-permute-done.top_ref, bf16[3,48,384]{2,1,0:T(8,128)(2,1)S(1)} %collective-permute-done.1.bottom_ref, f32[7,7,384]{2,1,0:T(8,128)S(1)} %copy-done.4), custom_call_target="tpu_custom_call" | custom-call | flops 43352064 | bytes 2654208 | tf_op jit(solution)/shard_map/depthwise/pallas_call | solution.py:53
  46.1 2.5 collective-permute-start.22
  50.3 2.2 copy-done.5
  52.5 1.4 collective-permute-start.10
  53.8 5.8 %reshape.48 = bf16[2,768,2,384]{3,2,1,0:T(2,128)(2,1)} reshape(bf16[1536,768]{1,0:T(8,128)(2,1)} %param.17) | data formatting | bytes 4718592 | tf_op jit(solution)/shard_map/reshape | solution.py:272
  60.9 3.2 constant_dynamic-slice_fusion.1
  64.1 39.3 %collective-permute-done.22.refs_0_ = bf16[1152,384]{1,0:T(8,128)(2,1)} collective-permute-done((bf16[1152,384]{1,0:T(8,128)(2,1)S(1)}, bf16[1152,384]{1,0:T(8,128)(2,1)}, u32[]{:S(2)}, u32[]{:S(2)}) %collective-permute-start.22) | collective-permute-done | bytes 884768 | tf_op jit(solution)/shard_map/ppermute | solution.py:89
  103.5 1.5 collective-permute-start.3
  105.0 1.5 collective-permute-start.2
  107.4 2.1 collective-permute-done.10
  110.0 1.4 bitcast_dynamic-update-slice_fusion.6
  111.4 2.6 collective-permute-start.12
  114.0 1.4 bitcast_dynamic-update-slice_fusion.5
  115.4 9.6 %collective-permute-done.3.refs_2_ = bf16[1152,384]{1,0:T(8,128)(2,1)S(1)} collective-permute-done((bf16[1152,384]{1,0:T(8,128)(2,1)S(1)}, bf16[1152,384]{1,0:T(8,128)(2,1)S(1)}, u32[]{:S(2)}, u32[]{:S(2)}) %collective-permute-start.3) | collective-permute-done | bytes 884768 | tf_op jit(solution)/shard_map/ppermute | solution.py:89
  125.0 1.5 collective-permute-start.23
  128.2 1.9 fusion.99
  130.1 15.2 %collective-permute-done.24.refs_2_ = bf16[1152,384]{1,0:T(8,128)(2,1)} collective-permute-done((bf16[1152,384]{1,0:T(8,128)(2,1)}, bf16[1152,384]{1,0:T(8,128)(2,1)}, u32[]{:S(2)}, u32[]{:S(2)}) %collective-permute-start.24) | collective-permute-done | bytes 884768 | tf_op jit(solution)/shard_map/ppermute | solution.py:89
  145.3 4.6 collective-permute-start.14
  150.7 14.2 %collective-permute-done.4.refs_3_ = bf16[1152,384]{1,0:T(8,128)(2,1)S(1)} collective-permute-done((bf16[1152,384]{1,0:T(8,128)(2,1)S(1)}, bf16[1152,384]{1,0:T(8,128)(2,1)S(1)}, u32[]{:S(2)}, u32[]{:S(2)}) %collective-permute-start.4) | collective-permute-done | bytes 884768 | tf_op jit(solution)/shard_map/ppermute | solution.py:89
  165.0 1.6 collective-permute-start.25
  167.1 22.4 %collective-permute-done.12 = bf16[2,768,384]{2,1,0:T(8,128)(2,1)S(1)} collective-permute-done((bf16[2,768,384]{2,1,0:T(8,128)(2,1)S(1)}, bf16[2,768,384]{2,1,0:T(8,128)(2,1)S(1)}, u32[]{:S(2)}, u32[]{:S(2)}) %collective-permute-start.12) | collective-permute-done | bytes 1179680 | tf_op jit(solution)/shard_map/ppermute | solution.py:89
  193.1 17.4 %expand.2 = (bf16[1152,768]{1,0:T(8,128)(2,1)}, f32[1152,768]{1,0:T(8,128)}, f32[1152,768]{1,0:T(8,128)}, f32[1152,1]{1,0:T(8,128)}, f32[1152,1]{1,0:T(8,128)}) custom-call(s32[8]{0:T(128)} %stack.63.owners, bf16[1152,384]{1,0:T(8,128)(2,1)} %bitcast.178, bf16[1152,384]{1,0:T(8,128)(2,1)} %copy-done.18, bf16[1152,384]{1,0:T(8,128)(2,1)} %copy-done.17, ...), custom_call_target="tpu_custom_call" | custom-call | flops 5435817984 | bytes 20643840 | tf_op jit(solution)/shard_map/expand/pallas_call | solution.py:176
  210.6 2.6 convolution_convert_fusion.13
  213.2 17.6 %expand.3 = (bf16[1152,768]{1,0:T(8,128)(2,1)}, f32[1152,768]{1,0:T(8,128)}, f32[1152,768]{1,0:T(8,128)}, f32[1152,1]{1,0:T(8,128)}, f32[1152,1]{1,0:T(8,128)}) custom-call(s32[8]{0:T(128)} %stack.68.owners, bf16[1152,384]{1,0:T(8,128)(2,1)} %collective-permute-done.22.refs_0_, bf16[1152,384]{1,0:T(8,128)(2,1)} %collective-permute-done.23.refs_1_, ...), custom_call_target="tpu_custom_call" | custom-call | flops 5435817984 | bytes 20643840 | tf_op jit(solution)/shard_map/expand/pallas_call | solution.py:176
  230.8 2.7 convolution_convert_fusion.8
  245.6 1.6 collective-permute-start.20
  247.2 15.6 %collective-permute-done.35 = bf16[1152,384]{1,0:T(8,128)(2,1)S(1)} collective-permute-done((bf16[1152,384]{1,0:T(8,128)(2,1)S(1)}, bf16[1152,384]{1,0:T(8,128)(2,1)S(1)}, u32[]{:S(2)}, u32[]{:S(2)}) %collective-permute-start.35) | collective-permute-done | bytes 884768 | tf_op jit(solution)/shard_map/ppermute | solution.py:89
  265.2 1.6 collective-permute-start.36
  271.8 13.6 %collective-permute-done.32 = bf16[1152,384]{1,0:T(8,128)(2,1)S(1)} collective-permute-done((bf16[1152,384]{1,0:T(8,128)(2,1)S(1)}, bf16[1152,384]{1,0:T(8,128)(2,1)S(1)}, u32[]{:S(2)}, u32[]{:S(2)}) %collective-permute-start.32) | collective-permute-done | bytes 884768 | tf_op jit(solution)/shard_map/ppermute | solution.py:89
  285.4 2.4 collective-permute-done.36
  289.1 22.4 %collective-permute-start.37 = (bf16[1152,384]{1,0:T(8,128)(2,1)S(1)}, bf16[1152,384]{1,0:T(8,128)(2,1)S(1)}, u32[]{:S(2)}, u32[]{:S(2)}) collective-permute-start(bf16[1152,384]{1,0:T(8,128)(2,1)S(1)} %fusion.29), channel_id=1, source_target_pairs={{0,8},{1,9},{2,10},{3,11},{4,12},{5,13},{6,14},{7,15},{8,0},{9,1},... | collective-permute-start | bytes 2654216 | tf_op jit(solution)/shard_map/ppermute | solution.py:89
  311.5 18.0 %collective-permute-done.37 = bf16[1152,384]{1,0:T(8,128)(2,1)S(1)} collective-permute-done((bf16[1152,384]{1,0:T(8,128)(2,1)S(1)}, bf16[1152,384]{1,0:T(8,128)(2,1)S(1)}, u32[]{:S(2)}, u32[]{:S(2)}) %collective-permute-start.37) | collective-permute-done | bytes 884768 | tf_op jit(solution)/shard_map/ppermute | solution.py:89
  329.5 1.4 fusion.18
  330.9 1.4 multiply_convert_fusion
  332.3 1.7 collective-permute-start.52
  335.8 15.7 %collective-permute-done.52.refs_0_ = bf16[1152,384]{1,0:T(8,128)(2,1)S(1)} collective-permute-done((bf16[1152,384]{1,0:T(8,128)(2,1)S(1)}, bf16[1152,384]{1,0:T(8,128)(2,1)S(1)}, u32[]{:S(2)}, u32[]{:S(2)}) %collective-permute-start.52) | collective-permute-done | bytes 884768 | tf_op jit(solution)/shard_map/ppermute | solution.py:89
  354.8 1.7 collective-permute-done.39.refs_2_
  356.9 18.5 %collective-permute-done.53.refs_1_ = bf16[1152,384]{1,0:T(8,128)(2,1)} collective-permute-done((bf16[1152,384]{1,0:T(8,128)(2,1)S(1)}, bf16[1152,384]{1,0:T(8,128)(2,1)}, u32[]{:S(2)}, u32[]{:S(2)}) %collective-permute-start.53) | collective-permute-done | bytes 884768 | tf_op jit(solution)/shard_map/ppermute | solution.py:89
  375.8 15.7 %collective-permute-done.40.refs_3_ = bf16[1152,384]{1,0:T(8,128)(2,1)S(1)} collective-permute-done((bf16[1152,384]{1,0:T(8,128)(2,1)S(1)}, bf16[1152,384]{1,0:T(8,128)(2,1)S(1)}, u32[]{:S(2)}, u32[]{:S(2)}) %collective-permute-start.40) | collective-permute-done | bytes 884768 | tf_op jit(solution)/shard_map/ppermute | solution.py:89
  395.3 14.5 %grad_units.2 = (bf16[1152,768]{1,0:T(8,128)(2,1)}, f32[1152,2]{1,0:T(8,128)}) custom-call(s32[8]{0:T(128)} %stack.63.owners, bf16[1152,384]{1,0:T(8,128)(2,1)} %bitcast.224, bf16[1152,384]{1,0:T(8,128)(2,1)} %copy-done.21, bf16[1152,384]{1,0:T(8,128)(2,1)} %copy-done.22, bf16[1152,384]{1,0:T(8,128)(2,1)} %copy-done.26, bf16[1152,384]{1,0:T(8,128)(2,1)} %copy-done.23, ...), custom_call_target="tpu_custom_call" | custom-call | flops 5435817984 | bytes 20643840 | tf_op jit(solution)/shard_map/grad_units/pallas_call | solution.py:220
  409.8 2.6 convolution_convert_fusion.5
  412.4 14.6 %grad_units.3 = (bf16[1152,768]{1,0:T(8,128)(2,1)}, f32[1152,2]{1,0:T(8,128)}) custom-call(s32[8]{0:T(128)} %stack.68.owners, bf16[1152,384]{1,0:T(8,128)(2,1)} %copy-done.19, bf16[1152,384]{1,0:T(8,128)(2,1)} %collective-permute-done.53.refs_1_, bf16[1152,384]{1,0:T(8,128)(2,1)} %collective-permute-done.54.refs_2_, ...), custom_call_target="tpu_custom_call" | custom-call | flops 5435817984 | bytes 20643840 | tf_op jit(solution)/shard_map/grad_units/pallas_call | solution.py:220
  427.0 2.7 convolution_convert_fusion
  442.1 16.9 %collective-permute-done.65 = bf16[1152,384]{1,0:T(8,128)(2,1)S(1)} collective-permute-done((bf16[1152,384]{1,0:T(8,128)(2,1)S(1)}, bf16[1152,384]{1,0:T(8,128)(2,1)S(1)}, u32[]{:S(2)}, u32[]{:S(2)}) %collective-permute-start.65) | collective-permute-done | bytes 884768 | tf_op jit(solution)/shard_map/ppermute | solution.py:89
  461.4 2.0 convolution_convert_fusion.7
  463.5 2.1 fusion.23
  465.5 1.6 collective-permute-start.47
  467.1 2.3 fusion.32
  470.7 10.8 %collective-permute-done.62 = bf16[1152,384]{1,0:T(8,128)(2,1)S(1)} collective-permute-done((bf16[1152,384]{1,0:T(8,128)(2,1)S(1)}, bf16[1152,384]{1,0:T(8,128)(2,1)S(1)}, u32[]{:S(2)}, u32[]{:S(2)}) %collective-permute-start.62) | collective-permute-done | bytes 884768 | tf_op jit(solution)/shard_map/ppermute | solution.py:89
  481.5 2.0 collective-permute-done.66
  483.5 2.2 fusion.28
  486.5 1.5 collective-permute-start.68
  488.0 18.0 %collective-permute-done.68 = f32[2,1152]{1,0:T(2,128)S(1)} collective-permute-done((f32[2,1152]{1,0:T(2,128)S(1)}, f32[2,1152]{1,0:T(2,128)S(1)}, u32[]{:S(2)}, u32[]{:S(2)}) %collective-permute-start.68) | collective-permute-done | bytes 9248 | tf_op jit(solution)/shard_map/ppermute | solution.py:89
  509.5 2.4 collective-permute-done.70
  513.8 1.3 reduce
  515.1 1.3 reduce.3
  518.3 3.9 fusion.27
  522.2 2.4 collective-permute-start.72
  526.9 4.3 collective-permute-done.73.bottom_ref
  531.2 10.1 %depthwise_flipped.1 = bf16[24,48,384]{2,1,0:T(8,128)(2,1)} custom-call(bf16[24,48,384]{2,1,0:T(8,128)(2,1)S(1)} %bitcast.173, bf16[3,48,384]{2,1,0:T(8,128)(2,1)S(1)} %collective-permute-done.72.top_ref, bf16[3,48,384]{2,1,0:T(8,128)(2,1)S(1)} %collective-permute-done.73.bottom_ref, f32[7,7,384]{2,1,0:T(8,128)S(1)} %copy-done.4, ...), custom_call_target="tpu_custom_call" | custom-call | flops 43352064 | bytes 2654208 | tf_op jit(solution)/shard_map/depthwise_flipped/pallas_call | solution.py:53
  (241 shorter events, 68.8 us)
Async XLA Ops:
  3.1 101.9 %collective-permute-start.11 = (bf16[768,768]{1,0:T(8,128)(2,1)}, bf16[768,768]{1,0:T(8,128)(2,1)S(1)}, u32[]{:S(2)}, u32[]{:S(2)}) collective-permute-start(bf16[768,768]{1,0:T(8,128)(2,1)} %constant_dynamic-slice_fusion), channel_id=1, source_target_pairs={{0,24},{1,25},{2,26},{3,27},{4,28},{5,29},{6,30},{7,31},{8,16},{9,... | collective-permute-start | bytes 3538952 | tf_op jit(solution)/shard_map/ppermute | solution.py:89
  8.2 28.7 %collective-permute-start.1 = (bf16[3,48,384]{2,1,0:T(8,128)(2,1)S(1)}, bf16[3,48,384]{2,1,0:T(8,128)(2,1)S(1)}, u32[]{:S(2)}, u32[]{:S(2)}) collective-permute-start(bf16[3,48,384]{2,1,0:T(8,128)(2,1)S(1)} %get-tuple-element.46), channel_id=1, source_target_pairs={{8,0},{24,16},{9,1},{25,17},{10,2},{26,18},{11,3},{27,19},{12,4},{... | collective-permute-start | bytes 331784 | tf_op jit(solution)/shard_map/ppermute | solution.py:76
  9.5 27.7 %collective-permute-start = (bf16[3,48,384]{2,1,0:T(8,128)(2,1)S(1)}, bf16[3,48,384]{2,1,0:T(8,128)(2,1)S(1)}, u32[]{:S(2)}, u32[]{:S(2)}) collective-permute-start(bf16[3,48,384]{2,1,0:T(8,128)(2,1)S(1)} %get-tuple-element.47), channel_id=1, source_target_pairs={{0,8},{16,24},{1,9},{17,25},{2,10},{18,26},{3,11},{19,27},{4,12},{... | collective-permute-start | bytes 331784 | tf_op jit(solution)/shard_map/ppermute | solution.py:76
  14.0 92.8 %collective-permute-start.9 = (bf16[768,768]{1,0:T(8,128)(2,1)}, bf16[768,768]{1,0:T(8,128)(2,1)}, u32[]{:S(2)}, u32[]{:S(2)}) collective-permute-start(bf16[768,768]{1,0:T(8,128)(2,1)} %constant_dynamic-slice_fusion), channel_id=1, source_target_pairs={{0,8},{1,9},{2,10},{3,11},{4,12},{5,13},{6,14},{7,15},{8,0},{9,1},... | collective-permute-start | bytes 3538952 | tf_op jit(solution)/shard_map/ppermute | solution.py:89
  46.1 57.3 %collective-permute-start.22 = (bf16[1152,384]{1,0:T(8,128)(2,1)S(1)}, bf16[1152,384]{1,0:T(8,128)(2,1)}, u32[]{:S(2)}, u32[]{:S(2)}) collective-permute-start(bf16[1152,384]{1,0:T(8,128)(2,1)S(1)} %bitcast.174), channel_id=1, source_target_pairs={{0,8},{1,9},{2,10},{3,11},{4,12},{5,13},{6,14},{7,15},{8,0},{9,1},... | collective-permute-start | bytes 2654216 | tf_op jit(solution)/shard_map/ppermute | solution.py:89
  52.5 57.0 %collective-permute-start.10 = (bf16[768,768]{1,0:T(8,128)(2,1)}, bf16[768,768]{1,0:T(8,128)(2,1)}, u32[]{:S(2)}, u32[]{:S(2)}) collective-permute-start(bf16[768,768]{1,0:T(8,128)(2,1)} %get-tuple-element.41), channel_id=1, source_target_pairs={{0,16},{1,17},{2,18},{3,19},{4,20},{5,21},{6,22},{7,23},{8,24},{9,... | collective-permute-start | bytes 3538952 | tf_op jit(solution)/shard_map/ppermute | solution.py:89
  53.8 57.6 %collective-permute-start.5 = (bf16[1152,384]{1,0:T(8,128)(2,1)S(1)}, bf16[1152,384]{1,0:T(8,128)(2,1)}, u32[]{:S(2)}, u32[]{:S(2)}) collective-permute-start(bf16[1152,384]{1,0:T(8,128)(2,1)S(1)} %bitcast.175), channel_id=1, source_target_pairs={{0,1},{1,0},{2,3},{3,2},{4,5},{5,4},{6,7},{7,6},{8,9},{9,8},{10,11... | collective-permute-start | bytes 2654216 | tf_op jit(solution)/shard_map/ppermute | solution.py:89
  103.5 21.6 %collective-permute-start.3 = (bf16[1152,384]{1,0:T(8,128)(2,1)S(1)}, bf16[1152,384]{1,0:T(8,128)(2,1)S(1)}, u32[]{:S(2)}, u32[]{:S(2)}) collective-permute-start(bf16[1152,384]{1,0:T(8,128)(2,1)S(1)} %bitcast.176), channel_id=1, source_target_pairs={{0,4},{1,5},{2,6},{3,7},{4,0},{5,1},{6,2},{7,3},{8,10},{9,11},{10,... | collective-permute-start | bytes 2654216 | tf_op jit(solution)/shard_map/ppermute | solution.py:89
  105.0 22.6 %collective-permute-start.2 = (bf16[1152,384]{1,0:T(8,128)(2,1)S(1)}, bf16[1152,384]{1,0:T(8,128)(2,1)S(1)}, u32[]{:S(2)}, u32[]{:S(2)}) collective-permute-start(bf16[1152,384]{1,0:T(8,128)(2,1)S(1)} %bitcast.177), channel_id=1, source_target_pairs={{0,2},{1,3},{2,0},{3,1},{4,6},{5,7},{6,4},{7,5},{8,12},{9,13},{10,... | collective-permute-start | bytes 2654216 | tf_op jit(solution)/shard_map/ppermute | solution.py:89
  106.8 38.5 %collective-permute-start.24 = (bf16[1152,384]{1,0:T(8,128)(2,1)}, bf16[1152,384]{1,0:T(8,128)(2,1)}, u32[]{:S(2)}, u32[]{:S(2)}) collective-permute-start(bf16[1152,384]{1,0:T(8,128)(2,1)} %collective-permute-done.22.refs_0_), channel_id=1, source_target_pairs={{0,2},{1,3},{2,0},{3,1},{4,6},{5,7},{6,4},{7,5},{8,12},{9,13},{10,... | collective-permute-start | bytes 2654216 | tf_op jit(solution)/shard_map/ppermute | solution.py:89
  109.5 55.5 %collective-permute-start.13 = (bf16[2,768,384]{2,1,0:T(8,128)(2,1)S(1)}, bf16[2,768,384]{2,1,0:T(8,128)(2,1)S(1)}, u32[]{:S(2)}, u32[]{:S(2)}) collective-permute-start(bf16[2,768,384]{2,1,0:T(8,128)(2,1)S(1)} %get-tuple-element.23), channel_id=1, source_target_pairs={{0,16},{1,17},{2,18},{3,19},{4,20},{5,21},{6,22},{7,23},{8,24},{9,... | collective-permute-start | bytes 3538952 | tf_op jit(solution)/shard_map/ppermute | solution.py:89
  111.4 78.1 %collective-permute-start.12 = (bf16[2,768,384]{2,1,0:T(8,128)(2,1)S(1)}, bf16[2,768,384]{2,1,0:T(8,128)(2,1)S(1)}, u32[]{:S(2)}, u32[]{:S(2)}) collective-permute-start(bf16[2,768,384]{2,1,0:T(8,128)(2,1)S(1)} %get-tuple-element.24), channel_id=1, source_target_pairs={{0,8},{1,9},{2,10},{3,11},{4,12},{5,13},{6,14},{7,15},{8,0},{9,1},... | collective-permute-start | bytes 3538952 | tf_op jit(solution)/shard_map/ppermute | solution.py:89
  125.0 25.6 %collective-permute-start.23 = (bf16[1152,384]{1,0:T(8,128)(2,1)}, bf16[1152,384]{1,0:T(8,128)(2,1)}, u32[]{:S(2)}, u32[]{:S(2)}) collective-permute-start(bf16[1152,384]{1,0:T(8,128)(2,1)} %collective-permute-done.22.refs_0_), channel_id=1, source_target_pairs={{0,4},{1,5},{2,6},{3,7},{4,0},{5,1},{6,2},{7,3},{8,10},{9,11},{10,... | collective-permute-start | bytes 2654216 | tf_op jit(solution)/shard_map/ppermute | solution.py:89
  127.5 37.4 %collective-permute-start.4 = (bf16[1152,384]{1,0:T(8,128)(2,1)S(1)}, bf16[1152,384]{1,0:T(8,128)(2,1)S(1)}, u32[]{:S(2)}, u32[]{:S(2)}) collective-permute-start(bf16[1152,384]{1,0:T(8,128)(2,1)S(1)} %collective-permute-done.2.refs_1_), channel_id=1, source_target_pairs={{0,4},{1,5},{2,6},{3,7},{4,0},{5,1},{6,2},{7,3},{8,10},{9,11},{10,... | collective-permute-start | bytes 2654216 | tf_op jit(solution)/shard_map/ppermute | solution.py:89
  145.3 46.0 %collective-permute-start.14 = (bf16[2,768,384]{2,1,0:T(8,128)(2,1)S(1)}, bf16[2,768,384]{2,1,0:T(8,128)(2,1)S(1)}, u32[]{:S(2)}, u32[]{:S(2)}) collective-permute-start(bf16[2,768,384]{2,1,0:T(8,128)(2,1)S(1)} %get-tuple-element.24), channel_id=1, source_target_pairs={{0,24},{1,25},{2,26},{3,27},{4,28},{5,29},{6,30},{7,31},{8,16},{9,... | collective-permute-start | bytes 3538952 | tf_op jit(solution)/shard_map/ppermute | solution.py:89
  150.6 40.7 %collective-permute-start.6 = (bf16[1152,384]{1,0:T(8,128)(2,1)S(1)}, bf16[1152,384]{1,0:T(8,128)(2,1)S(1)}, u32[]{:S(2)}, u32[]{:S(2)}) collective-permute-start(bf16[1152,384]{1,0:T(8,128)(2,1)S(1)} %collective-permute-done.2.refs_1_), channel_id=1, source_target_pairs={{0,1},{1,0},{2,3},{3,2},{4,5},{5,4},{6,7},{7,6},{8,9},{9,8},{10,11... | collective-permute-start | bytes 2654216 | tf_op jit(solution)/shard_map/ppermute | solution.py:89
  164.9 25.8 %collective-permute-start.7 = (bf16[1152,384]{1,0:T(8,128)(2,1)S(1)}, bf16[1152,384]{1,0:T(8,128)(2,1)S(1)}, u32[]{:S(2)}, u32[]{:S(2)}) collective-permute-start(bf16[1152,384]{1,0:T(8,128)(2,1)S(1)} %collective-permute-done.3.refs_2_), channel_id=1, source_target_pairs={{0,1},{1,0},{2,3},{3,2},{4,5},{5,4},{6,7},{7,6},{8,9},{9,8},{10,11... | collective-permute-start | bytes 2654216 | tf_op jit(solution)/shard_map/ppermute | solution.py:89
  165.0 26.8 %collective-permute-start.25 = (bf16[1152,384]{1,0:T(8,128)(2,1)}, bf16[1152,384]{1,0:T(8,128)(2,1)}, u32[]{:S(2)}, u32[]{:S(2)}) collective-permute-start(bf16[1152,384]{1,0:T(8,128)(2,1)} %collective-permute-done.23.refs_1_), channel_id=1, source_target_pairs={{0,2},{1,3},{2,0},{3,1},{4,6},{5,7},{6,4},{7,5},{8,12},{9,13},{10,... | collective-permute-start | bytes 2654216 | tf_op jit(solution)/shard_map/ppermute | solution.py:89
  190.7 22.4 %collective-permute-start.26 = (bf16[1152,384]{1,0:T(8,128)(2,1)}, bf16[1152,384]{1,0:T(8,128)(2,1)}, u32[]{:S(2)}, u32[]{:S(2)}) collective-permute-start(bf16[1152,384]{1,0:T(8,128)(2,1)} %collective-permute-done.22.refs_0_), channel_id=1, source_target_pairs={{0,1},{1,0},{2,3},{3,2},{4,5},{5,4},{6,7},{7,6},{8,9},{9,8},{10,11... | collective-permute-start | bytes 2654216 | tf_op jit(solution)/shard_map/ppermute | solution.py:89
  191.3 21.9 %collective-permute-start.27 = (bf16[1152,384]{1,0:T(8,128)(2,1)}, bf16[1152,384]{1,0:T(8,128)(2,1)}, u32[]{:S(2)}, u32[]{:S(2)}) collective-permute-start(bf16[1152,384]{1,0:T(8,128)(2,1)} %collective-permute-done.23.refs_1_), channel_id=1, source_target_pairs={{0,1},{1,0},{2,3},{3,2},{4,5},{5,4},{6,7},{7,6},{8,9},{9,8},{10,11... | collective-permute-start | bytes 2654216 | tf_op jit(solution)/shard_map/ppermute | solution.py:89
  191.4 21.8 %collective-permute-start.28 = (bf16[1152,384]{1,0:T(8,128)(2,1)}, bf16[1152,384]{1,0:T(8,128)(2,1)}, u32[]{:S(2)}, u32[]{:S(2)}) collective-permute-start(bf16[1152,384]{1,0:T(8,128)(2,1)} %collective-permute-done.24.refs_2_), channel_id=1, source_target_pairs={{0,1},{1,0},{2,3},{3,2},{4,5},{5,4},{6,7},{7,6},{8,9},{9,8},{10,11... | collective-permute-start | bytes 2654216 | tf_op jit(solution)/shard_map/ppermute | solution.py:89
  191.8 21.4 %collective-permute-start.29 = (bf16[1152,384]{1,0:T(8,128)(2,1)}, bf16[1152,384]{1,0:T(8,128)(2,1)}, u32[]{:S(2)}, u32[]{:S(2)}) collective-permute-start(bf16[1152,384]{1,0:T(8,128)(2,1)} %collective-permute-done.25.refs_3_), channel_id=1, source_target_pairs={{0,1},{1,0},{2,3},{3,2},{4,5},{5,4},{6,7},{7,6},{8,9},{9,8},{10,11... | collective-permute-start | bytes 2654216 | tf_op jit(solution)/shard_map/ppermute | solution.py:89
  233.5 6.1 %collective-permute-start.34 = (bf16[1152,384]{1,0:T(8,128)(2,1)S(1)}, bf16[1152,384]{1,0:T(8,128)(2,1)S(1)}, u32[]{:S(2)}, u32[]{:S(2)}) collective-permute-start(bf16[1152,384]{1,0:T(8,128)(2,1)S(1)} %convolution_convert_fusion.8), channel_id=1, source_target_pairs={{0,1},{1,0},{2,3},{3,2},{4,5},{5,4},{6,7},{7,6},{8,9},{9,8},{10,11... | collective-permute-start | bytes 2654216 | tf_op jit(solution)/shard_map/ppermute | solution.py:89
  235.0 30.1 %collective-permute-start.16 = (bf16[1152,384]{1,0:T(8,128)(2,1)S(1)}, bf16[1152,384]{1,0:T(8,128)(2,1)S(1)}, u32[]{:S(2)}, u32[]{:S(2)}) collective-permute-start(bf16[1152,384]{1,0:T(8,128)(2,1)S(1)} %convolution_convert_fusion.14), channel_id=1, source_target_pairs={{0,1},{1,0},{2,3},{3,2},{4,5},{5,4},{6,7},{7,6},{8,9},{9,8},{10,11... | collective-permute-start | bytes 2654216 | tf_op jit(solution)/shard_map/ppermute | solution.py:89
  235.2 33.7 %collective-permute-start.18 = (bf16[1152,384]{1,0:T(8,128)(2,1)S(1)}, bf16[1152,384]{1,0:T(8,128)(2,1)S(1)}, u32[]{:S(2)}, u32[]{:S(2)}) collective-permute-start(bf16[1152,384]{1,0:T(8,128)(2,1)S(1)} %convolution_convert_fusion.13), channel_id=1, source_target_pairs={{0,1},{1,0},{2,3},{3,2},{4,5},{5,4},{6,7},{7,6},{8,9},{9,8},{10,11... | collective-permute-start | bytes 2654216 | tf_op jit(solution)/shard_map/ppermute | solution.py:89
  238.0 6.3 %collective-permute-start.31 = (bf16[1152,384]{1,0:T(8,128)(2,1)S(1)}, bf16[1152,384]{1,0:T(8,128)(2,1)S(1)}, u32[]{:S(2)}, u32[]{:S(2)}) collective-permute-start(bf16[1152,384]{1,0:T(8,128)(2,1)S(1)} %convolution_convert_fusion.10), channel_id=1, source_target_pairs={{0,1},{1,0},{2,3},{3,2},{4,5},{5,4},{6,7},{7,6},{8,9},{9,8},{10,11... | collective-permute-start | bytes 2654216 | tf_op jit(solution)/shard_map/ppermute | solution.py:89
  239.5 6.1 %collective-permute-start.33 = (bf16[1152,384]{1,0:T(8,128)(2,1)S(1)}, bf16[1152,384]{1,0:T(8,128)(2,1)S(1)}, u32[]{:S(2)}, u32[]{:S(2)}) collective-permute-start(bf16[1152,384]{1,0:T(8,128)(2,1)S(1)} %convolution_convert_fusion.9), channel_id=1, source_target_pairs={{0,1},{1,0},{2,3},{3,2},{4,5},{5,4},{6,7},{7,6},{8,9},{9,8},{10,11... | collective-permute-start | bytes 2654216 | tf_op jit(solution)/shard_map/ppermute | solution.py:89
  240.8 22.0 %collective-permute-start.35 = (bf16[1152,384]{1,0:T(8,128)(2,1)S(1)}, bf16[1152,384]{1,0:T(8,128)(2,1)S(1)}, u32[]{:S(2)}, u32[]{:S(2)}) collective-permute-start(bf16[1152,384]{1,0:T(8,128)(2,1)S(1)} %fusion.22), channel_id=1, source_target_pairs={{0,2},{1,3},{2,0},{3,1},{4,6},{5,7},{6,4},{7,5},{8,12},{9,13},{10,... | collective-permute-start | bytes 2654216 | tf_op jit(solution)/shard_map/ppermute | solution.py:89
  244.3 26.6 %collective-permute-start.30 = (bf16[1152,384]{1,0:T(8,128)(2,1)S(1)}, bf16[1152,384]{1,0:T(8,128)(2,1)S(1)}, u32[]{:S(2)}, u32[]{:S(2)}) collective-permute-start(bf16[1152,384]{1,0:T(8,128)(2,1)S(1)} %convolution_convert_fusion.11), channel_id=1, source_target_pairs={{0,1},{1,0},{2,3},{3,2},{4,5},{5,4},{6,7},{7,6},{8,9},{9,8},{10,11... | collective-permute-start | bytes 2654216 | tf_op jit(solution)/shard_map/ppermute | solution.py:89
  245.6 23.4 %collective-permute-start.20 = (bf16[1152,384]{1,0:T(8,128)(2,1)S(1)}, bf16[1152,384]{1,0:T(8,128)(2,1)S(1)}, u32[]{:S(2)}, u32[]{:S(2)}) collective-permute-start(bf16[1152,384]{1,0:T(8,128)(2,1)S(1)} %fusion.20), channel_id=1, source_target_pairs={{0,4},{1,5},{2,6},{3,7},{4,0},{5,1},{6,2},{7,3},{8,10},{9,11},{10,... | collective-permute-start | bytes 2654216 | tf_op jit(solution)/shard_map/ppermute | solution.py:89
  262.9 22.6 %collective-permute-start.32 = (bf16[1152,384]{1,0:T(8,128)(2,1)S(1)}, bf16[1152,384]{1,0:T(8,128)(2,1)S(1)}, u32[]{:S(2)}, u32[]{:S(2)}) collective-permute-start(bf16[1152,384]{1,0:T(8,128)(2,1)S(1)} %fusion.21), channel_id=1, source_target_pairs={{0,2},{1,3},{2,0},{3,1},{4,6},{5,7},{6,4},{7,5},{8,12},{9,13},{10,... | collective-permute-start | bytes 2654216 | tf_op jit(solution)/shard_map/ppermute | solution.py:89
  265.2 22.7 %collective-permute-start.36 = (bf16[1152,384]{1,0:T(8,128)(2,1)S(1)}, bf16[1152,384]{1,0:T(8,128)(2,1)S(1)}, u32[]{:S(2)}, u32[]{:S(2)}) collective-permute-start(bf16[1152,384]{1,0:T(8,128)(2,1)S(1)} %fusion.31), channel_id=1, source_target_pairs={{0,4},{1,5},{2,6},{3,7},{4,0},{5,1},{6,2},{7,3},{8,10},{9,11},{10,... | collective-permute-start | bytes 2654216 | tf_op jit(solution)/shard_map/ppermute | solution.py:89
  269.0 42.5 %collective-permute-start.15 = (bf16[1152,384]{1,0:T(8,128)(2,1)S(1)}, bf16[1152,384]{1,0:T(8,128)(2,1)S(1)}, u32[]{:S(2)}, u32[]{:S(2)}) collective-permute-start(bf16[1152,384]{1,0:T(8,128)(2,1)S(1)} %convolution_convert_fusion.15), channel_id=1, source_target_pairs={{0,1},{1,0},{2,3},{3,2},{4,5},{5,4},{6,7},{7,6},{8,9},{9,8},{10,11... | collective-permute-start | bytes 2654216 | tf_op jit(solution)/shard_map/ppermute | solution.py:89
  269.1 42.4 %collective-permute-start.17 = (bf16[1152,384]{1,0:T(8,128)(2,1)S(1)}, bf16[1152,384]{1,0:T(8,128)(2,1)S(1)}, u32[]{:S(2)}, u32[]{:S(2)}) collective-permute-start(bf16[1152,384]{1,0:T(8,128)(2,1)S(1)} %fusion.19), channel_id=1, source_target_pairs={{0,4},{1,5},{2,6},{3,7},{4,0},{5,1},{6,2},{7,3},{8,10},{9,11},{10,... | collective-permute-start | bytes 2654216 | tf_op jit(solution)/shard_map/ppermute | solution.py:89
  270.9 40.5 %collective-permute-start.21 = (bf16[1152,384]{1,0:T(8,128)(2,1)S(1)}, bf16[1152,384]{1,0:T(8,128)(2,1)S(1)}, u32[]{:S(2)}, u32[]{:S(2)}) collective-permute-start(bf16[1152,384]{1,0:T(8,128)(2,1)S(1)} %fusion.30), channel_id=1, source_target_pairs={{0,2},{1,3},{2,0},{3,1},{4,6},{5,7},{6,4},{7,5},{8,12},{9,13},{10,... | collective-permute-start | bytes 2654216 | tf_op jit(solution)/shard_map/ppermute | solution.py:89
  289.1 40.4 %collective-permute-start.37 = (bf16[1152,384]{1,0:T(8,128)(2,1)S(1)}, bf16[1152,384]{1,0:T(8,128)(2,1)S(1)}, u32[]{:S(2)}, u32[]{:S(2)}) collective-permute-start(bf16[1152,384]{1,0:T(8,128)(2,1)S(1)} %fusion.29), channel_id=1, source_target_pairs={{0,8},{1,9},{2,10},{3,11},{4,12},{5,13},{6,14},{7,15},{8,0},{9,1},... | collective-permute-start | bytes 2654216 | tf_op jit(solution)/shard_map/ppermute | solution.py:89
  332.3 19.2 %collective-permute-start.52 = (bf16[1152,384]{1,0:T(8,128)(2,1)S(1)}, bf16[1152,384]{1,0:T(8,128)(2,1)S(1)}, u32[]{:S(2)}, u32[]{:S(2)}) collective-permute-start(bf16[1152,384]{1,0:T(8,128)(2,1)S(1)} %bitcast.220), channel_id=1, source_target_pairs={{0,8},{1,9},{2,10},{3,11},{4,12},{5,13},{6,14},{7,15},{8,0},{9,1},... | collective-permute-start | bytes 2654216 | tf_op jit(solution)/shard_map/ppermute | solution.py:89
  334.1 19.0 %collective-permute-start.38 = (bf16[1152,384]{1,0:T(8,128)(2,1)S(1)}, bf16[1152,384]{1,0:T(8,128)(2,1)S(1)}, u32[]{:S(2)}, u32[]{:S(2)}) collective-permute-start(bf16[1152,384]{1,0:T(8,128)(2,1)S(1)} %bitcast.221), channel_id=1, source_target_pairs={{0,2},{1,3},{2,0},{3,1},{4,6},{5,7},{6,4},{7,5},{8,12},{9,13},{10,... | collective-permute-start | bytes 2654216 | tf_op jit(solution)/shard_map/ppermute | solution.py:89
  335.3 21.1 %collective-permute-start.39 = (bf16[1152,384]{1,0:T(8,128)(2,1)S(1)}, bf16[1152,384]{1,0:T(8,128)(2,1)S(1)}, u32[]{:S(2)}, u32[]{:S(2)}) collective-permute-start(bf16[1152,384]{1,0:T(8,128)(2,1)S(1)} %bitcast.222), channel_id=1, source_target_pairs={{0,4},{1,5},{2,6},{3,7},{4,0},{5,1},{6,2},{7,3},{8,10},{9,11},{10,... | collective-permute-start | bytes 2654216 | tf_op jit(solution)/shard_map/ppermute | solution.py:89
  335.8 20.6 %collective-permute-start.41 = (bf16[1152,384]{1,0:T(8,128)(2,1)S(1)}, bf16[1152,384]{1,0:T(8,128)(2,1)S(1)}, u32[]{:S(2)}, u32[]{:S(2)}) collective-permute-start(bf16[1152,384]{1,0:T(8,128)(2,1)S(1)} %bitcast.223), channel_id=1, source_target_pairs={{0,1},{1,0},{2,3},{3,2},{4,5},{5,4},{6,7},{7,6},{8,9},{9,8},{10,11... | collective-permute-start | bytes 2654216 | tf_op jit(solution)/shard_map/ppermute | solution.py:89
  351.5 24.0 %collective-permute-start.53 = (bf16[1152,384]{1,0:T(8,128)(2,1)S(1)}, bf16[1152,384]{1,0:T(8,128)(2,1)}, u32[]{:S(2)}, u32[]{:S(2)}) collective-permute-start(bf16[1152,384]{1,0:T(8,128)(2,1)S(1)} %collective-permute-done.52.refs_0_), channel_id=1, source_target_pairs={{0,4},{1,5},{2,6},{3,7},{4,0},{5,1},{6,2},{7,3},{8,10},{9,11},{10,... | collective-permute-start | bytes 2654216 | tf_op jit(solution)/shard_map/ppermute | solution.py:89
  353.0 38.5 %collective-permute-start.40 = (bf16[1152,384]{1,0:T(8,128)(2,1)S(1)}, bf16[1152,384]{1,0:T(8,128)(2,1)S(1)}, u32[]{:S(2)}, u32[]{:S(2)}) collective-permute-start(bf16[1152,384]{1,0:T(8,128)(2,1)S(1)} %collective-permute-done.38.refs_1_), channel_id=1, source_target_pairs={{0,4},{1,5},{2,6},{3,7},{4,0},{5,1},{6,2},{7,3},{8,10},{9,11},{10,... | collective-permute-start | bytes 2654216 | tf_op jit(solution)/shard_map/ppermute | solution.py:89
  353.5 38.0 %collective-permute-start.54 = (bf16[1152,384]{1,0:T(8,128)(2,1)S(1)}, bf16[1152,384]{1,0:T(8,128)(2,1)}, u32[]{:S(2)}, u32[]{:S(2)}) collective-permute-start(bf16[1152,384]{1,0:T(8,128)(2,1)S(1)} %collective-permute-done.52.refs_0_), channel_id=1, source_target_pairs={{0,2},{1,3},{2,0},{3,1},{4,6},{5,7},{6,4},{7,5},{8,12},{9,13},{10,... | collective-permute-start | bytes 2654216 | tf_op jit(solution)/shard_map/ppermute | solution.py:89
  356.4 35.6 %collective-permute-start.43 = (bf16[1152,384]{1,0:T(8,128)(2,1)S(1)}, bf16[1152,384]{1,0:T(8,128)(2,1)S(1)}, u32[]{:S(2)}, u32[]{:S(2)}) collective-permute-start(bf16[1152,384]{1,0:T(8,128)(2,1)S(1)} %collective-permute-done.39.refs_2_), channel_id=1, source_target_pairs={{0,1},{1,0},{2,3},{3,2},{4,5},{5,4},{6,7},{7,6},{8,9},{9,8},{10,11... | collective-permute-start | bytes 2654216 | tf_op jit(solution)/shard_map/ppermute | solution.py:89
  356.4 35.7 %collective-permute-start.42 = (bf16[1152,384]{1,0:T(8,128)(2,1)S(1)}, bf16[1152,384]{1,0:T(8,128)(2,1)S(1)}, u32[]{:S(2)}, u32[]{:S(2)}) collective-permute-start(bf16[1152,384]{1,0:T(8,128)(2,1)S(1)} %collective-permute-done.38.refs_1_), channel_id=1, source_target_pairs={{0,1},{1,0},{2,3},{3,2},{4,5},{5,4},{6,7},{7,6},{8,9},{9,8},{10,11... | collective-permute-start | bytes 2654216 | tf_op jit(solution)/shard_map/ppermute | solution.py:89
  375.5 17.2 %collective-permute-start.55 = (bf16[1152,384]{1,0:T(8,128)(2,1)}, bf16[1152,384]{1,0:T(8,128)(2,1)}, u32[]{:S(2)}, u32[]{:S(2)}) collective-permute-start(bf16[1152,384]{1,0:T(8,128)(2,1)} %collective-permute-done.53.refs_1_), channel_id=1, source_target_pairs={{0,2},{1,3},{2,0},{3,1},{4,6},{5,7},{6,4},{7,5},{8,12},{9,13},{10,... | collective-permute-start | bytes 2654216 | tf_op jit(solution)/shard_map/ppermute | solution.py:89
  391.6 20.8 %collective-permute-start.56 = (bf16[1152,384]{1,0:T(8,128)(2,1)S(1)}, bf16[1152,384]{1,0:T(8,128)(2,1)}, u32[]{:S(2)}, u32[]{:S(2)}) collective-permute-start(bf16[1152,384]{1,0:T(8,128)(2,1)S(1)} %collective-permute-done.52.refs_0_), channel_id=1, source_target_pairs={{0,1},{1,0},{2,3},{3,2},{4,5},{5,4},{6,7},{7,6},{8,9},{9,8},{10,11... | collective-permute-start | bytes 2654216 | tf_op jit(solution)/shard_map/ppermute | solution.py:89
  392.1 20.4 %collective-permute-start.57 = (bf16[1152,384]{1,0:T(8,128)(2,1)}, bf16[1152,384]{1,0:T(8,128)(2,1)}, u32[]{:S(2)}, u32[]{:S(2)}) collective-permute-start(bf16[1152,384]{1,0:T(8,128)(2,1)} %collective-permute-done.53.refs_1_), channel_id=1, source_target_pairs={{0,1},{1,0},{2,3},{3,2},{4,5},{5,4},{6,7},{7,6},{8,9},{9,8},{10,11... | collective-permute-start | bytes 2654216 | tf_op jit(solution)/shard_map/ppermute | solution.py:89
  392.2 20.2 %collective-permute-start.58 = (bf16[1152,384]{1,0:T(8,128)(2,1)}, bf16[1152,384]{1,0:T(8,128)(2,1)}, u32[]{:S(2)}, u32[]{:S(2)}) collective-permute-start(bf16[1152,384]{1,0:T(8,128)(2,1)} %collective-permute-done.54.refs_2_), channel_id=1, source_target_pairs={{0,1},{1,0},{2,3},{3,2},{4,5},{5,4},{6,7},{7,6},{8,9},{9,8},{10,11... | collective-permute-start | bytes 2654216 | tf_op jit(solution)/shard_map/ppermute | solution.py:89
  393.0 19.4 %collective-permute-start.59 = (bf16[1152,384]{1,0:T(8,128)(2,1)}, bf16[1152,384]{1,0:T(8,128)(2,1)}, u32[]{:S(2)}, u32[]{:S(2)}) collective-permute-start(bf16[1152,384]{1,0:T(8,128)(2,1)} %collective-permute-done.55.refs_3_), channel_id=1, source_target_pairs={{0,1},{1,0},{2,3},{3,2},{4,5},{5,4},{6,7},{7,6},{8,9},{9,8},{10,11... | collective-permute-start | bytes 2654216 | tf_op jit(solution)/shard_map/ppermute | solution.py:89
  431.1 29.8 %collective-permute-start.46 = (bf16[1152,384]{1,0:T(8,128)(2,1)S(1)}, bf16[1152,384]{1,0:T(8,128)(2,1)S(1)}, u32[]{:S(2)}, u32[]{:S(2)}) collective-permute-start(bf16[1152,384]{1,0:T(8,128)(2,1)S(1)} %convolution_convert_fusion.6), channel_id=1, source_target_pairs={{0,1},{1,0},{2,3},{3,2},{4,5},{5,4},{6,7},{7,6},{8,9},{9,8},{10,11... | collective-permute-start | bytes 2654216 | tf_op jit(solution)/shard_map/ppermute | solution.py:89
  431.5 34.0 %collective-permute-start.48 = (bf16[1152,384]{1,0:T(8,128)(2,1)S(1)}, bf16[1152,384]{1,0:T(8,128)(2,1)S(1)}, u32[]{:S(2)}, u32[]{:S(2)}) collective-permute-start(bf16[1152,384]{1,0:T(8,128)(2,1)S(1)} %convolution_convert_fusion.5), channel_id=1, source_target_pairs={{0,1},{1,0},{2,3},{3,2},{4,5},{5,4},{6,7},{7,6},{8,9},{9,8},{10,11... | collective-permute-start | bytes 2654216 | tf_op jit(solution)/shard_map/ppermute | solution.py:89
  434.3 6.0 %collective-permute-start.61 = (bf16[1152,384]{1,0:T(8,128)(2,1)S(1)}, bf16[1152,384]{1,0:T(8,128)(2,1)S(1)}, u32[]{:S(2)}, u32[]{:S(2)}) collective-permute-start(bf16[1152,384]{1,0:T(8,128)(2,1)S(1)} %convolution_convert_fusion.2), channel_id=1, source_target_pairs={{0,1},{1,0},{2,3},{3,2},{4,5},{5,4},{6,7},{7,6},{8,9},{9,8},{10,11... | collective-permute-start | bytes 2654216 | tf_op jit(solution)/shard_map/ppermute | solution.py:89
  437.2 21.8 %collective-permute-start.65 = (bf16[1152,384]{1,0:T(8,128)(2,1)S(1)}, bf16[1152,384]{1,0:T(8,128)(2,1)S(1)}, u32[]{:S(2)}, u32[]{:S(2)}) collective-permute-start(bf16[1152,384]{1,0:T(8,128)(2,1)S(1)} %fusion.26), channel_id=1, source_target_pairs={{0,2},{1,3},{2,0},{3,1},{4,6},{5,7},{6,4},{7,5},{8,12},{9,13},{10,... | collective-permute-start | bytes 2654216 | tf_op jit(solution)/shard_map/ppermute | solution.py:89
  440.3 29.2 %collective-permute-start.60 = (bf16[1152,384]{1,0:T(8,128)(2,1)S(1)}, bf16[1152,384]{1,0:T(8,128)(2,1)S(1)}, u32[]{:S(2)}, u32[]{:S(2)}) collective-permute-start(bf16[1152,384]{1,0:T(8,128)(2,1)S(1)} %convolution_convert_fusion.3), channel_id=1, source_target_pairs={{0,1},{1,0},{2,3},{3,2},{4,5},{5,4},{6,7},{7,6},{8,9},{9,8},{10,11... | collective-permute-start | bytes 2654216 | tf_op jit(solution)/shard_map/ppermute | solution.py:89
  441.5 24.1 %collective-permute-start.50 = (bf16[1152,384]{1,0:T(8,128)(2,1)S(1)}, bf16[1152,384]{1,0:T(8,128)(2,1)S(1)}, u32[]{:S(2)}, u32[]{:S(2)}) collective-permute-start(bf16[1152,384]{1,0:T(8,128)(2,1)S(1)} %fusion.24), channel_id=1, source_target_pairs={{0,4},{1,5},{2,6},{3,7},{4,0},{5,1},{6,2},{7,3},{8,10},{9,11},{10,... | collective-permute-start | bytes 2654216 | tf_op jit(solution)/shard_map/ppermute | solution.py:89
  458.9 22.6 %collective-permute-start.62 = (bf16[1152,384]{1,0:T(8,128)(2,1)S(1)}, bf16[1152,384]{1,0:T(8,128)(2,1)S(1)}, u32[]{:S(2)}, u32[]{:S(2)}) collective-permute-start(bf16[1152,384]{1,0:T(8,128)(2,1)S(1)} %fusion.25), channel_id=1, source_target_pairs={{0,2},{1,3},{2,0},{3,1},{4,6},{5,7},{6,4},{7,5},{8,12},{9,13},{10,... | collective-permute-start | bytes 2654216 | tf_op jit(solution)/shard_map/ppermute | solution.py:89
  460.9 22.7 %collective-permute-start.66 = (bf16[1152,384]{1,0:T(8,128)(2,1)S(1)}, bf16[1152,384]{1,0:T(8,128)(2,1)S(1)}, u32[]{:S(2)}, u32[]{:S(2)}) collective-permute-start(bf16[1152,384]{1,0:T(8,128)(2,1)S(1)} %fusion.33), channel_id=1, source_target_pairs={{0,4},{1,5},{2,6},{3,7},{4,0},{5,1},{6,2},{7,3},{8,10},{9,11},{10,... | collective-permute-start | bytes 2654216 | tf_op jit(solution)/shard_map/ppermute | solution.py:89
  465.5 51.8 %collective-permute-start.45 = (bf16[1152,384]{1,0:T(8,128)(2,1)}, bf16[1152,384]{1,0:T(8,128)(2,1)}, u32[]{:S(2)}, u32[]{:S(2)}) collective-permute-start(bf16[1152,384]{1,0:T(8,128)(2,1)} %convolution_convert_fusion.7), channel_id=1, source_target_pairs={{0,1},{1,0},{2,3},{3,2},{4,5},{5,4},{6,7},{7,6},{8,9},{9,8},{10,11... | collective-permute-start | bytes 2654216 | tf_op jit(solution)/shard_map/ppermute | solution.py:89
  465.5 51.8 %collective-permute-start.47 = (bf16[1152,384]{1,0:T(8,128)(2,1)}, bf16[1152,384]{1,0:T(8,128)(2,1)}, u32[]{:S(2)}, u32[]{:S(2)}) collective-permute-start(bf16[1152,384]{1,0:T(8,128)(2,1)} %fusion.23), channel_id=1, source_target_pairs={{0,4},{1,5},{2,6},{3,7},{4,0},{5,1},{6,2},{7,3},{8,10},{9,11},{10,... | collective-permute-start | bytes 2654216 | tf_op jit(solution)/shard_map/ppermute | solution.py:89
  469.5 47.9 %collective-permute-start.51 = (bf16[1152,384]{1,0:T(8,128)(2,1)}, bf16[1152,384]{1,0:T(8,128)(2,1)}, u32[]{:S(2)}, u32[]{:S(2)}) collective-permute-start(bf16[1152,384]{1,0:T(8,128)(2,1)} %fusion.32), channel_id=1, source_target_pairs={{0,2},{1,3},{2,0},{3,1},{4,6},{5,7},{6,4},{7,5},{8,12},{9,13},{10,... | collective-permute-start | bytes 2654216 | tf_op jit(solution)/shard_map/ppermute | solution.py:89
  485.7 31.7 %collective-permute-start.67 = (bf16[1152,384]{1,0:T(8,128)(2,1)}, bf16[1152,384]{1,0:T(8,128)(2,1)}, u32[]{:S(2)}, u32[]{:S(2)}) collective-permute-start(bf16[1152,384]{1,0:T(8,128)(2,1)} %fusion.28), channel_id=1, source_target_pairs={{0,8},{1,9},{2,10},{3,11},{4,12},{5,13},{6,14},{7,15},{8,0},{9,1},... | collective-permute-start | bytes 2654216 | tf_op jit(solution)/shard_map/ppermute | solution.py:89
  486.5 19.5 %collective-permute-start.68 = (f32[2,1152]{1,0:T(2,128)S(1)}, f32[2,1152]{1,0:T(2,128)S(1)}, u32[]{:S(2)}, u32[]{:S(2)}) collective-permute-start(f32[2,1152]{1,0:T(2,128)S(1)} %copy.28), channel_id=1, source_target_pairs={{0,8},{1,9},{2,10},{3,11},{4,12},{5,13},{6,14},{7,15},{8,0},{9,1},... | collective-permute-start | bytes 27656 | tf_op jit(solution)/shard_map/ppermute | solution.py:89
  524.5 6.6 %collective-permute-start.73 = (bf16[3,48,384]{2,1,0:T(8,128)(2,1)S(1)}, bf16[3,48,384]{2,1,0:T(8,128)(2,1)S(1)}, u32[]{:S(2)}, u32[]{:S(2)}) collective-permute-start(bf16[3,48,384]{2,1,0:T(8,128)(2,1)S(1)} %bitcast.226), channel_id=1, source_target_pairs={{8,0},{24,16},{9,1},{25,17},{10,2},{26,18},{11,3},{27,19},{12,4},{... | collective-permute-start | bytes 331784 | tf_op jit(solution)/shard_map/ppermute | solution.py:76
  (49 other events, 1007.4 us)

commit v2 on v0

v2 whole, which is shorter than its diff:
```python
import functools

import jax
import jax.numpy as jnp
from jax import lax
from jax.experimental import pallas as pl
from jax.experimental.pallas import tpu as pltpu
from jax.sharding import PartitionSpec as P

H = 48
LANES = 128

epsilon = 1e-06
root_half = 0.7071067811865476
density_scale = 0.3989422804014327


def conv_kernel(flip, add, x_ref, top_ref, bottom_ref, k_ref, *rest):
    if add:
        add_ref, o_ref, field = rest
    else:
        o_ref, field = rest
    rows, width, lanes = x_ref.shape
    field[...] = jnp.zeros_like(field)
    field[0:3, 8 : 8 + width, :] = top_ref[...].astype(jnp.float32)
    field[3 : 3 + rows, 8 : 8 + width, :] = x_ref[...].astype(jnp.float32)
    field[3 + rows : 6 + rows, 8 : 8 + width, :] = bottom_ref[...].astype(jnp.float32)

    @pl.loop(0, rows)
    def _(r):
        total = jnp.zeros((width, lanes), jnp.float32)
        for a in range(7):
            for b in range(7):
                weight = k_ref[6 - a, 6 - b] if flip else k_ref[a, b]
                total += weight[None, :] * field[r + a, 5 + b : 5 + b + width, :]
        mixed = total.astype(jnp.bfloat16)
        if add:
            mixed = (add_ref[r].astype(jnp.float32) + mixed.astype(jnp.float32)).astype(
                jnp.bfloat16
            )
        o_ref[r] = mixed


def depthwise(field, top, bottom, kernel, flip, add=None):
    rows, width, channels = field.shape
    lanes = LANES if channels % LANES == 0 else channels
    block = lambda n: pl.BlockSpec((n, width, lanes), lambda i: (0, 0, i))
    operands = [field, top, bottom, kernel]
    specs = [block(rows), block(3), block(3), pl.BlockSpec((7, 7, lanes), lambda i: (0, 0, i))]
    if add is not None:
        operands.append(add)
        specs.append(block(rows))
    return pl.pallas_call(
        functools.partial(conv_kernel, flip, add is not None),
        out_shape=jax.ShapeDtypeStruct(field.shape, jnp.bfloat16),
        grid=(channels // lanes,),
        in_specs=specs,
        out_specs=block(rows),
        scratch_shapes=[pltpu.VMEM((rows + 6, width + 16, lanes), jnp.float32)],
        compiler_params=pltpu.CompilerParams(vmem_limit_bytes=32 * 2**20),
        cost_estimate=pl.CostEstimate(
            flops=98 * rows * width * channels,
            bytes_accessed=6 * rows * width * channels,
            transcendentals=0,
        ),
        name="depthwise_flipped" if flip else "depthwise",
    )(*operands)


def halo(field):
    rows = field.shape[0]
    per_image = H // rows
    count = lax.axis_size("row")
    down = [(i, i + 1) for i in range(count - 1) if (i + 1) % per_image]
    up = [(j, i) for i, j in down]
    return lax.ppermute(field[-3:], "row", down), lax.ppermute(field[:3], "row", up)


MESH = pl.DeviceIdType.MESH
VMEM_LIMIT = 63 * 2**20


def flip(index, bit):
    return index + bit - 2 * bit * ((index // bit) % 2)


def flip_all(index, mask):
    bit = 1
    while bit <= mask:
        if mask & bit:
            index = flip(index, bit)
        bit *= 2
    return index


def token_tile(tokens):
    for tile in (384, 192, 96, 48, 16):
        if tokens % tile == 0:
            return tile
    return tokens


def split_columns(narrow, first):
    if narrow % LANES:
        return [(0, narrow)]
    groups = narrow // LANES
    head = min(first, groups)
    ranges = [(0, head * LANES)]
    if groups > head:
        ranges.append((head * LANES, (groups - head) * LANES))
    return ranges


def block_kernel(
    rows,
    cols,
    act,
    grad,
    w_expand,
    w_reduce,
    taps,
    bias,
    gain,
    shift,
    vectors,
    local_gain,
    scale,
    b_reduce,
    out,
    grad_mixed,
    mixes,
    grads,
    stage,
    expand,
    reduce,
    hidden,
    slopes,
    preact,
    mixed,
    stats,
    units_in,
    sums,
    sums_in,
    top,
    bottom,
    send,
    recv,
    local,
    free,
):
    tokens, narrow = grad.shape
    row_count, width, _ = act.shape
    channels = narrow * cols
    depth, units = expand.shape[1:]
    per = depth // narrow
    sliced = narrow % LANES == 0
    tile = token_tile(tokens)
    tiles = tokens // tile
    per_image = H // row_count
    r, c = lax.axis_index("row"), lax.axis_index("col")
    parity = r % 2
    blocks = cols // 2
    bits = [1 << b for b in range(1, cols.bit_length() - 1)]
    steps = len(bits)
    second = bits[steps // 2 :] + bits[: steps // 2]
    f32, bf16 = jnp.float32, jnp.bfloat16
    dot = functools.partial(jnp.dot, preferred_element_type=f32)
    turned = lambda left, right: lax.dot_general(
        left, right, (((1,), (1,)), ((), ())), preferred_element_type=f32
    )
    row_of = lambda distance: (flip_all(r, distance), c)
    core = (r, flip(c, 1))
    partner = row_of(1)

    def step_column(index, half, s):
        e = (r + half) % 2
        return flip(index, bits[s]) * (1 - e) + flip(index, second[s]) * e

    def owner_of(half, j):
        index = c
        for s in range(steps):
            index = index + ((j // (1 << s)) % 2) * (step_column(index, half, s) - index)
        return index

    counter = [0]

    def new(count=1):
        counter[0] += count
        return counter[0] - count

    def remote(src, dst, sem, device):
        return pltpu.make_async_remote_copy(
            src_ref=src,
            dst_ref=dst,
            send_sem=send.at[sem],
            recv_sem=recv.at[sem],
            device_id=device,
            device_id_type=MESH,
        )

    barrier = pltpu.get_barrier_semaphore()
    others = [row_of(d) for d in range(1, rows)] + [(r, flip(c, bit)) for bit in [1] + bits]
    for device in others:
        pl.semaphore_signal(barrier, inc=1, device_id=device, device_id_type=MESH)
    pl.semaphore_wait(barrier, len(others))

    has_top, has_bottom = r % per_image != 0, (r + 1) % per_image != 0
    up_device = ((r + rows - 1) % rows, c)
    down_device = ((r + 1) % rows, c)
    down = remote(act.at[pl.ds(row_count - 3, 3)], top, new(), down_device)
    up = remote(act.at[pl.ds(0, 3)], bottom, new(), up_device)
    if per_image > 1:
        pl.when(has_bottom)(down.start)
        pl.when(has_top)(up.start)

    def parts_of_expand(distance):
        half = (flip_all(r, distance) % 2) * units
        return w_expand.at[:, pl.ds(pl.multiple_of(half, units), units)]

    reduce_ranges = split_columns(narrow, 2)

    def parts_of_reduce(distance, start, size):
        half = flip_all(r, distance) % 2
        pairs = []
        for i in range(per):
            if sliced:
                span = pl.ds(i * narrow + start, size)
                rows_of = pl.ds(pl.multiple_of(half * units, units), units)
                pairs.append((w_reduce.at[rows_of, span], reduce.at[r, :, span]))
            else:
                pairs.append((w_reduce.at[half, i], reduce.at[r * per + i]))
        return pairs

    def loads(pairs, base):
        copies = []
        for index, (src, dst) in enumerate(pairs):
            copies.append(pltpu.make_async_copy(src, dst, local.at[base + index]))
            copies[-1].start()
        return copies

    taken = stage.at[0]
    act_in = [
        pltpu.make_async_copy(
            act.at[i], taken.at[pl.ds(i * width, width)], local.at[0]
        )
        for i in range(row_count)
    ]
    expand_own = loads([(parts_of_expand(0), expand.at[r])], 3)
    grad_own = loads([(grad, grads.at[0, c])], 4)

    expand_copies = [
        remote(parts_of_expand(d), expand.at[r], new(), row_of(d)) for d in range(rows - 1, 0, -1)
    ]

    def gather(buffer, source):
        step_copies = [[], []]
        for half in (0, 1):
            for s in range(steps):
                step_copies[half].append(
                    [
                        remote(
                            source if half == 0 and j == 0 else buffer.at[half, owner_of(half, j)],
                            buffer.at[half, owner_of(half, j)],
                            new(),
                            (r, step_column(c, half, s)),
                        )
                        for j in range(1 << s)
                    ]
                )
        across = remote(source, buffer.at[1, c], new(), partner)
        core_copies = [
            [
                remote(
                    source if half == 0 and j == 0 else buffer.at[half, owner_of(half, j)],
                    buffer.at[half, owner_of(half, j)],
                    new(),
                    core,
                )
                for j in range(blocks)
            ]
            for half in (0, 1)
        ]
        return step_copies, across, core_copies

    grad_steps, grad_across, grad_core = gather(grads, grad)
    mix_steps, mix_across, mix_core = gather(mixes, mixed)

    def begin(copies):
        for copy in copies:
            copy.start()

    def arrive(copies):
        for copy in copies:
            copy.wait_recv()

    def leave(copies):
        for copy in copies:
            copy.wait_send()

    begin(grad_steps[0][0])
    begin(expand_copies[:1])
    reduce_own = loads(
        [pair for start, size in reduce_ranges for pair in parts_of_reduce(0, start, size)], 5
    )

    for i in range(row_count):
        act_in[i].start()
        act_in[i].wait()
    if per_image > 1:

        @pl.when(has_top)
        def _():
            down.wait_recv()

        @pl.when(has_bottom)
        def _():
            up.wait_recv()

    lanes = LANES if sliced else narrow
    pitch = preact.shape[1]

    def place(row, value):
        preact[row, 8 : 8 + width, 0:lanes] = value.astype(f32)

    for group in range(narrow // lanes):
        span = pl.ds(group * lanes, lanes)

        @pl.loop(0, row_count + 6)
        def _(i):
            preact[i, :, 0:lanes] = jnp.zeros((pitch, lanes), f32)

        @pl.loop(0, row_count)
        def _(i):
            place(i + 3, stage[0, pl.ds(pl.multiple_of(i * width, 16), width), span])

        if per_image > 1:

            @pl.when(has_top)
            def _():
                for i in range(3):
                    place(i, top[i, :, span])

            @pl.when(has_bottom)
            def _():
                for i in range(3):
                    place(i + row_count + 3, bottom[i, :, span])

        @pl.loop(0, row_count)
        def _(i):
            total = jnp.zeros((width, lanes), f32)
            for a in range(7):
                for b in range(7):
                    total += (
                        taps[a, b, span][None, :]
                        * preact[i + a, 5 + b : 5 + b + width, 0:lanes]
                    )
            value = total.astype(bf16)
            mixed[pl.ds(pl.multiple_of(i * width, 16), width), span] = value

    begin([mix_across])
    begin(mix_steps[0][0])
    own_mixed = loads([(mixed, mixes.at[0, c])], 1)
    begin(mix_core[0][:1])
    begin([grad_across])
    begin(expand_copies[1:])
    for copy in own_mixed + grad_own:
        copy.wait()
    arrive([mix_across])
    begin(mix_steps[1][0])
    begin(mix_core[1][:1])
    for s in range(steps):
        for half in (0, 1):
            arrive(mix_steps[half][s])
            if s + 1 < steps:
                begin(mix_steps[half][s + 1])
            begin(mix_core[half][1 << s : 2 << s])
        if s == 0:
            arrive(grad_steps[0][0])
            if steps > 1:
                begin(grad_steps[0][1])
            arrive([grad_across])
            begin(grad_steps[1][0])
            begin(grad_core[0][:1] + grad_core[1][:1])
    arrive(grad_steps[1][0])
    if steps > 1:
        begin(grad_steps[1][1])
    for half in (0, 1):
        begin(grad_core[half][1:2])

    for copy in expand_own:
        copy.wait()
    arrive(expand_copies)
    for copy in reduce_own:
        copy.wait()
    reduce_copies = []
    for start, size in reduce_ranges:
        copies = []
        for d in range(rows - 1, 0, -1):
            copies += [
                remote(src, dst, new(), row_of(d)) for src, dst in parts_of_reduce(d, start, size)
            ]
        reduce_copies.append(copies)
    begin(reduce_copies[0])

    extra = jnp.zeros((vectors.shape[1], units), f32)
    for b in range(rows):
        extra += dot(vectors[b], expand[b])
    units_in[0:1, :] = extra[0:1] + extra[1:2] + extra[2:3]
    units_in[1:2, :] = bias[...] + (extra[3:4] + extra[4:5] + extra[5:6])

    def at(half, t):
        return pl.ds(pl.multiple_of(half * tokens + t * tile, 16), tile)

    def group_at(half, t):
        return pl.ds(half * (tokens // pitch) + t * (tile // pitch), tile // pitch)

    def expand_tokens(half):
        @pl.loop(0, tiles)
        def _(t):
            rows_at = pl.ds(pl.multiple_of(t * tile, 16), tile)
            total = jnp.zeros((tile, 1), f32)
            square = jnp.zeros((tile, 1), f32)
            for o in range(cols):
                value = mixes[half, o, rows_at, :].astype(f32)
                total += jnp.sum(value, 1, keepdims=True)
                square += jnp.sum(value * value, 1, keepdims=True)
            mean = total / channels
            inv = lax.rsqrt(square / channels - mean * mean + epsilon)
            if half == 0:
                stats[rows_at, 0:1] = mean
                stats[rows_at, 1:2] = inv
            value = jnp.zeros((tile, units), f32) + bias[...]
            for b in range(rows):
                group = [b * per + i for i in range(per)]
                normed = [
                    (
                        (mixes[half, o, rows_at, :].astype(f32) - mean) * inv * gain[o] + shift[o]
                    ).astype(bf16)
                    for o in group
                ]
                if sliced:
                    value += dot(jnp.concatenate(normed, 1), expand[b])
                else:
                    for i in range(per):
                        value += dot(normed[i], expand[b, i * narrow : (i + 1) * narrow, :])
            cumulative = 0.5 * (1.0 + lax.erf(value * root_half))
            hidden[at(half, t), :] = (value * cumulative).astype(bf16)
            preact[group_at(half, t)] = value.reshape(-1, pitch, units)

    arrive(mix_core[0])
    expand_tokens(0)
    for half in (0, 1):
        for s in range(1, steps):
            arrive(grad_steps[half][s])
            if s + 1 < steps:
                begin(grad_steps[half][s + 1])
            begin(grad_core[half][1 << s : 2 << s])
    arrive(mix_core[1])
    expand_tokens(1)

    nearby = [core, partner] + [(r, flip(c, bit)) for bit in bits]

    def release(index):
        for device in nearby:
            pl.semaphore_signal(free.at[index], inc=1, device_id=device, device_id_type=MESH)

    for half in (0, 1):
        for s in range(steps):
            leave(mix_steps[half][s])
        leave(mix_core[half])
    leave([mix_across])
    release(0)

    def sum_part(buffer, part, start, size, emit):
        base = new(4 * blocks - 1)
        span = pl.ds(start, size)

        def core_copy(half, j, slot):
            return remote(
                stage.at[slot, :, span], buffer.at[half, j, :, span], base + half * blocks + j, core
            )

        def step_copy(half, s, i):
            return remote(
                stage.at[2 * ((1 << s) - 1) + 2 * i + half, :, span],
                buffer.at[half, blocks + (1 << s) - 1 + i, :, span],
                base + 2 * blocks + 2 * ((1 << s) - 1) + 2 * i + half,
                (r, step_column(c, half, s)),
            )

        pair_copy = remote(
            stage.at[2 * (blocks - 1), :, span],
            buffer.at[0, cols - 1, :, span],
            base + 4 * blocks - 2,
            partner,
        )

        def total(half, t, owner, j, later):
            rows_at = pl.ds(pl.multiple_of(t * tile, 16), tile)
            value = part(half, t, owner, start, size)
            value += buffer[half, j, rows_at, span].astype(f32)
            for s in later:
                value += buffer[half, blocks + (1 << s) - 1 + j, rows_at, span].astype(f32)
            return value

        def over_tiles(slot, value_of):
            @pl.loop(0, tiles)
            def _(t):
                rows_at = pl.ds(pl.multiple_of(t * tile, 16), tile)
                stage[slot, rows_at, span] = value_of(t).astype(bf16)

        def first():
            @pl.loop(0, 2 * blocks)
            def _(i):
                half, j = i % 2, blocks - 1 - i // 2
                owner = flip(owner_of(half, j), 1)
                over_tiles(i, lambda t: part(half, t, owner, start, size))
                core_copy(half, j, i).start()

        def clear():
            @pl.loop(0, 2 * blocks)
            def _(i):
                core_copy(i % 2, blocks - 1 - i // 2, i).wait_send()

        def step(s):
            @pl.loop(0, 2 << s)
            def _(n):
                half, i = n % 2, n // 2
                j = i + (1 << s)
                core_copy(half, j, 0).wait_recv()
                for later in range(s + 1, steps):
                    step_copy(half, later, j).wait_recv()
                owner = owner_of(half, j)
                over_tiles(
                    2 * ((1 << s) - 1) + n,
                    lambda t: total(half, t, owner, j, range(s + 1, steps)),
                )
                step_copy(half, s, i).start()

        def across():
            core_copy(1, 0, 0).wait_recv()
            for s in range(steps):
                step_copy(1, s, 0).wait_recv()
            over_tiles(2 * (blocks - 1), lambda t: total(1, t, c, 0, range(steps)))
            pair_copy.start()

        def last():
            core_copy(0, 0, 0).wait_recv()
            for s in range(steps):
                step_copy(0, s, 0).wait_recv()
            pair_copy.wait_recv()

            @pl.loop(0, tiles)
            def _(t):
                rows_at = pl.ds(pl.multiple_of(t * tile, 16), tile)
                value = total(0, t, c, 0, range(steps))
                value += buffer[0, cols - 1, rows_at, span].astype(f32)
                emit(t, rows_at, span, start, size, value)

        def finish():
            for s in range(steps):

                @pl.loop(0, 2 << s)
                def _(n):
                    step_copy(n % 2, s, n // 2).wait_send()

            pair_copy.wait_send()

        stages = [first, clear] + [functools.partial(step, s) for s in range(steps - 1, -1, -1)]
        return stages + [across, last, finish]

    def branch_part(half, t, owner, start, size):
        if sliced:
            at_lane = pl.multiple_of((owner % per) * narrow + start, LANES)
            weights = reduce[owner // per, :, pl.ds(at_lane, size)]
        else:
            weights = reduce[owner]
        return dot(hidden[at(half, t), :], weights)

    def grad_part(half, t, owner, start, size):
        at_row = pl.multiple_of((owner % per) * narrow + start, 16)
        return turned(slopes[at(half, t), :], expand[owner // per, pl.ds(at_row, size), :])

    def emit_branch(t, rows_at, span, start, size, value):
        lane = slice(start, start + size)
        value = scale[:, lane] * (value + b_reduce[:, lane])
        value += stage[2 * blocks - 1, rows_at, span].astype(f32)
        stage[2 * blocks - 1, rows_at, span] = value.astype(bf16)

    def emit_grad(t, rows_at, span, start, size, value):
        lane = slice(start, start + size)
        mean, inv = stats[rows_at, 0:1], stats[rows_at, 1:2]
        both = jnp.transpose(sums[0, t])
        normal = (mixed[rows_at, span].astype(f32) - mean) * inv
        value = value * local_gain[:, lane]
        value = inv * (value - both[:, 0:1] / channels - normal * both[:, 1:2] / channels)
        mixed[rows_at, span] = value.astype(bf16)

    def grad_tokens(half):
        @pl.loop(0, tiles)
        def _(t):
            rows_at = pl.ds(pl.multiple_of(t * tile, 16), tile)
            value = jnp.zeros((tile, units), f32)
            for b in range(rows):
                group = [grads[half, b * per + i, rows_at, :] for i in range(per)]
                if sliced:
                    value += turned(jnp.concatenate(group, 1), reduce[b])
                else:
                    for i in range(per):
                        value += turned(group[i], reduce[b * per + i])
            a = preact[group_at(half, t)].reshape(tile, units)
            cumulative = 0.5 * (1.0 + lax.erf(a * root_half))
            slope = cumulative + a * jnp.exp(-0.5 * a * a) * density_scale
            rounded = (value * slope).astype(bf16)
            slopes[at(half, t), :] = rounded
            rounded = rounded.astype(f32)
            total = jnp.sum(rounded * units_in[0:1, :], 1, keepdims=True)
            cross = jnp.sum(rounded * (a - units_in[1:2, :]), 1, keepdims=True)
            lane = lax.broadcasted_iota(jnp.int32, (tile, LANES), 1)
            both = jnp.where(lane == 0, total, jnp.where(lane == 1, cross, 0.0))
            sums[half, t] = jnp.transpose(both)[0:8]

    arrive(reduce_copies[0])
    for copies in reduce_copies[1:]:
        begin(copies)
    pl.semaphore_wait(free.at[0], len(nearby))
    branch_parts = [
        sum_part(mixes, branch_part, start, size, emit_branch) for start, size in reduce_ranges
    ]
    head = branch_parts[0]
    for run in head[:-3]:
        run()
    for half in (0, 1):
        arrive(grad_core[half])
    for copies in reduce_copies[1:]:
        arrive(copies)
    tail = branch_parts[1] if len(branch_parts) > 1 else None
    if tail:
        tail[0]()
        tail[1]()
    grad_tokens(0)
    head[-3]()
    if tail:
        tail[2]()
    grad_tokens(1)
    for half in (0, 1):
        for s in range(steps):
            leave(grad_steps[half][s])
        leave(grad_core[half])
    leave([grad_across])
    release(1)

    sum_devices = [partner] + [(r, flip(c, bit)) for bit in [1] + bits]
    sum_copies = [
        remote(sums.at[1 if n == 0 else 0], sums_in.at[n], new(), device)
        for n, device in enumerate(sum_devices)
    ]

    def sum_step(n):
        if n:
            sum_copies[n - 1].wait()
            sums[0] = sums[0] + sums_in[n - 1]
        if n < len(sum_copies):
            sum_copies[n].start()

    sum_step(0)
    if tail:
        for run in tail[3:-2]:
            run()
    final_act = [
        pltpu.make_async_copy(
            act.at[i],
            stage.at[2 * blocks - 1, pl.ds(i * width, width)],
            local.at[0],
        )
        for i in range(row_count)
    ]
    for copy in final_act:
        copy.start()
        copy.wait()
    for run in head[-2:]:
        run()
    if tail:
        for run in tail[-2:]:
            run()
    out_copy = pltpu.make_async_copy(stage.at[2 * blocks - 1], out, local.at[0])
    out_copy.start()
    out_copy.wait()
    pl.semaphore_wait(free.at[1], len(nearby))

    grad_parts = [
        sum_part(grads, grad_part, start, size, emit_grad) for start, size in split_columns(narrow, 2)
    ]
    sum_index = 1
    for level in range(len(grad_parts[0]) - 2):
        for stages in grad_parts:
            stages[level]()
        if sum_index <= len(sum_copies):
            sum_step(sum_index)
            sum_index += 1
    while sum_index <= len(sum_copies):
        sum_step(sum_index)
        sum_index += 1
    for stages in grad_parts:
        stages[-2]()
    grad_copy = pltpu.make_async_copy(mixed, grad_mixed, local.at[1])
    grad_copy.start()
    for stages in grad_parts:
        stages[-1]()
    grad_copy.wait()

    leave(expand_copies)
    for copies in reduce_copies:
        leave(copies)
    if per_image > 1:
        pl.when(has_bottom)(down.wait_send)
        pl.when(has_top)(up.wait_send)


def semaphores_needed(rows, cols, per, reduce_parts, grad_parts):
    blocks, steps = cols // 2, cols.bit_length() - 2
    gathers = 2 * (2 * (blocks - 1) + 1 + 2 * blocks)
    weights = (rows - 1) * (1 + per * reduce_parts)
    return 2 + weights + gathers + (reduce_parts + grad_parts) * (4 * blocks - 1) + steps + 2


def body(
    activations,
    cotangent,
    kernel,
    ln_gain,
    ln_bias,
    w_expand,
    b_expand,
    w_reduce,
    b_reduce,
    layer_scale,
):
    row_count, grid_width, narrow = activations.shape
    rows, cols = lax.axis_size("row"), lax.axis_size("col")
    me_row, me_col = lax.axis_index("row"), lax.axis_index("col")
    channels = narrow * cols
    depth = channels // rows
    per = depth // narrow
    tokens = row_count * grid_width
    units = w_expand.shape[1] // 2
    sliced = narrow % LANES == 0
    tile = token_tile(tokens)
    f32, bf16 = jnp.float32, jnp.bfloat16

    cot_f = cotangent.astype(f32)
    grad_branch = (layer_scale * cot_f).reshape(tokens, narrow).astype(bf16)
    bias = lax.dynamic_slice_in_dim(b_expand, (me_row % 2) * units, units)[None, :]
    exact = []
    for vector in (ln_gain, ln_bias):
        for _ in range(3):
            piece = lax.reduce_precision(vector, 8, 7)
            exact.append(piece.astype(bf16))
            vector = vector - piece
    exact += [jnp.zeros_like(exact[0])] * (16 - len(exact))
    vectors = jnp.stack(exact).reshape(16, rows, depth).transpose(1, 0, 2)
    if sliced:
        reduce_source = w_reduce
        reduce_shape = (rows, units, depth)
    else:
        reduce_source = w_reduce.reshape(2, units, per, narrow).transpose(0, 2, 1, 3)
        reduce_shape = (cols, units, narrow)
    local_gain = lax.dynamic_slice_in_dim(ln_gain, me_col * narrow, narrow)
    reduce_parts = len(split_columns(narrow, 2))
    count = semaphores_needed(rows, cols, per, reduce_parts, len(split_columns(narrow, 2)))
    steps = cols.bit_length() - 2

    anywhere = pl.BlockSpec(memory_space=pl.ANY)
    inside = pl.BlockSpec(memory_space=pltpu.VMEM)
    flops = 8 * 2 * tokens * channels * units
    block_out, grad_mixed = pl.pallas_call(
        functools.partial(block_kernel, rows, cols),
        out_shape=[jax.ShapeDtypeStruct((tokens, narrow), bf16)] * 2,
        in_specs=[anywhere] * 4 + [inside] * 8,
        out_specs=[anywhere] * 2,
        scratch_shapes=[
            pltpu.VMEM((2, cols, tokens, narrow), bf16),
            pltpu.VMEM((2, cols, tokens, narrow), bf16),
            pltpu.VMEM((cols, tokens, narrow), bf16),
            pltpu.VMEM((rows, depth, units), bf16),
            pltpu.VMEM(reduce_shape, bf16),
            pltpu.VMEM((2 * tokens, units), bf16),
            pltpu.VMEM((2 * tokens, units), bf16),
            pltpu.VMEM((2 * tokens // (grid_width + 16), grid_width + 16, units), f32),
            pltpu.VMEM((tokens, narrow), bf16),
            pltpu.VMEM((tokens, 2), f32),
            pltpu.VMEM((2, units), f32),
            pltpu.VMEM((2, tokens // tile, 8, tile), f32),
            pltpu.VMEM((steps + 2, tokens // tile, 8, tile), f32),
            pltpu.VMEM((3, grid_width, narrow), bf16),
            pltpu.VMEM((3, grid_width, narrow), bf16),
            pltpu.SemaphoreType.DMA((count,)),
            pltpu.SemaphoreType.DMA((count,)),
            pltpu.SemaphoreType.DMA((5 + per * reduce_parts,)),
            pltpu.SemaphoreType.REGULAR((2,)),
        ],
        compiler_params=pltpu.CompilerParams(
            collective_id=0, has_side_effects=True, vmem_limit_bytes=VMEM_LIMIT
        ),
        cost_estimate=pl.CostEstimate(
            flops=flops, bytes_accessed=8 * channels * units, transcendentals=0
        ),
        name="block",
    )(
        activations,
        grad_branch,
        w_expand,
        reduce_source,
        kernel,
        bias,
        ln_gain.reshape(cols, 1, narrow),
        ln_bias.reshape(cols, 1, narrow),
        vectors,
        local_gain[None, :],
        layer_scale[None, :],
        b_reduce[None, :],
    )
    grad_mixed = grad_mixed.reshape(row_count, grid_width, narrow)
    top, bottom = halo(grad_mixed)
    grad_input = depthwise(grad_mixed, top, bottom, kernel, True, cotangent)
    return (block_out.reshape(row_count, grid_width, narrow), grad_input)


def solution(mesh):
    return jax.shard_map(
        body,
        mesh=mesh,
        in_specs=(
            P("row", None, "col"),
            P("row", None, "col"),
            P(None, None, "col"),
            P(),
            P(),
            P("row", "col"),
            P("col"),
            P("col", "row"),
            P("col"),
            P("col"),
        ),
        out_specs=(P("row", None, "col"), P("row", None, "col")),
        check_vma=False,
    )
```

time: 484 us -> 490 us (1.012)
  Pallas kernels: 19 us -> 464 us
  waiting for transfers between devices: 240 us -> 5.34 us
  matrix products: 82.5 us -> 0 us
  starting transfers between devices: 44.6 us -> 2.59 us
  local copies, waits for them, and re-layouts: 43.3 us -> 9.76 us
  blocking collectives: 25.9 us -> 0 us
  between operations: 15.1 us -> 0.71 us
  other arithmetic: 9.65 us -> 3.68 us
    pallas_call x0 -> x1, Pallas kernels: none -> 455 us  [body(): pl.pallas_call(functools.partial(block_kernel, rows, cols), out_shape=[ja...]
    ppermute x48 -> x0, waiting for transfers between devices: 135 us -> none  [the longest x45 85.5 us: swap(): return lax.ppermute(value, 'col', [(i, i ^ distance) for i in range(count)])]
    dot_general x28 -> x0, matrix products: 82.5 us -> none  [the longest x10 38.4 us: turned(): lax.dot_general(left, right, (((1,), (1,)), ((), ())), preferred_element_...]
    ppermute x2 -> x1, waiting for transfers between devices: 62.4 us -> 1 us  [halo(): lax.ppermute(field[-3:], 'row', down)]
    ppermute x48 -> x0, starting transfers between devices: 38.2 us -> none  [the longest x45 31.4 us: swap(): return lax.ppermute(value, 'col', [(i, i ^ distance) for i in range(count)])]
    all_gather x2 -> x0, waiting for transfers between devices: 37.1 us -> none  [the longest x1 37.1 us: body(): lax.all_gather(owners[:, :, cut:].reshape(units, -1), 'row', axis=1, tile...]
    psum x1 -> x0, blocking collectives: 25.9 us -> none  [body(): lax.psum((jnp.sum(local_mixed, 1), jnp.sum(local_mixed * local_mixed, 1))...]
    dynamic_update_slice x25 -> x0, local copies, waits for them, and re-layouts: 19.4 us -> none  [the longest x12 9.4 us: gather_columns(): lax.dynamic_update_slice(out, other, (0, (me ^ distance ^ 1) * narrow))]
  transfers between devices with their start and end apart: 54 -> 2, of which waited for: 15 -> 2; matrix products, arithmetic and copies ran while one was open for 22% -> 0% of each run, Pallas kernels for 4% -> 0%
where the time goes in v2:
time: 490 us; the launch traced here: 486 us
  Pallas kernels  464 us (95%)
  local copies, waits for them, and re-layouts  9.76 us (2%)
  waiting for transfers between devices  5.34 us (1%)
    pallas_call x1, Pallas kernels, body(): pl.pallas_call(functools.partial(block_kernel, rows, cols), out_shape=[ja...  455 us
  transfers between devices with their start and end apart: 2, of which 2 were waited for; matrix products, arithmetic and copies ran while one was open for 0% of the time, Pallas kernels for 0%

profile of v2, /device:TPU:0, one launch (start us, length us, event | category | flops | bytes accessed | tf_op | source)
XLA Modules:
  0.0 486.3 jit_solution(1962842529327071787)
XLA Ops:
  0.6 1.3 broadcast_in_dim.16.b_reduce
  1.9 1.3 broadcast_in_dim.15.scale
  3.2 0.7 fusion.1
  3.9 0.8 dynamic_slice.7
  4.7 0.6 broadcast_in_dim.14.local_gain
  5.2 0.8 dynamic_slice.6
  6.0 0.6 broadcast_in_dim.13.bias
  6.6 0.7 fusion.3
  7.4 2.3 multiply_convert_fusion
  9.7 1.4 stack.35
  11.0 0.0 copy-start
  11.0 0.0 copy-start.2
  11.1 454.6 %block.1 = (bf16[1152,384]{1,0:T(8,128)(2,1)}, bf16[1152,384]{1,0:T(8,128)(2,1)}) custom-call(bf16[24,48,384]{2,1,0:T(8,128)(2,1)} %act.1, bf16[1152,384]{1,0:T(8,128)(2,1)} %bitcast.10, bf16[768,1536]{1,0:T(8,128)(2,1)} %w_expand.1, bf16[1536,768]{1,0:T(8,128)(2,1)} %w_reduce.1, f32[7,7,384]{2,1,0:T(8,128)} %k_ref.1, f32[1,768]{1,0:T(1,128)} %broadcast_in_dim.13.bias, ...), custom_call_target="tpu_custom_call" | custom-call | flops 43486543872 | bytes 18874368 | tf_op jit(solution)/shard_map/block/pallas_call | solution.py:776
  465.6 1.0 fusion.4
  466.6 1.3 collective-permute-start
  467.9 1.3 collective-permute-start.1
  469.2 1.0 collective-permute-done.top_ref
  470.2 4.3 collective-permute-done.1.bottom_ref
  474.6 0.0 copy-done
  474.6 0.0 copy-done.2
  474.6 0.0 copy-start.1
  474.6 1.2 copy-done.1
  475.7 0.0 copy-start.3
  475.7 9.7 %depthwise_flipped.1 = bf16[24,48,384]{2,1,0:T(8,128)(2,1)} custom-call(bf16[24,48,384]{2,1,0:T(8,128)(2,1)S(1)} %bitcast.8, bf16[3,48,384]{2,1,0:T(8,128)(2,1)S(1)} %collective-permute-done.top_ref, bf16[3,48,384]{2,1,0:T(8,128)(2,1)S(1)} %collective-permute-done.1.bottom_ref, f32[7,7,384]{2,1,0:T(8,128)S(1)} %copy-done.2, bf16[24,48,384]{2,1,0:T(8,128)(2,1)S(1)} %copy-done), custom_call_target="tpu_custom_call" | custom-call | flops 43352064 | bytes 2654208 | tf_op jit(solution)/shard_map/depthwise_flipped/pallas_call | solution.py:53
  485.4 0.0 copy-done.3
  485.4 0.9 copy.19
  (8 shorter events, 0.1 us)
Async XLA Ops:
  11.0 463.5 %copy-start = (bf16[24,48,384]{2,1,0:T(8,128)(2,1)S(1)}, bf16[24,48,384]{2,1,0:T(8,128)(2,1)}, u32[]{:S(2)}) copy-start(bf16[24,48,384]{2,1,0:T(8,128)(2,1)} %rest_0_.1) | copy-start | bytes 2654212
  11.0 463.5 %copy-start.2 = (f32[7,7,384]{2,1,0:T(8,128)S(1)}, f32[7,7,384]{2,1,0:T(8,128)}, u32[]{:S(2)}) copy-start(f32[7,7,384]{2,1,0:T(8,128)} %k_ref.1) | copy-start | bytes 225796
  466.6 3.6 collective-permute-start
  467.9 6.6 %collective-permute-start.1 = (bf16[3,48,384]{2,1,0:T(8,128)(2,1)S(1)}, bf16[3,48,384]{2,1,0:T(8,128)(2,1)S(1)}, u32[]{:S(2)}, u32[]{:S(2)}) collective-permute-start(bf16[3,48,384]{2,1,0:T(8,128)(2,1)S(1)} %bitcast.11), channel_id=1, source_target_pairs={{8,0},{24,16},{9,1},{25,17},{10,2},{26,18},{11,3},{27,19},{12,4},{... | collective-permute-start | bytes 331784 | tf_op jit(solution)/shard_map/ppermute | solution.py:76
  474.6 1.2 copy-start.1
  475.7 9.7 %copy-start.3 = (bf16[1152,384]{1,0:T(8,128)(2,1)S(1)}, bf16[1152,384]{1,0:T(8,128)(2,1)}, u32[]{:S(2)}) copy-start(bf16[1152,384]{1,0:T(8,128)(2,1)} %get-tuple-element.4) | copy-start | bytes 2654212

commit v3 on v2

--- a/solution.py
+++ b/solution.py
@@ -77,7 +77,7 @@
 
 
 MESH = pl.DeviceIdType.MESH
-VMEM_LIMIT = 63 * 2**20
+VMEM_LIMIT = 127 * 2**19
 
 
 def flip(index, bit):
@@ -100,15 +100,10 @@
     return tokens
 
 
-def split_columns(narrow, first):
+def split_columns(narrow):
     if narrow % LANES:
         return [(0, narrow)]
-    groups = narrow // LANES
-    head = min(first, groups)
-    ranges = [(0, head * LANES)]
-    if groups > head:
-        ranges.append((head * LANES, (groups - head) * LANES))
-    return ranges
+    return [(start, LANES) for start in range(0, narrow, LANES)]
 
 
 def block_kernel(
@@ -131,6 +126,7 @@
     mixes,
     grads,
     stage,
+    held,
     expand,
     reduce,
     hidden,
@@ -149,13 +145,15 @@
     free,
 ):
     tokens, narrow = grad.shape
-    row_count, width, _ = act.shape
+    width = top.shape[0] // 3
+    row_count = tokens // width
     channels = narrow * cols
     depth, units = expand.shape[1:]
     per = depth // narrow
     sliced = narrow % LANES == 0
     tile = token_tile(tokens)
     tiles = tokens // tile
+    small = min(tile, 192)
     per_image = H // row_count
     r, c = lax.axis_index("row"), lax.axis_index("col")
     parity = r % 2
@@ -207,8 +205,8 @@
     has_top, has_bottom = r % per_image != 0, (r + 1) % per_image != 0
     up_device = ((r + rows - 1) % rows, c)
     down_device = ((r + 1) % rows, c)
-    down = remote(act.at[pl.ds(row_count - 3, 3)], top, new(), down_device)
-    up = remote(act.at[pl.ds(0, 3)], bottom, new(), up_device)
+    down = remote(act.at[pl.ds(tokens - 3 * width, 3 * width)], top, new(), down_device)
+    up = remote(act.at[pl.ds(0, 3 * width)], bottom, new(), up_device)
     if per_image > 1:
         pl.when(has_bottom)(down.start)
         pl.when(has_top)(up.start)
@@ -217,7 +215,7 @@
         half = (flip_all(r, distance) % 2) * units
         return w_expand.at[:, pl.ds(pl.multiple_of(half, units), units)]
 
-    reduce_ranges = split_columns(narrow, 2)
+    reduce_ranges = split_columns(narrow)
 
     def parts_of_reduce(distance, start, size):
         half = flip_all(r, distance) % 2
@@ -238,13 +236,7 @@
             copies[-1].start()
         return copies
 
-    taken = stage.at[0]
-    act_in = [
-        pltpu.make_async_copy(
-            act.at[i], taken.at[pl.ds(i * width, width)], local.at[0]
-        )
-        for i in range(row_count)
-    ]
+    act_in = loads([(act, held)], 0)
     expand_own = loads([(parts_of_expand(0), expand.at[r])], 3)
     grad_own = loads([(grad, grads.at[0, c])], 4)
 
@@ -252,35 +244,37 @@
         remote(parts_of_expand(d), expand.at[r], new(), row_of(d)) for d in range(rows - 1, 0, -1)
     ]
 
+    sets = 2
+    set_tokens = tokens // sets
+
     def gather(buffer, source):
-        step_copies = [[], []]
-        for half in (0, 1):
+        def there(half, j, q):
+            span = pl.ds(q * set_tokens, set_tokens)
+            order = (bits, second)[q]
+            owner = c
             for s in range(steps):
-                step_copies[half].append(
-                    [
-                        remote(
-                            source if half == 0 and j == 0 else buffer.at[half, owner_of(half, j)],
-                            buffer.at[half, owner_of(half, j)],
-                            new(),
-                            (r, step_column(c, half, s)),
-                        )
-                        for j in range(1 << s)
-                    ]
-                )
-        across = remote(source, buffer.at[1, c], new(), partner)
-        core_copies = [
-            [
-                remote(
-                    source if half == 0 and j == 0 else buffer.at[half, owner_of(half, j)],
-                    buffer.at[half, owner_of(half, j)],
-                    new(),
-                    core,
-                )
-                for j in range(blocks)
-            ]
+                if (j >> s) & 1:
+                    owner = flip(owner, order[s])
+            target = buffer.at[half, owner, span]
+            return (source.at[span] if half == 0 and j == 0 else target), target
+
+        def step_copies(half, s, q):
+            device = (r, flip(c, (bits, second)[q][s]))
+            return [remote(*there(half, j, q), new(), device) for j in range(1 << s)]
+
+        step_list = [
+            [[step_copies(half, s, q) for q in range(sets)] for s in range(steps)]
             for half in (0, 1)
         ]
-        return step_copies, across, core_copies
+        across = []
+        for q in range(sets):
+            span = pl.ds(q * set_tokens, set_tokens)
+            across.append(remote(source.at[span], buffer.at[1, c, span], new(), partner))
+        core_list = [
+            [[remote(*there(half, j, q), new(), core) for j in range(blocks)] for q in range(sets)]
+            for half in (0, 1)
+        ]
+        return step_list, across, core_list
 
     grad_steps, grad_across, grad_core = gather(grads, grad)
     mix_steps, mix_across, mix_core = gather(mixes, mixed)
@@ -297,15 +291,15 @@
         for copy in copies:
             copy.wait_send()
 
-    begin(grad_steps[0][0])
+    for q in range(sets):
+        begin(grad_steps[0][0][q])
     begin(expand_copies[:1])
     reduce_own = loads(
         [pair for start, size in reduce_ranges for pair in parts_of_reduce(0, start, size)], 5
     )
 
-    for i in range(row_count):
-        act_in[i].start()
-        act_in[i].wait()
+    for copy in act_in:
+        copy.wait()
     if per_image > 1:
 
         @pl.when(has_top)
@@ -331,19 +325,19 @@
 
         @pl.loop(0, row_count)
         def _(i):
-            place(i + 3, stage[0, pl.ds(pl.multiple_of(i * width, 16), width), span])
+            place(i + 3, held[pl.ds(pl.multiple_of(i * width, 16), width), span])
 
         if per_image > 1:
 
             @pl.when(has_top)
             def _():
                 for i in range(3):
-                    place(i, top[i, :, span])
+                    place(i, top[i * width : (i + 1) * width, span])
 
             @pl.when(has_bottom)
             def _():
                 for i in range(3):
-                    place(i + row_count + 3, bottom[i, :, span])
+                    place(i + row_count + 3, bottom[i * width : (i + 1) * width, span])
 
         @pl.loop(0, row_count)
         def _(i):
@@ -357,39 +351,45 @@
             value = total.astype(bf16)
             mixed[pl.ds(pl.multiple_of(i * width, 16), width), span] = value
 
-    begin([mix_across])
-    begin(mix_steps[0][0])
+    begin(mix_across)
+    for q in range(sets):
+        begin(mix_steps[0][0][q])
     own_mixed = loads([(mixed, mixes.at[0, c])], 1)
-    begin(mix_core[0][:1])
-    begin([grad_across])
-    begin(expand_copies[1:])
+    for q in range(sets):
+        begin(mix_core[0][q][:1])
     for copy in own_mixed + grad_own:
         copy.wait()
-    arrive([mix_across])
-    begin(mix_steps[1][0])
-    begin(mix_core[1][:1])
-    for s in range(steps):
-        for half in (0, 1):
-            arrive(mix_steps[half][s])
+
+    def advance(step_list, core_list, half, s):
+        for q in range(sets):
+            arrive(step_list[half][s][q])
             if s + 1 < steps:
-                begin(mix_steps[half][s + 1])
-            begin(mix_core[half][1 << s : 2 << s])
-        if s == 0:
-            arrive(grad_steps[0][0])
-            if steps > 1:
-                begin(grad_steps[0][1])
-            arrive([grad_across])
-            begin(grad_steps[1][0])
-            begin(grad_core[0][:1] + grad_core[1][:1])
-    arrive(grad_steps[1][0])
-    if steps > 1:
-        begin(grad_steps[1][1])
-    for half in (0, 1):
-        begin(grad_core[half][1:2])
+                begin(step_list[half][s + 1][q])
+            begin(core_list[half][q][1 << s : 2 << s])
+
+    advance(mix_steps, mix_core, 0, 0)
+    for q in range(sets):
+        arrive(mix_across[q : q + 1])
+        begin(mix_steps[1][0][q])
+        begin(mix_core[1][q][:1])
+    begin(expand_copies[1:-1])
+    for s in range(1, steps):
+        advance(mix_steps, mix_core, 0, s)
+        advance(mix_steps, mix_core, 1, s - 1)
+    advance(grad_steps, grad_core, 0, 0)
+    begin(expand_copies[-1:])
+    begin(grad_across)
+    for q in range(sets):
+        begin(grad_core[0][q][:1])
+    advance(mix_steps, mix_core, 1, steps - 1)
+    for q in range(sets):
+        arrive(grad_across[q : q + 1])
+        begin(grad_steps[1][0][q])
+        begin(grad_core[1][q][:1])
 
     for copy in expand_own:
         copy.wait()
-    arrive(expand_copies)
+    arrive(expand_copies[:-1])
     for copy in reduce_own:
         copy.wait()
     reduce_copies = []
@@ -401,6 +401,7 @@
             ]
         reduce_copies.append(copies)
     begin(reduce_copies[0])
+    arrive(expand_copies[-1:])
 
     extra = jnp.zeros((vectors.shape[1], units), f32)
     for b in range(rows):
@@ -408,18 +409,18 @@
     units_in[0:1, :] = extra[0:1] + extra[1:2] + extra[2:3]
     units_in[1:2, :] = bias[...] + (extra[3:4] + extra[4:5] + extra[5:6])
 
-    def at(half, t):
+    def at(half, t, tile=tile):
         return pl.ds(pl.multiple_of(half * tokens + t * tile, 16), tile)
 
-    def group_at(half, t):
+    def group_at(half, t, tile=tile):
         return pl.ds(half * (tokens // pitch) + t * (tile // pitch), tile // pitch)
 
     def expand_tokens(half):
-        @pl.loop(0, tiles)
+        @pl.loop(0, tokens // small)
         def _(t):
-            rows_at = pl.ds(pl.multiple_of(t * tile, 16), tile)
-            total = jnp.zeros((tile, 1), f32)
-            square = jnp.zeros((tile, 1), f32)
+            rows_at = pl.ds(pl.multiple_of(t * small, 16), small)
+            total = jnp.zeros((small, 1), f32)
+            square = jnp.zeros((small, 1), f32)
             for o in range(cols):
                 value = mixes[half, o, rows_at, :].astype(f32)
                 total += jnp.sum(value, 1, keepdims=True)
@@ -429,7 +430,7 @@
             if half == 0:
                 stats[rows_at, 0:1] = mean
                 stats[rows_at, 1:2] = inv
-            value = jnp.zeros((tile, units), f32) + bias[...]
+            value = jnp.zeros((small, units), f32) + bias[...]
             for b in range(rows):
                 group = [b * per + i for i in range(per)]
                 normed = [
@@ -444,19 +445,22 @@
                     for i in range(per):
                         value += dot(normed[i], expand[b, i * narrow : (i + 1) * narrow, :])
             cumulative = 0.5 * (1.0 + lax.erf(value * root_half))
-            hidden[at(half, t), :] = (value * cumulative).astype(bf16)
-            preact[group_at(half, t)] = value.reshape(-1, pitch, units)
-
-    arrive(mix_core[0])
+            hidden[at(half, t, small), :] = (value * cumulative).astype(bf16)
+            preact[group_at(half, t, small)] = value.reshape(-1, pitch, units)
+
+    def arrive_core(core_list, half):
+        for q in range(sets):
+            arrive(core_list[half][q])
+
+    arrive_core(mix_core, 0)
     expand_tokens(0)
-    for half in (0, 1):
-        for s in range(1, steps):
-            arrive(grad_steps[half][s])
-            if s + 1 < steps:
-                begin(grad_steps[half][s + 1])
-            begin(grad_core[half][1 << s : 2 << s])
-    arrive(mix_core[1])
+    for s in range(1, steps):
+        advance(grad_steps, grad_core, 0, s)
+    advance(grad_steps, grad_core, 1, 0)
+    arrive_core(mix_core, 1)
     expand_tokens(1)
+    for s in range(1, steps):
+        advance(grad_steps, grad_core, 1, s)
 
     nearby = [core, partner] + [(r, flip(c, bit)) for bit in bits]
 
@@ -464,33 +468,44 @@
         for device in nearby:
             pl.semaphore_signal(free.at[index], inc=1, device_id=device, device_id_type=MESH)
 
-    for half in (0, 1):
-        for s in range(steps):
-            leave(mix_steps[half][s])
-        leave(mix_core[half])
-    leave([mix_across])
+    def leave_gather(step_list, across, core_list):
+        leave(across)
+        for half in (0, 1):
+            for q in range(sets):
+                leave(core_list[half][q])
+                for s in range(steps):
+                    leave(step_list[half][s][q])
+
+    leave_gather(mix_steps, mix_across, mix_core)
     release(0)
 
-    def sum_part(buffer, part, start, size, emit):
+    def sum_part(buffer, part, columns, tile_range, emit, stage=stage):
         base = new(4 * blocks - 1)
+        start, size = columns[:2]
         span = pl.ds(start, size)
+        stage_span = pl.ds(columns[-1] if len(columns) > 2 else start, size)
+        first_tile, tile_count = tile_range
+        here = pl.ds(first_tile * tile, tile_count * tile)
 
         def core_copy(half, j, slot):
             return remote(
-                stage.at[slot, :, span], buffer.at[half, j, :, span], base + half * blocks + j, core
+                stage.at[slot, here, stage_span],
+                buffer.at[half, j, here, span],
+                base + half * blocks + j,
+                core,
             )
 
         def step_copy(half, s, i):
             return remote(
-                stage.at[2 * ((1 << s) - 1) + 2 * i + half, :, span],
-                buffer.at[half, blocks + (1 << s) - 1 + i, :, span],
+                stage.at[2 * ((1 << s) - 1) + 2 * i + half, here, stage_span],
+                buffer.at[half, blocks + (1 << s) - 1 + i, here, span],
                 base + 2 * blocks + 2 * ((1 << s) - 1) + 2 * i + half,
                 (r, step_column(c, half, s)),
             )
 
         pair_copy = remote(
-            stage.at[2 * (blocks - 1), :, span],
-            buffer.at[0, cols - 1, :, span],
+            stage.at[2 * (blocks - 1), here, stage_span],
+            buffer.at[0, cols - 1, here, span],
             base + 4 * blocks - 2,
             partner,
         )
@@ -504,10 +519,10 @@
             return value
 
         def over_tiles(slot, value_of):
-            @pl.loop(0, tiles)
+            @pl.loop(first_tile, first_tile + tile_count)
             def _(t):
                 rows_at = pl.ds(pl.multiple_of(t * tile, 16), tile)
-                stage[slot, rows_at, span] = value_of(t).astype(bf16)
+                stage[slot, rows_at, stage_span] = value_of(t).astype(bf16)
 
         def first():
             @pl.loop(0, 2 * blocks)
@@ -550,7 +565,7 @@
                 step_copy(0, s, 0).wait_recv()
             pair_copy.wait_recv()
 
-            @pl.loop(0, tiles)
+            @pl.loop(first_tile, first_tile + tile_count)
             def _(t):
                 rows_at = pl.ds(pl.multiple_of(t * tile, 16), tile)
                 value = total(0, t, c, 0, range(steps))
@@ -566,8 +581,13 @@
 
             pair_copy.wait_send()
 
-        stages = [first, clear] + [functools.partial(step, s) for s in range(steps - 1, -1, -1)]
-        return stages + [across, last, finish]
+        def step_cleared(s):
+            if s == steps - 1:
+                clear()
+            step(s)
+
+        turns = [functools.partial(step_cleared, s) for s in range(steps - 1, -1, -1)]
+        return [first] + turns + [across, last, finish]
 
     def branch_part(half, t, owner, start, size):
         if sliced:
@@ -584,8 +604,7 @@
     def emit_branch(t, rows_at, span, start, size, value):
         lane = slice(start, start + size)
         value = scale[:, lane] * (value + b_reduce[:, lane])
-        value += stage[2 * blocks - 1, rows_at, span].astype(f32)
-        stage[2 * blocks - 1, rows_at, span] = value.astype(bf16)
+        held[rows_at, span] = (held[rows_at, span].astype(f32) + value).astype(bf16)
 
     def emit_grad(t, rows_at, span, start, size, value):
         lane = slice(start, start + size)
@@ -596,9 +615,9 @@
         value = inv * (value - both[:, 0:1] / channels - normal * both[:, 1:2] / channels)
         mixed[rows_at, span] = value.astype(bf16)
 
-    def grad_tokens(half):
-        @pl.loop(0, tiles)
-        def _(t):
+    def grad_tokens(t):
+        @pl.loop(0, 2)
+        def _(half):
             rows_at = pl.ds(pl.multiple_of(t * tile, 16), tile)
             value = jnp.zeros((tile, units), f32)
             for b in range(rows):
@@ -620,35 +639,44 @@
             both = jnp.where(lane == 0, total, jnp.where(lane == 1, cross, 0.0))
             sums[half, t] = jnp.transpose(both)[0:8]
 
+    pl.semaphore_wait(free.at[0], len(nearby))
+    branch_units = []
+    for index, (start, size) in enumerate(reduce_ranges):
+        columns, where = (start, size), stage
+        if index == len(reduce_ranges) - 1 and index >= 2:
+            columns, where = (start, size, reduce_ranges[0][0]), mixes.at[0]
+        branch_units.append(
+            sum_part(mixes, branch_part, columns, (0, tiles), emit_branch, where)
+        )
+    first_index, turn, across_index, last_index = 0, 1, 1 + steps, 2 + steps
+    spare = len(branch_units) >= 3
     arrive(reduce_copies[0])
-    for copies in reduce_copies[1:]:
-        begin(copies)
-    pl.semaphore_wait(free.at[0], len(nearby))
-    branch_parts = [
-        sum_part(mixes, branch_part, start, size, emit_branch) for start, size in reduce_ranges
-    ]
-    head = branch_parts[0]
-    for run in head[:-3]:
-        run()
-    for half in (0, 1):
-        arrive(grad_core[half])
-    for copies in reduce_copies[1:]:
-        arrive(copies)
-    tail = branch_parts[1] if len(branch_parts) > 1 else None
-    if tail:
-        tail[0]()
-        tail[1]()
-    grad_tokens(0)
-    head[-3]()
-    if tail:
-        tail[2]()
-    grad_tokens(1)
-    for half in (0, 1):
-        for s in range(steps):
-            leave(grad_steps[half][s])
-        leave(grad_core[half])
-    leave([grad_across])
-    release(1)
+    begin([copy for copies in reduce_copies[1:2] for copy in copies])
+    for index, unit in enumerate(branch_units):
+        if index:
+            arrive(reduce_copies[index])
+            begin([copy for copies in reduce_copies[index + 1 : index + 2] for copy in copies])
+            before = branch_units[index - 1]
+            for s in range(1, steps):
+                before[turn + s]()
+            if spare and index == len(branch_units) - 1:
+                for done in branch_units[: index - 1]:
+                    done[last_index]()
+        unit[first_index]()
+        if index:
+            before[across_index]()
+        unit[turn]()
+
+    arrive_core(grad_core, 0)
+    arrive_core(grad_core, 1)
+    leave_gather(grad_steps, grad_across, grad_core)
+    latest = branch_units[-1]
+    for unit in branch_units[:-1]:
+        unit[-1]()
+
+    def finish_latest():
+        for s in range(1, steps):
+            latest[turn + s]()
 
     sum_devices = [partner] + [(r, flip(c, bit)) for bit in [1] + bits]
     sum_copies = [
@@ -657,56 +685,57 @@
     ]
 
     def sum_step(n):
-        if n:
+        if 0 < n <= len(sum_copies):
             sum_copies[n - 1].wait()
             sums[0] = sums[0] + sums_in[n - 1]
         if n < len(sum_copies):
             sum_copies[n].start()
 
-    sum_step(0)
-    if tail:
-        for run in tail[3:-2]:
-            run()
-    final_act = [
-        pltpu.make_async_copy(
-            act.at[i],
-            stage.at[2 * blocks - 1, pl.ds(i * width, width)],
-            local.at[0],
-        )
-        for i in range(row_count)
-    ]
-    for copy in final_act:
-        copy.start()
-        copy.wait()
-    for run in head[-2:]:
-        run()
-    if tail:
-        for run in tail[-2:]:
-            run()
-    out_copy = pltpu.make_async_copy(stage.at[2 * blocks - 1], out, local.at[0])
-    out_copy.start()
-    out_copy.wait()
-    pl.semaphore_wait(free.at[1], len(nearby))
-
-    grad_parts = [
-        sum_part(grads, grad_part, start, size, emit_grad) for start, size in split_columns(narrow, 2)
-    ]
+    grad_units = [sum_part(grads, grad_part, (0, narrow), (t, 1), emit_grad) for t in range(tiles)]
+
+    if not spare:
+        finish_latest()
+        latest[across_index]()
+        latest[-1]()
+    for t, unit in enumerate(grad_units):
+        grad_tokens(t)
+        release(1 + t)
+        if t == tiles - 1:
+            sum_step(0)
+        if t:
+            grad_units[t - 1][turn]()
+        pl.semaphore_wait(free.at[1 + t], len(nearby))
+        unit[first_index]()
+        if spare and t == 0:
+            finish_latest()
+        if spare and t == min(1, tiles - 1):
+            latest[across_index]()
+    grad_units[-1][turn]()
     sum_index = 1
-    for level in range(len(grad_parts[0]) - 2):
-        for stages in grad_parts:
-            stages[level]()
-        if sum_index <= len(sum_copies):
-            sum_step(sum_index)
-            sum_index += 1
+    for t, unit in enumerate(grad_units):
+        for s in range(1, steps):
+            unit[turn + s]()
+        if t:
+            grad_units[t - 1][across_index]()
+        sum_step(sum_index)
+        sum_index += 1
+    grad_units[-1][across_index]()
     while sum_index <= len(sum_copies):
         sum_step(sum_index)
         sum_index += 1
-    for stages in grad_parts:
-        stages[-2]()
+    for unit in branch_units[-2:] if spare else branch_units:
+        unit[last_index]()
+    out_copy = pltpu.make_async_copy(held, out, local.at[0])
+    out_copy.start()
+    for unit in grad_units:
+        unit[last_index]()
     grad_copy = pltpu.make_async_copy(mixed, grad_mixed, local.at[1])
     grad_copy.start()
-    for stages in grad_parts:
-        stages[-1]()
+    if spare:
+        latest[-1]()
+    for unit in grad_units:
+        unit[-1]()
+    out_copy.wait()
     grad_copy.wait()
 
     leave(expand_copies)
@@ -719,7 +748,7 @@
 
 def semaphores_needed(rows, cols, per, reduce_parts, grad_parts):
     blocks, steps = cols // 2, cols.bit_length() - 2
-    gathers = 2 * (2 * (blocks - 1) + 1 + 2 * blocks)
+    gathers = 4 * (2 * (blocks - 1) + 1 + 2 * blocks)
     weights = (rows - 1) * (1 + per * reduce_parts)
     return 2 + weights + gathers + (reduce_parts + grad_parts) * (4 * blocks - 1) + steps + 2
 
@@ -766,8 +795,8 @@
         reduce_source = w_reduce.reshape(2, units, per, narrow).transpose(0, 2, 1, 3)
         reduce_shape = (cols, units, narrow)
     local_gain = lax.dynamic_slice_in_dim(ln_gain, me_col * narrow, narrow)
-    reduce_parts = len(split_columns(narrow, 2))
-    count = semaphores_needed(rows, cols, per, reduce_parts, len(split_columns(narrow, 2)))
+    reduce_parts = len(split_columns(narrow))
+    count = semaphores_needed(rows, cols, per, reduce_parts, tokens // tile)
     steps = cols.bit_length() - 2
 
     anywhere = pl.BlockSpec(memory_space=pl.ANY)
@@ -782,6 +811,7 @@
             pltpu.VMEM((2, cols, tokens, narrow), bf16),
             pltpu.VMEM((2, cols, tokens, narrow), bf16),
             pltpu.VMEM((cols, tokens, narrow), bf16),
+            pltpu.VMEM((tokens, narrow), bf16),
             pltpu.VMEM((rows, depth, units), bf16),
             pltpu.VMEM(reduce_shape, bf16),
             pltpu.VMEM((2 * tokens, units), bf16),
@@ -792,12 +822,12 @@
             pltpu.VMEM((2, units), f32),
             pltpu.VMEM((2, tokens // tile, 8, tile), f32),
             pltpu.VMEM((steps + 2, tokens // tile, 8, tile), f32),
-            pltpu.VMEM((3, grid_width, narrow), bf16),
-            pltpu.VMEM((3, grid_width, narrow), bf16),
+            pltpu.VMEM((3 * grid_width, narrow), bf16),
+            pltpu.VMEM((3 * grid_width, narrow), bf16),
             pltpu.SemaphoreType.DMA((count,)),
             pltpu.SemaphoreType.DMA((count,)),
             pltpu.SemaphoreType.DMA((5 + per * reduce_parts,)),
-            pltpu.SemaphoreType.REGULAR((2,)),
+            pltpu.SemaphoreType.REGULAR((1 + tokens // tile,)),
         ],
         compiler_params=pltpu.CompilerParams(
             collective_id=0, has_side_effects=True, vmem_limit_bytes=VMEM_LIMIT
@@ -807,7 +837,7 @@
         ),
         name="block",
     )(
-        activations,
+        activations.reshape(tokens, narrow),
         grad_branch,
         w_expand,
         reduce_source,

time: 490 us -> 377 us (0.77)
  Pallas kernels: 464 us -> 350 us
    pallas_call x1, Pallas kernels: 455 us -> 340 us  [body(): pl.pallas_call(functools.partial(block_kernel, rows, cols), out_shape=[ja...]
where the time goes in v3:
time: 377 us; the launch traced here: 375 us
  Pallas kernels  350 us (93%)
  local copies, waits for them, and re-layouts  10.9 us (3%)
  waiting for transfers between devices  5.34 us (1%)
  starting transfers between devices  4.33 us (1%)
    pallas_call x1, Pallas kernels, body(): pl.pallas_call(functools.partial(block_kernel, rows, cols), out_shape=[ja...  340 us
    pallas_call x1, Pallas kernels, depthwise(): pl.pallas_call(functools.partial(conv_kernel, flip, add is not None), out...  9.67 us
  transfers between devices with their start and end apart: 2, of which 2 were waited for; matrix products, arithmetic and copies ran while one was open for 0% of the time, Pallas kernels for 0%

profile of v3, /device:TPU:0, one launch (start us, length us, event | category | flops | bytes accessed | tf_op | source)
XLA Modules:
  0.0 374.7 jit_solution(4592866773290686015)
XLA Ops:
  0.6 1.3 broadcast_in_dim.16.b_reduce
  1.9 1.3 broadcast_in_dim.15.scale
  3.2 0.7 fusion.1
  3.9 0.8 dynamic_slice.7
  4.7 0.6 broadcast_in_dim.14.local_gain
  5.2 0.8 dynamic_slice.6
  6.0 0.6 broadcast_in_dim.13.bias
  6.6 0.7 fusion.3
  7.4 2.3 multiply_convert_fusion
  9.7 1.4 stack.35
  11.0 0.0 copy-start.2
  11.0 340.0 %block.1 = (bf16[1152,384]{1,0:T(8,128)(2,1)}, bf16[1152,384]{1,0:T(8,128)(2,1)}) custom-call(bf16[1152,384]{1,0:T(8,128)(2,1)} %bitcast.17, bf16[1152,384]{1,0:T(8,128)(2,1)} %bitcast.11, bf16[768,1536]{1,0:T(8,128)(2,1)} %w_expand.1, bf16[1536,768]{1,0:T(8,128)(2,1)} %w_reduce.1, f32[7,7,384]{2,1,0:T(8,128)} %k_ref.1, f32[1,768]{1,0:T(1,128)} %broadcast_in_dim.13.bias, ...), custom_call_target="tpu_custom_call" | custom-call | flops 43486543872 | bytes 18874368 | tf_op jit(solution)/shard_map/block/pallas_call | solution.py:805
  351.1 1.0 fusion.4
  352.1 3.0 collective-permute-start
  355.1 1.3 collective-permute-start.1
  356.4 1.0 collective-permute-done.top_ref
  357.4 4.3 %collective-permute-done.1.bottom_ref = bf16[3,48,384]{2,1,0:T(8,128)(2,1)S(1)} collective-permute-done((bf16[3,48,384]{2,1,0:T(8,128)(2,1)S(1)}, bf16[3,48,384]{2,1,0:T(8,128)(2,1)S(1)}, u32[]{:S(2)}, u32[]{:S(2)}) %collective-permute-start.1) | collective-permute-done | bytes 110624 | tf_op jit(solution)/shard_map/ppermute | solution.py:76
  361.7 0.0 copy-done.2
  361.7 0.0 copy-start
  361.7 1.2 copy-done
  362.9 0.0 copy-start.1
  362.9 1.2 copy-done.1
  364.1 0.0 copy-start.3
  364.1 9.7 %depthwise_flipped.1 = bf16[24,48,384]{2,1,0:T(8,128)(2,1)} custom-call(bf16[24,48,384]{2,1,0:T(8,128)(2,1)S(1)} %bitcast.9, bf16[3,48,384]{2,1,0:T(8,128)(2,1)S(1)} %collective-permute-done.top_ref, bf16[3,48,384]{2,1,0:T(8,128)(2,1)S(1)} %collective-permute-done.1.bottom_ref, f32[7,7,384]{2,1,0:T(8,128)S(1)} %copy-done.2, bf16[24,48,384]{2,1,0:T(8,128)(2,1)S(1)} %copy-done), custom_call_target="tpu_custom_call" | custom-call | flops 43352064 | bytes 2654208 | tf_op jit(solution)/shard_map/depthwise_flipped/pallas_call | solution.py:53
  373.8 0.0 copy-done.3
  373.8 0.9 copy.19
  (8 shorter events, 0.1 us)
Async XLA Ops:
  11.0 350.7 %copy-start.2 = (f32[7,7,384]{2,1,0:T(8,128)S(1)}, f32[7,7,384]{2,1,0:T(8,128)}, u32[]{:S(2)}) copy-start(f32[7,7,384]{2,1,0:T(8,128)} %k_ref.1) | copy-start | bytes 225796
  352.1 5.3 %collective-permute-start = (bf16[3,48,384]{2,1,0:T(8,128)(2,1)S(1)}, bf16[3,48,384]{2,1,0:T(8,128)(2,1)S(1)}, u32[]{:S(2)}, u32[]{:S(2)}) collective-permute-start(bf16[3,48,384]{2,1,0:T(8,128)(2,1)S(1)} %bitcast.13), channel_id=1, source_target_pairs={{0,8},{16,24},{1,9},{17,25},{2,10},{18,26},{3,11},{19,27},{4,12},{... | collective-permute-start | bytes 331784 | tf_op jit(solution)/shard_map/ppermute | solution.py:76
  355.1 6.6 %collective-permute-start.1 = (bf16[3,48,384]{2,1,0:T(8,128)(2,1)S(1)}, bf16[3,48,384]{2,1,0:T(8,128)(2,1)S(1)}, u32[]{:S(2)}, u32[]{:S(2)}) collective-permute-start(bf16[3,48,384]{2,1,0:T(8,128)(2,1)S(1)} %bitcast.12), channel_id=1, source_target_pairs={{8,0},{24,16},{9,1},{25,17},{10,2},{26,18},{11,3},{27,19},{12,4},{... | collective-permute-start | bytes 331784 | tf_op jit(solution)/shard_map/ppermute | solution.py:76
  361.7 1.2 copy-start
  362.9 1.2 copy-start.1
  364.1 9.7 %copy-start.3 = (bf16[1152,384]{1,0:T(8,128)(2,1)S(1)}, bf16[1152,384]{1,0:T(8,128)(2,1)}, u32[]{:S(2)}) copy-start(bf16[1152,384]{1,0:T(8,128)(2,1)} %get-tuple-element.4) | copy-start | bytes 2654212

commit v4 on v3

--- a/solution.py
+++ b/solution.py
@@ -117,7 +117,6 @@
     bias,
     gain,
     shift,
-    vectors,
     local_gain,
     scale,
     b_reduce,
@@ -279,6 +278,15 @@
     grad_steps, grad_across, grad_core = gather(grads, grad)
     mix_steps, mix_across, mix_core = gather(mixes, mixed)
 
+    reduce_copies = []
+    for start, size in reduce_ranges:
+        copies = []
+        for d in range(rows - 1, 0, -1):
+            copies += [
+                remote(src, dst, new(), row_of(d)) for src, dst in parts_of_reduce(d, start, size)
+            ]
+        reduce_copies.append(copies)
+
     def begin(copies):
         for copy in copies:
             copy.start()
@@ -372,40 +380,38 @@
         arrive(mix_across[q : q + 1])
         begin(mix_steps[1][0][q])
         begin(mix_core[1][q][:1])
-    begin(expand_copies[1:-1])
+        if q == 0:
+            begin(expand_copies[1:-1])
+    begin(grad_across)
+    begin(expand_copies[-1:])
     for s in range(1, steps):
         advance(mix_steps, mix_core, 0, s)
         advance(mix_steps, mix_core, 1, s - 1)
+    advance(mix_steps, mix_core, 1, steps - 1)
     advance(grad_steps, grad_core, 0, 0)
-    begin(expand_copies[-1:])
-    begin(grad_across)
     for q in range(sets):
         begin(grad_core[0][q][:1])
-    advance(mix_steps, mix_core, 1, steps - 1)
     for q in range(sets):
         arrive(grad_across[q : q + 1])
         begin(grad_steps[1][0][q])
         begin(grad_core[1][q][:1])
-
-    for copy in expand_own:
+    for copy in reduce_own + expand_own:
         copy.wait()
-    arrive(expand_copies[:-1])
-    for copy in reduce_own:
-        copy.wait()
-    reduce_copies = []
-    for start, size in reduce_ranges:
-        copies = []
-        for d in range(rows - 1, 0, -1):
-            copies += [
-                remote(src, dst, new(), row_of(d)) for src, dst in parts_of_reduce(d, start, size)
-            ]
-        reduce_copies.append(copies)
     begin(reduce_copies[0])
-    arrive(expand_copies[-1:])
-
-    extra = jnp.zeros((vectors.shape[1], units), f32)
-    for b in range(rows):
-        extra += dot(vectors[b], expand[b])
+    arrive(expand_copies)
+
+    extra = jnp.zeros((16, units), f32)
+    for o in range(cols):
+        exact = []
+        for vector in (gain[o], shift[o]):
+            for _ in range(3):
+                piece = vector.astype(bf16).astype(f32)
+                exact.append(piece)
+                vector = vector - piece
+        exact.append(jnp.zeros((16 - len(exact), narrow), f32))
+        exact = jnp.concatenate(exact, 0).astype(bf16)
+        lane = (o % per) * narrow
+        extra += dot(exact, expand[o // per, lane : lane + narrow, :])
     units_in[0:1, :] = extra[0:1] + extra[1:2] + extra[2:3]
     units_in[1:2, :] = bias[...] + (extra[3:4] + extra[4:5] + extra[5:6])
 
@@ -454,11 +460,15 @@
 
     arrive_core(mix_core, 0)
     expand_tokens(0)
+    for copies in reduce_copies[1:2]:
+        begin(copies)
     for s in range(1, steps):
         advance(grad_steps, grad_core, 0, s)
     advance(grad_steps, grad_core, 1, 0)
     arrive_core(mix_core, 1)
     expand_tokens(1)
+    for copies in reduce_copies[2:]:
+        begin(copies)
     for s in range(1, steps):
         advance(grad_steps, grad_core, 1, s)
 
@@ -651,11 +661,9 @@
     first_index, turn, across_index, last_index = 0, 1, 1 + steps, 2 + steps
     spare = len(branch_units) >= 3
     arrive(reduce_copies[0])
-    begin([copy for copies in reduce_copies[1:2] for copy in copies])
     for index, unit in enumerate(branch_units):
         if index:
             arrive(reduce_copies[index])
-            begin([copy for copies in reduce_copies[index + 1 : index + 2] for copy in copies])
             before = branch_units[index - 1]
             for s in range(1, steps):
                 before[turn + s]()
@@ -702,15 +710,13 @@
         release(1 + t)
         if t == tiles - 1:
             sum_step(0)
-        if t:
-            grad_units[t - 1][turn]()
         pl.semaphore_wait(free.at[1 + t], len(nearby))
         unit[first_index]()
+        unit[turn]()
         if spare and t == 0:
             finish_latest()
         if spare and t == min(1, tiles - 1):
             latest[across_index]()
-    grad_units[-1][turn]()
     sum_index = 1
     for t, unit in enumerate(grad_units):
         for s in range(1, steps):
@@ -780,14 +786,6 @@
     cot_f = cotangent.astype(f32)
     grad_branch = (layer_scale * cot_f).reshape(tokens, narrow).astype(bf16)
     bias = lax.dynamic_slice_in_dim(b_expand, (me_row % 2) * units, units)[None, :]
-    exact = []
-    for vector in (ln_gain, ln_bias):
-        for _ in range(3):
-            piece = lax.reduce_precision(vector, 8, 7)
-            exact.append(piece.astype(bf16))
-            vector = vector - piece
-    exact += [jnp.zeros_like(exact[0])] * (16 - len(exact))
-    vectors = jnp.stack(exact).reshape(16, rows, depth).transpose(1, 0, 2)
     if sliced:
         reduce_source = w_reduce
         reduce_shape = (rows, units, depth)
@@ -805,7 +803,7 @@
     block_out, grad_mixed = pl.pallas_call(
         functools.partial(block_kernel, rows, cols),
         out_shape=[jax.ShapeDtypeStruct((tokens, narrow), bf16)] * 2,
-        in_specs=[anywhere] * 4 + [inside] * 8,
+        in_specs=[anywhere] * 4 + [inside] * 7,
         out_specs=[anywhere] * 2,
         scratch_shapes=[
             pltpu.VMEM((2, cols, tokens, narrow), bf16),
@@ -845,7 +843,6 @@
         bias,
         ln_gain.reshape(cols, 1, narrow),
         ln_bias.reshape(cols, 1, narrow),
-        vectors,
         local_gain[None, :],
         layer_scale[None, :],
         b_reduce[None, :],

time: 377 us -> 362 us (0.960)
  Pallas kernels: 350 us -> 340 us
    pallas_call x1, Pallas kernels: 340 us -> 330 us  [body(): pl.pallas_call(functools.partial(block_kernel, rows, cols), out_shape=[ja...]
where the time goes in v4:
time: 362 us
  Pallas kernels  340 us (94%)
  local copies, waits for them, and re-layouts  9.46 us (3%)
  waiting for transfers between devices  5.34 us (1%)
  starting transfers between devices  4.72 us (1%)
    pallas_call x1, Pallas kernels, body(): pl.pallas_call(functools.partial(block_kernel, rows, cols), out_shape=[ja...  330 us
    pallas_call x1, Pallas kernels, depthwise(): pl.pallas_call(functools.partial(conv_kernel, flip, add is not None), out...  9.67 us
  transfers between devices with their start and end apart: 2, of which 2 were waited for; matrix products, arithmetic and copies ran while one was open for 0% of the time, Pallas kernels for 0%

profile of v4, /device:TPU:0, one launch (start us, length us, event | category | flops | bytes accessed | tf_op | source)
XLA Modules:
  0.0 362.0 jit_solution(1586993059045084258)
XLA Ops:
  0.6 1.3 broadcast_in_dim.16.b_reduce
  1.9 0.8 dynamic_slice.7
  2.7 0.6 broadcast_in_dim.14.local_gain
  3.3 1.3 broadcast_in_dim.15.scale
  4.5 0.8 dynamic_slice.6
  5.3 0.6 broadcast_in_dim.13.bias
  5.9 2.2 multiply_convert_fusion
  8.1 0.0 copy-start.2
  8.1 329.9 %block.1 = (bf16[1152,384]{1,0:T(8,128)(2,1)}, bf16[1152,384]{1,0:T(8,128)(2,1)}) custom-call(bf16[1152,384]{1,0:T(8,128)(2,1)} %bitcast.14, bf16[1152,384]{1,0:T(8,128)(2,1)} %bitcast.10, bf16[768,1536]{1,0:T(8,128)(2,1)} %w_expand.1, bf16[1536,768]{1,0:T(8,128)(2,1)} %w_reduce.1, f32[7,7,384]{2,1,0:T(8,128)} %k_ref.1, f32[1,768]{1,0:T(1,128)} %broadcast_in_dim.13.bias, ...), custom_call_target="tpu_custom_call" | custom-call | flops 43486543872 | bytes 18874368 | tf_op jit(solution)/shard_map/block/pallas_call | solution.py:803
  338.0 1.0 fusion
  339.0 3.4 collective-permute-start
  342.5 1.3 collective-permute-start.1
  343.8 1.0 collective-permute-done.top_ref
  344.8 4.3 %collective-permute-done.1.bottom_ref = bf16[3,48,384]{2,1,0:T(8,128)(2,1)S(1)} collective-permute-done((bf16[3,48,384]{2,1,0:T(8,128)(2,1)S(1)}, bf16[3,48,384]{2,1,0:T(8,128)(2,1)S(1)}, u32[]{:S(2)}, u32[]{:S(2)}) %collective-permute-start.1) | collective-permute-done | bytes 110624 | tf_op jit(solution)/shard_map/ppermute | solution.py:76
  349.1 0.0 copy-done.2
  349.1 0.0 copy-start
  349.1 1.2 copy-done
  350.3 0.0 copy-start.1
  350.3 1.2 copy-done.1
  351.4 0.0 copy-start.3
  351.4 9.7 %depthwise_flipped.1 = bf16[24,48,384]{2,1,0:T(8,128)(2,1)} custom-call(bf16[24,48,384]{2,1,0:T(8,128)(2,1)S(1)} %bitcast.8, bf16[3,48,384]{2,1,0:T(8,128)(2,1)S(1)} %collective-permute-done.top_ref, bf16[3,48,384]{2,1,0:T(8,128)(2,1)S(1)} %collective-permute-done.1.bottom_ref, f32[7,7,384]{2,1,0:T(8,128)S(1)} %copy-done.2, bf16[24,48,384]{2,1,0:T(8,128)(2,1)S(1)} %copy-done), custom_call_target="tpu_custom_call" | custom-call | flops 43352064 | bytes 2654208 | tf_op jit(solution)/shard_map/depthwise_flipped/pallas_call | solution.py:53
  361.1 0.0 copy-done.3
  361.1 0.9 copy.13
Async XLA Ops:
  8.1 341.0 %copy-start.2 = (f32[7,7,384]{2,1,0:T(8,128)S(1)}, f32[7,7,384]{2,1,0:T(8,128)}, u32[]{:S(2)}) copy-start(f32[7,7,384]{2,1,0:T(8,128)} %k_ref.1) | copy-start | bytes 225796
  339.0 5.7 %collective-permute-start = (bf16[3,48,384]{2,1,0:T(8,128)(2,1)S(1)}, bf16[3,48,384]{2,1,0:T(8,128)(2,1)S(1)}, u32[]{:S(2)}, u32[]{:S(2)}) collective-permute-start(bf16[3,48,384]{2,1,0:T(8,128)(2,1)S(1)} %bitcast.12), channel_id=1, source_target_pairs={{0,8},{16,24},{1,9},{17,25},{2,10},{18,26},{3,11},{19,27},{4,12},{... | collective-permute-start | bytes 331784 | tf_op jit(solution)/shard_map/ppermute | solution.py:76
  342.5 6.6 %collective-permute-start.1 = (bf16[3,48,384]{2,1,0:T(8,128)(2,1)S(1)}, bf16[3,48,384]{2,1,0:T(8,128)(2,1)S(1)}, u32[]{:S(2)}, u32[]{:S(2)}) collective-permute-start(bf16[3,48,384]{2,1,0:T(8,128)(2,1)S(1)} %bitcast.11), channel_id=1, source_target_pairs={{8,0},{24,16},{9,1},{25,17},{10,2},{26,18},{11,3},{27,19},{12,4},{... | collective-permute-start | bytes 331784 | tf_op jit(solution)/shard_map/ppermute | solution.py:76
  349.1 1.2 copy-start
  350.3 1.2 copy-start.1
  351.4 9.7 %copy-start.3 = (bf16[1152,384]{1,0:T(8,128)(2,1)S(1)}, bf16[1152,384]{1,0:T(8,128)(2,1)}, u32[]{:S(2)}) copy-start(bf16[1152,384]{1,0:T(8,128)(2,1)} %get-tuple-element.4) | copy-start | bytes 2654212

commit v5 on v4

--- a/solution.py
+++ b/solution.py
@@ -117,7 +117,6 @@
     bias,
     gain,
     shift,
-    local_gain,
     scale,
     b_reduce,
     out,
@@ -413,7 +412,7 @@
         lane = (o % per) * narrow
         extra += dot(exact, expand[o // per, lane : lane + narrow, :])
     units_in[0:1, :] = extra[0:1] + extra[1:2] + extra[2:3]
-    units_in[1:2, :] = bias[...] + (extra[3:4] + extra[4:5] + extra[5:6])
+    units_in[1:2, :] = bias[parity] + (extra[3:4] + extra[4:5] + extra[5:6])
 
     def at(half, t, tile=tile):
         return pl.ds(pl.multiple_of(half * tokens + t * tile, 16), tile)
@@ -436,7 +435,7 @@
             if half == 0:
                 stats[rows_at, 0:1] = mean
                 stats[rows_at, 1:2] = inv
-            value = jnp.zeros((small, units), f32) + bias[...]
+            value = jnp.zeros((small, units), f32) + bias[parity]
             for b in range(rows):
                 group = [b * per + i for i in range(per)]
                 normed = [
@@ -613,7 +612,7 @@
 
     def emit_branch(t, rows_at, span, start, size, value):
         lane = slice(start, start + size)
-        value = scale[:, lane] * (value + b_reduce[:, lane])
+        value = scale[lane][None, :] * (value + b_reduce[lane][None, :])
         held[rows_at, span] = (held[rows_at, span].astype(f32) + value).astype(bf16)
 
     def emit_grad(t, rows_at, span, start, size, value):
@@ -621,7 +620,7 @@
         mean, inv = stats[rows_at, 0:1], stats[rows_at, 1:2]
         both = jnp.transpose(sums[0, t])
         normal = (mixed[rows_at, span].astype(f32) - mean) * inv
-        value = value * local_gain[:, lane]
+        value = value * gain[c, :, lane]
         value = inv * (value - both[:, 0:1] / channels - normal * both[:, 1:2] / channels)
         mixed[rows_at, span] = value.astype(bf16)
 
@@ -773,7 +772,6 @@
 ):
     row_count, grid_width, narrow = activations.shape
     rows, cols = lax.axis_size("row"), lax.axis_size("col")
-    me_row, me_col = lax.axis_index("row"), lax.axis_index("col")
     channels = narrow * cols
     depth = channels // rows
     per = depth // narrow
@@ -785,14 +783,12 @@
 
     cot_f = cotangent.astype(f32)
     grad_branch = (layer_scale * cot_f).reshape(tokens, narrow).astype(bf16)
-    bias = lax.dynamic_slice_in_dim(b_expand, (me_row % 2) * units, units)[None, :]
     if sliced:
         reduce_source = w_reduce
         reduce_shape = (rows, units, depth)
     else:
         reduce_source = w_reduce.reshape(2, units, per, narrow).transpose(0, 2, 1, 3)
         reduce_shape = (cols, units, narrow)
-    local_gain = lax.dynamic_slice_in_dim(ln_gain, me_col * narrow, narrow)
     reduce_parts = len(split_columns(narrow))
     count = semaphores_needed(rows, cols, per, reduce_parts, tokens // tile)
     steps = cols.bit_length() - 2
@@ -803,7 +799,7 @@
     block_out, grad_mixed = pl.pallas_call(
         functools.partial(block_kernel, rows, cols),
         out_shape=[jax.ShapeDtypeStruct((tokens, narrow), bf16)] * 2,
-        in_specs=[anywhere] * 4 + [inside] * 7,
+        in_specs=[anywhere] * 4 + [inside] * 6,
         out_specs=[anywhere] * 2,
         scratch_shapes=[
             pltpu.VMEM((2, cols, tokens, narrow), bf16),
@@ -840,12 +836,11 @@
         w_expand,
         reduce_source,
         kernel,
-        bias,
+        b_expand.reshape(2, 1, units),
         ln_gain.reshape(cols, 1, narrow),
         ln_bias.reshape(cols, 1, narrow),
-        local_gain[None, :],
-        layer_scale[None, :],
-        b_reduce[None, :],
+        layer_scale,
+        b_reduce,
     )
     grad_mixed = grad_mixed.reshape(row_count, grid_width, narrow)
     top, bottom = halo(grad_mixed)

time: 362 us -> 358 us (0.989)
  local copies, waits for them, and re-layouts: 9.46 us -> 5.53 us
    broadcast_in_dim x4 -> x0, local copies, waits for them, and re-layouts: 3.7 us -> none  [the longest x1 1.27 us: body(): layer_scale[None, :]]
where the time goes in v5:
time: 358 us
  Pallas kernels  340 us (95%)
  local copies, waits for them, and re-layouts  5.53 us (2%)
  waiting for transfers between devices  5.34 us (1%)
  starting transfers between devices  4.62 us (1%)
    pallas_call x1, Pallas kernels, body(): pl.pallas_call(functools.partial(block_kernel, rows, cols), out_shape=[ja...  330 us
    pallas_call x1, Pallas kernels, depthwise(): pl.pallas_call(functools.partial(conv_kernel, flip, add is not None), out...  9.67 us
  transfers between devices with their start and end apart: 2, of which 2 were waited for; matrix products, arithmetic and copies ran while one was open for 0% of the time, Pallas kernels for 0%

profile of v5, /device:TPU:0, one launch (start us, length us, event | category | flops | bytes accessed | tf_op | source)
XLA Modules:
  0.0 358.0 jit_solution(14428461983511259848)
XLA Ops:
  0.6 1.3 reshape.28.bias
  1.9 2.2 multiply_convert_fusion
  4.2 0.0 copy-start.2
  4.2 329.9 %block.1 = (bf16[1152,384]{1,0:T(8,128)(2,1)}, bf16[1152,384]{1,0:T(8,128)(2,1)}) custom-call(bf16[1152,384]{1,0:T(8,128)(2,1)} %bitcast.13, bf16[1152,384]{1,0:T(8,128)(2,1)} %bitcast.10, bf16[768,1536]{1,0:T(8,128)(2,1)} %w_expand.1, bf16[1536,768]{1,0:T(8,128)(2,1)} %w_reduce.1, f32[7,7,384]{2,1,0:T(8,128)} %k_ref.1, f32[2,1,768]{2,1,0:T(1,128)} %reshape.28.bias, ...), custom_call_target="tpu_custom_call" | custom-call | flops 43486543872 | bytes 18874368 | tf_op jit(solution)/shard_map/block/pallas_call | solution.py:799
  334.1 1.0 fusion
  335.1 3.3 collective-permute-start
  338.4 1.3 collective-permute-start.1
  339.7 1.0 collective-permute-done.top_ref
  340.8 4.3 %collective-permute-done.1.bottom_ref = bf16[3,48,384]{2,1,0:T(8,128)(2,1)S(1)} collective-permute-done((bf16[3,48,384]{2,1,0:T(8,128)(2,1)S(1)}, bf16[3,48,384]{2,1,0:T(8,128)(2,1)S(1)}, u32[]{:S(2)}, u32[]{:S(2)}) %collective-permute-start.1) | collective-permute-done | bytes 110624 | tf_op jit(solution)/shard_map/ppermute | solution.py:76
  345.1 0.0 copy-done.2
  345.1 0.0 copy-start
  345.1 1.2 copy-done
  346.3 0.0 copy-start.1
  346.3 1.2 copy-done.1
  347.4 0.0 copy-start.3
  347.4 9.7 %depthwise_flipped.1 = bf16[24,48,384]{2,1,0:T(8,128)(2,1)} custom-call(bf16[24,48,384]{2,1,0:T(8,128)(2,1)S(1)} %bitcast.8, bf16[3,48,384]{2,1,0:T(8,128)(2,1)S(1)} %collective-permute-done.top_ref, bf16[3,48,384]{2,1,0:T(8,128)(2,1)S(1)} %collective-permute-done.1.bottom_ref, f32[7,7,384]{2,1,0:T(8,128)S(1)} %copy-done.2, bf16[24,48,384]{2,1,0:T(8,128)(2,1)S(1)} %copy-done), custom_call_target="tpu_custom_call" | custom-call | flops 43352064 | bytes 2654208 | tf_op jit(solution)/shard_map/depthwise_flipped/pallas_call | solution.py:53
  357.1 0.0 copy-done.3
  357.1 0.9 copy.13
Async XLA Ops:
  4.2 340.9 %copy-start.2 = (f32[7,7,384]{2,1,0:T(8,128)S(1)}, f32[7,7,384]{2,1,0:T(8,128)}, u32[]{:S(2)}) copy-start(f32[7,7,384]{2,1,0:T(8,128)} %k_ref.1) | copy-start | bytes 225796
  335.1 5.6 %collective-permute-start = (bf16[3,48,384]{2,1,0:T(8,128)(2,1)S(1)}, bf16[3,48,384]{2,1,0:T(8,128)(2,1)S(1)}, u32[]{:S(2)}, u32[]{:S(2)}) collective-permute-start(bf16[3,48,384]{2,1,0:T(8,128)(2,1)S(1)} %bitcast.12), channel_id=1, source_target_pairs={{0,8},{16,24},{1,9},{17,25},{2,10},{18,26},{3,11},{19,27},{4,12},{... | collective-permute-start | bytes 331784 | tf_op jit(solution)/shard_map/ppermute | solution.py:76
  338.4 6.6 %collective-permute-start.1 = (bf16[3,48,384]{2,1,0:T(8,128)(2,1)S(1)}, bf16[3,48,384]{2,1,0:T(8,128)(2,1)S(1)}, u32[]{:S(2)}, u32[]{:S(2)}) collective-permute-start(bf16[3,48,384]{2,1,0:T(8,128)(2,1)S(1)} %bitcast.11), channel_id=1, source_target_pairs={{8,0},{24,16},{9,1},{25,17},{10,2},{26,18},{11,3},{27,19},{12,4},{... | collective-permute-start | bytes 331784 | tf_op jit(solution)/shard_map/ppermute | solution.py:76
  345.1 1.2 copy-start
  346.3 1.2 copy-start.1
  347.4 9.7 %copy-start.3 = (bf16[1152,384]{1,0:T(8,128)(2,1)S(1)}, bf16[1152,384]{1,0:T(8,128)(2,1)}, u32[]{:S(2)}) copy-start(bf16[1152,384]{1,0:T(8,128)(2,1)} %get-tuple-element.4) | copy-start | bytes 2654212
